TPU v7x, 32 devices: a whole 2x2x4 slice. The times are simulated.
32 devices in a mesh: chan: 8 (over y, x, core), win: 4 (over z).
Axes of the slice: x: 2, y: 2, z: 4, core: 2. Of those that a mesh axis runs over, the one named last changes fastest.
Arguments:
- spectra: bfloat16 [16, 256, 4096], P('win', 'chan'), may hold values from -80 to 80
- quality: int32 [256], P('chan'), may hold values 0 or 1
- source_block: int32 [2], replicated, may hold values from 0 to 31
Outputs:
- correlations: bfloat16 [2, 256, 8, 512], P(None, ('chan', 'win'))
All inputs are finite; a program needn't handle non-finite values. No bound on the sum of `quality` on one device may be relied on, other than what follows from the above.
Results may differ from a plain program's by a relative error of at most 0.0045.
Values may be sent and summed in bfloat16 or wider, within the bound.
No kernel may reach another device: no remote copies, remote signals or barrier semaphores. Data moves between devices by JAX's collectives and lax.ppermute only.
A program may use at most 192 MiB of HBM per device.

v0:
```python
import math

import jax
import jax.numpy as jnp
from jax import lax
from jax.sharding import PartitionSpec as P

L = 512
SRC = 8
STEPS = 2


def from_root(value, axis, source):
    kept = jnp.where(lax.axis_index(axis) == source, value, 0).astype(value.dtype)
    return lax.psum(kept, axis)


def lag_table(bins, lags, factor):
    bin_index = lax.iota(jnp.int32, bins)[:, None]
    shifts = lax.iota(jnp.int32, lags)[None, :] - lags // 2
    residue = jnp.mod(bin_index * shifts, 2 * bins)
    phase_angle = residue.astype(jnp.float32) * (2.0 * math.pi / (2 * bins))
    return jnp.concatenate([jnp.cos(phase_angle), -jnp.sin(phase_angle)], axis=0) * factor


def whiten(block, quality):
    values = block.astype(jnp.float32)
    bins = values.shape[-1] // 2
    energy = jnp.sum(values * values, axis=-1) / bins
    weights = quality.astype(jnp.float32)[None, :] / jnp.sqrt(energy + 1e-06)
    return (values * weights[:, :, None]).astype(jnp.bfloat16)


def cross_spectra(sources, receivers):
    bins = sources.shape[-1] // 2
    src_real = sources[:, :, :bins]
    src_imag = sources[:, :, bins:]
    rec_real = receivers[:, :, :bins]
    rec_imag = receivers[:, :, bins:]
    real_part = jnp.einsum("wsf,wrf->rsf", src_real, rec_real, preferred_element_type=jnp.float32)
    real_part = real_part + jnp.einsum(
        "wsf,wrf->rsf", src_imag, rec_imag, preferred_element_type=jnp.float32
    )
    imag_part = jnp.einsum("wsf,wrf->rsf", src_real, rec_imag, preferred_element_type=jnp.float32)
    imag_part = imag_part - jnp.einsum(
        "wsf,wrf->rsf", src_imag, rec_real, preferred_element_type=jnp.float32
    )
    return jnp.concatenate([real_part, imag_part], axis=-1)


def apply_lags(cross, transform):
    lagged = jnp.dot(
        cross.reshape(-1, cross.shape[-1]),
        transform,
        precision=lax.Precision.HIGHEST,
        preferred_element_type=jnp.float32,
    )
    return lagged.reshape(cross.shape[0], cross.shape[1], transform.shape[1])


def body(spectra, quality, source_block):
    window_count, channel_count, row_width = spectra.shape
    bins = row_width // 2
    total_windows = window_count * lax.axis_size("win")
    transform = lag_table(bins, L, 1.0 / math.sqrt(row_width * total_windows))
    whitened = whiten(spectra, quality)
    per_group = channel_count // SRC
    results = []
    for step in range(STEPS):
        block_index = source_block[step]
        root_group = block_index // per_group
        offset = block_index % per_group * SRC
        own_block = lax.dynamic_slice_in_dim(whitened, offset, SRC, 1)
        sources = from_root(own_block, "chan", root_group)
        partial_cross = cross_spectra(sources, whitened)
        stacked = lax.psum_scatter(partial_cross, "win", scatter_dimension=0, tiled=True)
        lagged = apply_lags(stacked, transform)
        results.append(lagged.astype(jnp.bfloat16))
    return jnp.stack(results)


def solution(mesh):
    return jax.shard_map(
        body,
        mesh=mesh,
        in_specs=(P("win", "chan", None), P("chan"), P()),
        out_specs=P(None, ("chan", "win"), None, None),
        check_vma=False,
    )
```

profile of v0, /device:TPU:0, one launch (start us, length us, event | category | flops | bytes accessed | tf_op | source)
XLA Modules:
  0.0 307.7 jit_solution(4543536564017385176)
XLA Ops:
  17.8 2.5 copy.4
  21.7 53.5 %all-reduce.3.cloned.1.call-done = (bf16[4,8,4096]{2,1,0:T(8,128)(2,1)}, bf16[4,8,4096]{2,1,0:T(8,128)(2,1)}) async-done(((bf16[4,8,4096]{2,1,0:T(8,128)(2,1)}, bf16[4,8,4096]{2,1,0:T(8,128)(2,1)}), (bf16[4,8,4096]{2,1,0:T(8,128)(2,1)}, bf16[4,8,4096]{2,1,0:T(8,128)(2,1)})) %all-reduce.3.cloned.1.call-update) | async-done | bytes 524304 | tf_op jit(solution)/shard_map/psum | solution.py:15
  81.2 7.4 %fusion.36 = f32[2048,32,8]{1,2,0:T(8,128)} fusion(bf16[4,32,2048]{1,0,2:T(4,128)(2,1)} %copy.4, bf16[4,8,2048]{1,0,2:T(4,128)(2,1)} %copy.5), kind=kOutput, calls=%fused_computation.44 | convolution fusion | flops 4194304 | bytes 2752512 | tf_op jit(solution)/shard_map/wsf,wrf->rsf/dot_general | solution.py:40
  88.6 4.8 %fusion.38 = f32[2048,32,8]{1,2,0:T(8,128)} fusion(bf16[4,32,2048]{1,0,2:T(4,128)(2,1)S(1)} %copy.7, bf16[4,8,2048]{1,0,2:T(4,128)(2,1)S(1)} %copy-done.2), kind=kOutput, calls=%fused_computation.46 | convolution fusion | flops 4194304 | bytes 2752512 | tf_op jit(solution)/shard_map/wsf,wrf->rsf/dot_general | solution.py:44
  93.4 4.8 %fusion.37 = f32[2048,32,8]{1,2,0:T(8,128)} fusion(bf16[4,32,2048]{1,0,2:T(4,128)(2,1)S(1)} %copy.7, bf16[4,8,2048]{1,0,2:T(4,128)(2,1)S(1)} %copy-done.1), kind=kOutput, calls=%fused_computation.45 | convolution fusion | flops 4194304 | bytes 2752512 | tf_op jit(solution)/shard_map/wsf,wrf->rsf/dot_general | solution.py:41
  98.2 4.8 %fusion.39 = f32[2048,32,8]{1,2,0:T(8,128)} fusion(bf16[4,32,2048]{1,0,2:T(4,128)(2,1)S(1)} %copy-done, bf16[4,8,2048]{1,0,2:T(4,128)(2,1)S(1)} %copy-done.1), kind=kOutput, calls=%fused_computation.47 | convolution fusion | flops 4194304 | bytes 2752512 | tf_op jit(solution)/shard_map/wsf,wrf->rsf/dot_general | solution.py:45
  102.9 6.7 %copy.6 = f32[2048,32,8]{0,2,1:T(8,128)} copy(f32[2048,32,8]{1,2,0:T(8,128)} %fusion.36) | data formatting | bytes 4194304 | tf_op jit(solution)/shard_map/wsf,wrf->rsf/dot_general | solution.py:40
  109.6 6.6 %copy.9 = f32[2048,32,8]{0,2,1:T(8,128)} copy(f32[2048,32,8]{1,2,0:T(8,128)} %fusion.37) | data formatting | bytes 4194304 | tf_op jit(solution)/shard_map/wsf,wrf->rsf/dot_general | solution.py:41
  116.2 6.6 %copy.10 = f32[2048,32,8]{0,2,1:T(8,128)} copy(f32[2048,32,8]{1,2,0:T(8,128)} %fusion.38) | data formatting | bytes 4194304 | tf_op jit(solution)/shard_map/wsf,wrf->rsf/dot_general | solution.py:44
  122.8 6.6 %copy.11 = f32[2048,32,8]{0,2,1:T(8,128)} copy(f32[2048,32,8]{1,2,0:T(8,128)} %fusion.39) | data formatting | bytes 4194304 | tf_op jit(solution)/shard_map/wsf,wrf->rsf/dot_general | solution.py:45
  129.4 2.7 add_bitcast_fusion.1
  135.8 2.5 copy.12
  138.3 7.3 %fusion.40 = f32[2048,32,8]{1,2,0:T(8,128)} fusion(bf16[4,32,2048]{1,0,2:T(4,128)(2,1)} %copy.4, bf16[4,8,2048]{1,0,2:T(4,128)(2,1)} %copy.12), kind=kOutput, calls=%fused_computation.48 | convolution fusion | flops 4194304 | bytes 2752512 | tf_op jit(solution)/shard_map/wsf,wrf->rsf/dot_general | solution.py:40
  145.6 6.6 %copy.13 = f32[2048,32,8]{0,2,1:T(8,128)} copy(f32[2048,32,8]{1,2,0:T(8,128)} %fusion.40) | data formatting | bytes 4194304 | tf_op jit(solution)/shard_map/wsf,wrf->rsf/dot_general | solution.py:40
  154.7 6.0 %fusion.41 = f32[2048,32,8]{1,2,0:T(8,128)} fusion(bf16[4,32,2048]{1,0,2:T(4,128)(2,1)S(1)} %copy.7, bf16[4,8,2048]{1,0,2:T(4,128)(2,1)} %copy.14), kind=kOutput, calls=%fused_computation.49 | convolution fusion | flops 4194304 | bytes 2752512 | tf_op jit(solution)/shard_map/wsf,wrf->rsf/dot_general | solution.py:41
  160.7 6.7 %copy.15 = f32[2048,32,8]{0,2,1:T(8,128)} copy(f32[2048,32,8]{1,2,0:T(8,128)} %fusion.41) | data formatting | bytes 4194304 | tf_op jit(solution)/shard_map/wsf,wrf->rsf/dot_general | solution.py:41
  167.4 7.2 %fusion.43 = f32[2048,32,8]{1,2,0:T(8,128)} fusion(bf16[4,32,2048]{1,0,2:T(4,128)(2,1)} %copy.4, bf16[4,8,2048]{1,0,2:T(4,128)(2,1)} %copy.14), kind=kOutput, calls=%fused_computation.51 | convolution fusion | flops 4194304 | bytes 2752512 | tf_op jit(solution)/shard_map/wsf,wrf->rsf/dot_general | solution.py:45
  174.6 6.7 %copy.17 = f32[2048,32,8]{0,2,1:T(8,128)} copy(f32[2048,32,8]{1,2,0:T(8,128)} %fusion.43) | data formatting | bytes 4194304 | tf_op jit(solution)/shard_map/wsf,wrf->rsf/dot_general | solution.py:45
  181.3 6.0 %fusion.42 = f32[2048,32,8]{1,2,0:T(8,128)} fusion(bf16[4,32,2048]{1,0,2:T(4,128)(2,1)S(1)} %copy.7, bf16[4,8,2048]{1,0,2:T(4,128)(2,1)} %copy.12), kind=kOutput, calls=%fused_computation.50 | convolution fusion | flops 4194304 | bytes 2752512 | tf_op jit(solution)/shard_map/wsf,wrf->rsf/dot_general | solution.py:44
  187.4 6.8 %copy.16 = f32[2048,32,8]{0,2,1:T(8,128)} copy(f32[2048,32,8]{1,2,0:T(8,128)} %fusion.42) | data formatting | bytes 4194304 | tf_op jit(solution)/shard_map/wsf,wrf->rsf/dot_general | solution.py:44
  199.8 18.0 %fusion.15 = (f32[2048,512]{1,0:T(8,128)}, f32[2048,512]{1,0:T(8,128)}) fusion(s32[512]{0:T(512)S(1)} %iota_add_fusion), kind=kLoop, calls=%fused_computation.24 | loop fusion | flops 15728640 | bytes 8390656 | tf_op jit(solution)/shard_map/cos | solution.py:23
  217.8 9.8 %fusion.25 = bf16[1,8,8,512]{3,2,1,0:T(8,128)(2,1)S(1)} fusion(f32[8,8,4096]{2,1,0:T(8,128)} %reduce-scatter.3.cloned.1.call-done, f32[2048,512]{1,0:T(8,128)} %get-tuple-element.16, f32[2048,512]{1,0:T(8,128)} %get-tuple-element.15), kind=kOutput, calls=%fused_computation.30 | convolution fusion | flops 1614839808 | bytes 9502720 | tf_op jit(solution)/shard_map/dot_general | solution.py:52
  227.7 63.8 %reduce-scatter.5.cloned.1.call-done = f32[8,8,4096]{2,1,0:T(8,128)} async-done(((f32[32,8,4096]{2,1,0:T(8,128)}), f32[8,8,4096]{2,1,0:T(8,128)}) %reduce-scatter.5.cloned.1.call-update) | async-done | bytes 1048592 | tf_op jit(solution)/shard_map/reduce_scatter | solution.py:76
  291.4 9.1 %fusion.22 = bf16[1,8,8,512]{3,2,1,0:T(8,128)(2,1)S(1)} fusion(f32[8,8,4096]{2,1,0:T(8,128)} %reduce-scatter.5.cloned.1.call-done, f32[2048,512]{1,0:T(8,128)} %get-tuple-element.16, f32[2048,512]{1,0:T(8,128)} %get-tuple-element.15), kind=kOutput, calls=%fused_computation.29 | convolution fusion | flops 1614839808 | bytes 9502720 | tf_op jit(solution)/shard_map/dot_general | solution.py:52
  (42 shorter events, 25.9 us)
Async XLA Ops:
  6.5 68.6 %all-reduce.3.cloned.1.call-start = ((), (), s32[]{:S(2)}) async-start(), calls=%async_computation.4 | async-start | bytes 1048576 | tf_op jit(solution)/shard_map/psum | solution.py:15
  17.7 200.2 %reduce-scatter.3.cloned.1.call-start = ((), (), s32[]{:S(2)}) async-start(), calls=%async_computation.2 | async-start | bytes 5242880 | tf_op jit(solution)/shard_map/reduce_scatter | solution.py:76
  81.2 7.4 %copy-start.2 = (bf16[4,8,2048]{1,0,2:T(4,128)(2,1)S(1)}, bf16[4,8,2048]{1,0,2:T(4,128)(2,1)}, u32[]{:S(2)}) copy-start(bf16[4,8,2048]{1,0,2:T(4,128)(2,1)} %copy.5) | copy-start | bytes 393220
  88.6 4.8 %copy-start.1 = (bf16[4,8,2048]{1,0,2:T(4,128)(2,1)S(1)}, bf16[4,8,2048]{1,0,2:T(4,128)(2,1)}, u32[]{:S(2)}) copy-start(bf16[4,8,2048]{1,0,2:T(4,128)(2,1)} %copy.8) | copy-start | bytes 393220
  93.4 4.8 %copy-start = (bf16[4,32,2048]{1,0,2:T(4,128)(2,1)S(1)}, bf16[4,32,2048]{1,0,2:T(4,128)(2,1)}, u32[]{:S(2)}) copy-start(bf16[4,32,2048]{1,0,2:T(4,128)(2,1)} %copy.4) | copy-start | bytes 1572868
  129.4 2.9 copy-start.5
  129.4 3.5 %copy-start.6 = (f32[2048,32,8]{0,2,1:T(8,128)S(1)}, f32[2048,32,8]{0,2,1:T(8,128)}, u32[]{:S(2)}) copy-start(f32[2048,32,8]{0,2,1:T(8,128)} %copy.11) | copy-start | bytes 6291460
  135.6 155.8 %reduce-scatter.5.cloned.1.call-start = ((), (), s32[]{:S(2)}) async-start(), calls=%async_computation.3 | async-start | bytes 5242880 | tf_op jit(solution)/shard_map/reduce_scatter | solution.py:76
  187.4 6.8 %copy-start.3 = (f32[2048,32,8]{0,2,1:T(8,128)S(1)}, f32[2048,32,8]{0,2,1:T(8,128)}, u32[]{:S(2)}) copy-start(f32[2048,32,8]{0,2,1:T(8,128)} %copy.13) | copy-start | bytes 6291460
  194.2 2.3 copy-start.4
  194.2 2.9 copy-start.7
Sparse Core Ops, SparseCore 0:
  17.8 57.3 all-reduce.2
  135.7 76.0 reduce-scatter.2
  214.1 77.2 reduce-scatter.4
where the time goes:
time: 309 us; the launch traced here: 308 us
  waiting for transfers between devices  117 us (38%)
  local copies, waits for them, and re-layouts  71.1 us (23%)
  matrix products  67.2 us (22%)
  other arithmetic  33.4 us (11%)
  between operations  18.4 us (6%)
    reduce_scatter x2, waiting for transfers between devices, body(): lax.psum_scatter(partial_cross, 'win', scatter_dimension=0, tiled=True)  63.8 us
    psum x1, waiting for transfers between devices, from_root(): return lax.psum(kept, axis)  53.5 us
    dot_general x2, matrix products, apply_lags(): jnp.dot(cross.reshape(-1, cross.shape[-1]), transform, precision=lax.Prec...  18.9 us
    cos x1, other arithmetic, lag_table(): jnp.cos(phase_angle)  18 us
    dot_general x2, matrix products, cross_spectra(): jnp.einsum('wsf,wrf->rsf', src_real, rec_real, preferred_element_type=jnp...  14.7 us
    dot_general x2, local copies, waits for them, and re-layouts, cross_spectra(): jnp.einsum('wsf,wrf->rsf', src_real, rec_imag, preferred_element_type=jnp...  13.4 us
    dot_general x2, local copies, waits for them, and re-layouts, cross_spectra(): jnp.einsum('wsf,wrf->rsf', src_real, rec_real, preferred_element_type=jnp...  13.3 us
    dot_general x2, local copies, waits for them, and re-layouts, cross_spectra(): jnp.einsum('wsf,wrf->rsf', src_imag, rec_real, preferred_element_type=jnp...  13.3 us
  transfers between devices with their start and end apart: 3, of which 2 were waited for; matrix products, arithmetic and copies ran while one was open for 31% of the time, Pallas kernels for 0%

commit v1 on v0

v1 whole, which is shorter than its diff:
```python
import functools
import math

import jax
import jax.numpy as jnp
from jax import lax
from jax.experimental import pallas as pl
from jax.experimental.pallas import tpu as pltpu
from jax.sharding import PartitionSpec as P

L = 512
SRC = 8
STEPS = 2
LANES = 128
BINS_PER_CHUNK = 256
TABLE_ROWS = 64
EPS = 1e-06
F32 = jnp.float32
BF16 = jnp.bfloat16
VMEM_LIMIT = 48 * 1024 * 1024


def smem():
    return pl.BlockSpec(memory_space=pltpu.SMEM)


def vmem():
    return pl.BlockSpec(memory_space=pltpu.VMEM)


def params():
    return pltpu.CompilerParams(vmem_limit_bytes=VMEM_LIMIT)


def column(count, read):
    rows = lax.broadcasted_iota(jnp.int32, (count, 1), 0)
    result = jnp.zeros((count, 1), F32)
    for row in range(count):
        result = jnp.where(rows == row, read(row), result)
    return result


def whitened_rows(values, quality):
    energy = jnp.sum(values * values, axis=-1, keepdims=True) / (values.shape[-1] // 2)
    return (values * (quality / jnp.sqrt(energy + EPS))).astype(BF16)


def sources_kernel(scalars, quality, spectra, mine, other):
    for place, out in enumerate((mine, other)):
        held, base = scalars[1 + 2 * place], scalars[2 + 2 * place]
        aligned = pl.multiple_of(base // 16 * 16, 16)
        upper = base % 16 != 0
        flags = column(SRC, lambda row: (quality[base + row] * held).astype(F32))
        for window in range(spectra.shape[0]):
            rows = spectra[window, pl.ds(aligned, 16), :].astype(F32)
            values = jnp.where(upper, rows[SRC:], rows[:SRC])
            out[window] = whitened_rows(values, flags)


def receivers_kernel(quality, spectra, out):
    owners, windows, rows, _ = out.shape
    flags = column(owners * rows, lambda row: quality[row].astype(F32))
    for window in range(windows):
        values = whitened_rows(spectra[window].astype(F32), flags).astype(F32)
        for owner in range(owners):
            out[owner, window] = values[owner * rows : (owner + 1) * rows]


def table_kernel(factor, out, turn_cos, turn_sin, base_cos, base_sin):
    bins, lags = out.shape[0] // 2, out.shape[1]

    def angles(count, stride):
        rows = lax.broadcasted_iota(jnp.int32, (count, lags), 0) * stride
        shifts = lax.broadcasted_iota(jnp.int32, (count, lags), 1) - lags // 2
        residue = (rows * shifts) & (2 * bins - 1)
        residue = jnp.where(residue >= bins, residue - 2 * bins, residue)
        return residue.astype(F32) * (2.0 * math.pi / (2 * bins))

    turns = angles(bins // TABLE_ROWS, TABLE_ROWS)
    turn_cos[...] = jnp.cos(turns) * factor
    turn_sin[...] = jnp.sin(turns) * factor
    base = angles(TABLE_ROWS, 1)
    base_cos[...] = jnp.cos(base)
    base_sin[...] = jnp.sin(base)

    @pl.loop(0, bins // TABLE_ROWS)
    def _(turn):
        far_cos, far_sin = turn_cos[pl.ds(turn, 1), :], turn_sin[pl.ds(turn, 1), :]
        near_cos, near_sin = base_cos[...], base_sin[...]
        start = pl.multiple_of(turn * TABLE_ROWS, TABLE_ROWS)
        out[pl.ds(start, TABLE_ROWS), :] = (near_cos * far_cos - near_sin * far_sin).astype(BF16)
        out[pl.ds(bins + start, TABLE_ROWS), :] = (
            -(near_sin * far_cos + near_cos * far_sin)
        ).astype(BF16)


def lagged_kernel(owners, mine, other, receivers, table, *rest):
    outs, (even, odd, total) = rest[:-3], rest[-3:]
    _, windows, rows, width = receivers.shape
    bins = width // 2
    chunk = BINS_PER_CHUNK
    chunks = bins // chunk

    def cross(index, held):
        for tile in range(chunk // LANES):
            at = index * chunk + tile * LANES
            if not isinstance(index, int):
                at = pl.multiple_of(at, LANES)
            real, imag = pl.ds(at, LANES), pl.ds(bins + at, LANES)
            sources = [
                [(ref[w, :, real].astype(F32), ref[w, :, imag].astype(F32)) for w in range(windows)]
                for ref in (mine, other)
            ]
            for place in range(len(outs)):
                owner = owners[place]
                for row in range(rows):
                    sums = [[None, None], [None, None]]
                    for w in range(windows):
                        rec_real = receivers[owner, w, pl.ds(row, 1), real]
                        rec_imag = receivers[owner, w, pl.ds(row, 1), imag]
                        for s in range(2):
                            src_real, src_imag = sources[s][w]
                            re = src_real * rec_real + src_imag * rec_imag
                            im = src_real * rec_imag - src_imag * rec_real
                            sums[s][0] = re if w == 0 else sums[s][0] + re
                            sums[s][1] = im if w == 0 else sums[s][1] + im
                    start = (place * rows + row) * 2 * SRC
                    for part in range(2):
                        both = jnp.concatenate([sums[0][part], sums[1][part]], axis=0)
                        lane = part * chunk + tile * LANES
                        held[start : start + 2 * SRC, lane : lane + LANES] = both.astype(BF16)

    def lags(index, held, first=False):
        at = index * chunk
        if not isinstance(index, int):
            at = pl.multiple_of(at, chunk)
        product = jnp.dot(
            held[:, :chunk], table[pl.ds(at, chunk), :], preferred_element_type=F32
        ) + jnp.dot(
            held[:, chunk:], table[pl.ds(bins + at, chunk), :], preferred_element_type=F32
        )
        total[...] = product if first else total[...] + product

    cross(0, even)
    cross(1, odd)
    lags(0, even, first=True)

    @pl.loop(0, chunks // 2 - 1)
    def _(pair):
        cross(2 * pair + 2, even)
        lags(2 * pair + 1, odd)
        cross(2 * pair + 3, odd)
        lags(2 * pair + 2, even)

    lags(chunks - 1, odd)
    for place, out in enumerate(outs):
        for row in range(rows):
            start = (place * rows + row) * 2 * SRC
            out[row] = total[start : start + 2 * SRC, :].astype(out.dtype)


def stack_kernel(scalars, own, *rest):
    received, out = rest[:-1], rest[-1]
    step = scalars[0]
    for row in range(own.shape[0]):
        total = own[row]
        for ref in received:
            total = total + ref[row].astype(F32)
        out[step, row] = total[:SRC].astype(BF16)
        out[1 - step, row] = total[SRC:].astype(BF16)


def lagged_call(owners, mine, other, receivers, table, dtype):
    count = owners.shape[0]
    _, windows, rows, width = receivers.shape
    lines = count * rows * 2 * SRC
    shape = jax.ShapeDtypeStruct((rows, 2 * SRC, L), dtype)
    return pl.pallas_call(
        lagged_kernel,
        out_shape=[shape] * count,
        in_specs=[smem(), vmem(), vmem(), vmem(), vmem()],
        out_specs=[vmem()] * count,
        scratch_shapes=[
            pltpu.VMEM((lines, 2 * BINS_PER_CHUNK), BF16),
            pltpu.VMEM((lines, 2 * BINS_PER_CHUNK), BF16),
            pltpu.VMEM((lines, L), F32),
        ],
        compiler_params=params(),
        cost_estimate=pl.CostEstimate(
            flops=2 * lines * width * L, bytes_accessed=2 * width * L, transcendentals=0
        ),
    )(owners, mine, other, receivers, table)


def exchange(value, axis, distance):
    size = lax.axis_size(axis)
    return lax.ppermute(value, axis, [(i, i ^ distance) for i in range(size)])


def body(spectra, quality, source_block):
    windows, channels, width = spectra.shape
    group, groups = lax.axis_index("chan"), lax.axis_size("chan")
    place, places = lax.axis_index("win"), lax.axis_size("win")
    bins = width // 2
    rows = channels // places
    factor = 1.0 / math.sqrt(width * windows * places)

    core = group % 2
    blocks = jnp.stack([source_block[core], source_block[1 - core]]).astype(jnp.int32)
    per_group = channels // SRC
    held = (blocks // per_group == group).astype(jnp.int32)
    base = blocks % per_group * SRC
    scalars = jnp.stack([core, held[0], base[0], held[1], base[1]]).astype(jnp.int32)

    candidate = jax.ShapeDtypeStruct((windows, SRC, width), BF16)
    mine, other = pl.pallas_call(
        sources_kernel,
        out_shape=[candidate, candidate],
        in_specs=[smem(), smem(), vmem()],
        out_specs=[vmem(), vmem()],
        compiler_params=params(),
    )(scalars, quality, spectra)

    receivers = pl.pallas_call(
        receivers_kernel,
        out_shape=jax.ShapeDtypeStruct((places, windows, rows, width), F32),
        in_specs=[smem(), vmem()],
        out_specs=vmem(),
        compiler_params=params(),
    )(quality, spectra)
    table = pl.pallas_call(
        functools.partial(table_kernel, factor),
        out_shape=jax.ShapeDtypeStruct((width, L), BF16),
        out_specs=vmem(),
        scratch_shapes=[pltpu.VMEM((bins // TABLE_ROWS, L), F32)] * 2
        + [pltpu.VMEM((TABLE_ROWS, L), F32)] * 2,
        compiler_params=params(),
    )()

    both = mine + exchange(other, "chan", 1)
    halves = [both[: windows // 2], both[windows // 2 :]]
    distances = [1 << bit for bit in range(1, (groups - 1).bit_length())]
    for one, two in zip(distances, reversed(distances), strict=True):
        halves = [halves[0] + exchange(halves[0], "chan", one), halves[1] + exchange(halves[1], "chan", two)]
    mine = jnp.concatenate(halves)
    other = exchange(mine, "chan", 1)

    far_first = sorted(range(1, places), key=lambda d: (-(d.bit_length()), d))
    received = []
    for distance in far_first:
        owners = jnp.reshape(place ^ distance, (1,)).astype(jnp.int32)
        (partial,) = lagged_call(owners, mine, other, receivers, table, BF16)
        received.append(exchange(partial, "win", distance))
    owners = jnp.reshape(place, (1,)).astype(jnp.int32)
    (own,) = lagged_call(owners, mine, other, receivers, table, F32)

    return pl.pallas_call(
        stack_kernel,
        out_shape=jax.ShapeDtypeStruct((STEPS, rows, SRC, L), BF16),
        in_specs=[smem(), vmem()] + [vmem()] * len(received),
        out_specs=vmem(),
        compiler_params=params(),
    )(scalars, own, *received)


def solution(mesh):
    return jax.shard_map(
        body,
        mesh=mesh,
        in_specs=(P("win", "chan", None), P("chan"), P()),
        out_specs=P(None, ("chan", "win"), None, None),
        check_vma=False,
    )
```

time: 309 us -> 56.3 us (0.18)
  waiting for transfers between devices: 117 us -> 9.92 us
  matrix products: 67.2 us -> 0 us
  local copies, waits for them, and re-layouts: 71.1 us -> 8.49 us
  other arithmetic: 33.4 us -> 2.84 us
  Pallas kernels: 0 us -> 22.9 us
  between operations: 18.4 us -> 0.15 us
  starting transfers between devices: 0.27 us -> 11.5 us
    dot_general x10 -> x0, matrix products: 67.2 us -> none  [the longest x2 18.9 us: apply_lags(): jnp.dot(cross.reshape(-1, cross.shape[-1]), transform, precision=lax.Prec...]
    reduce_scatter x2 -> x0, waiting for transfers between devices: 63.8 us -> none  [body(): lax.psum_scatter(partial_cross, 'win', scatter_dimension=0, tiled=True)]
    psum x1 -> x0, waiting for transfers between devices: 53.5 us -> none  [from_root(): return lax.psum(kept, axis)]
    dot_general x8 -> x0, local copies, waits for them, and re-layouts: 53.3 us -> none  [the longest x2 13.4 us: cross_spectra(): jnp.einsum('wsf,wrf->rsf', src_real, rec_imag, preferred_element_type=jnp...]
    pallas_call x0 -> x8, Pallas kernels: none -> 22.9 us  [the longest x4 17.7 us: lagged_call(): pl.pallas_call(lagged_kernel, out_shape=[shape] * count, in_specs=[smem()...]
    cos x1 -> x0, other arithmetic: 18 us -> none  [lag_table(): jnp.cos(phase_angle)]
    slice x9 -> x2, local copies, waits for them, and re-layouts: 16.2 us -> 0.68 us  [the longest x1 0.67 us: body(): base[1]]
    ppermute x0 -> x9, starting transfers between devices: none -> 11.5 us  [exchange(): return lax.ppermute(value, axis, [(i, i ^ distance) for i in range(size)])]
  transfers between devices with their start and end apart: 3 -> 9, of which waited for: 2 -> 6; matrix products, arithmetic and copies ran while one was open for 31% -> 0% of each run, Pallas kernels for 0% -> 29%
where the time goes in v1:
time: 56.3 us; the launch traced here: 55.9 us
  Pallas kernels  22.9 us (41%)
  starting transfers between devices  11.5 us (20%)
  waiting for transfers between devices  9.92 us (18%)
  local copies, waits for them, and re-layouts  8.49 us (15%)
  other arithmetic  2.84 us (5%)
    pallas_call x4, Pallas kernels, lagged_call(): pl.pallas_call(lagged_kernel, out_shape=[shape] * count, in_specs=[smem()...  17.7 us
    ppermute x9, starting transfers between devices, exchange(): return lax.ppermute(value, axis, [(i, i ^ distance) for i in range(size)])  11.5 us
    ppermute x9, waiting for transfers between devices, exchange(): return lax.ppermute(value, axis, [(i, i ^ distance) for i in range(size)])  9.92 us
    unnamed x10, local copies, waits for them, and re-layouts  3.83 us
    another operation x1, local copies, waits for them, and re-layouts, body(): jnp.stack([core, held[0], base[0], held[1], base[1]]).astype(jnp.int32)  2.58 us
    pallas_call x1, Pallas kernels, body(): pl.pallas_call(functools.partial(table_kernel, factor), out_shape=jax.Sha...  2.09 us
    dynamic_slice x1, local copies, waits for them, and re-layouts, body(): source_block[core]  1.39 us
    mul x1, other arithmetic, body(): base = blocks % per_group * SRC  1.33 us
  transfers between devices with their start and end apart: 9, of which 6 were waited for; matrix products, arithmetic and copies ran while one was open for 0% of the time, Pallas kernels for 29%

profile of v1, /device:TPU:0, one launch (start us, length us, event | category | flops | bytes accessed | tf_op | source)
XLA Modules:
  0.0 55.9 jit_solution(11362951787378091607)
XLA Ops:
  0.0 1.4 %fusion.4 = (s32[1]{0:T(128)}, s32[1]{0:T(128)}) fusion(s32[2]{0:T(128)} %param.5, s32[]{:T(128)S(6)} %select_n.25, s32[]{:T(128)S(6)} %select_n.26), kind=kLoop, calls=%fused_computation.14 | loop fusion | bytes 24 | tf_op jit(solution)/shard_map/dynamic_slice | solution.py:209
  1.4 1.3 %fusion = (s32[2]{0:T(128)S(1)}, s32[2]{0:T(128)S(1)}) fusion(s32[1]{0:T(128)} %get-tuple-element.20, s32[1]{0:T(128)} %get-tuple-element.19), kind=kLoop, calls=%fused_computation.7 | loop fusion | flops 26 | bytes 24 | tf_op jit(solution)/shard_map/mul | solution.py:212
  2.7 1.3 %compare_convert_fusion = s32[2]{0:T(128)S(1)} fusion(s32[2]{0:T(128)S(1)} %get-tuple-element.10, s32[]{:T(128)S(6)} %axis_index.23, s32[1]{0:T(128)} %get-tuple-element.20, s32[1]{0:T(128)} %get-tuple-element.19), kind=kLoop, calls=%fused_computation.2 | loop fusion | flops 30 | bytes 28 | tf_op jit(solution)/shard_map/convert_element_type | solution.py:211
  4.7 2.6 %stack.11.scalars = s32[5]{0:T(128)S(1)} concatenate(s32[1]{0:T(128)} %bitcast, s32[1]{0:T(128)} %get-tuple-element.21, s32[1]{0:T(128)} %get-tuple-element.16, s32[1]{0:T(128)} %get-tuple-element.22, s32[1]{0:T(128)} %get-tuple-element.15), dimensions={0} | concatenate | bytes 40 | tf_op jit(solution)/shard_map/stack | solution.py:213
  7.3 1.2 %copy-done.1 = bf16[4,32,4096]{2,1,0:T(8,128)(2,1)S(1)} copy-done((bf16[4,32,4096]{2,1,0:T(8,128)(2,1)S(1)}, bf16[4,32,4096]{2,1,0:T(8,128)(2,1)}, u32[]{:S(2)}) %copy-start.1) | copy-done | bytes 1048600
  9.2 0.8 %shard_map.37 = (bf16[4,8,4096]{2,1,0:T(8,128)(2,1)S(1)}, bf16[4,8,4096]{2,1,0:T(8,128)(2,1)S(1)}) custom-call(s32[5]{0:T(128)S(1)} %stack.11.scalars, s32[32]{0:T(128)S(1)} %copy-done.3, bf16[4,32,4096]{2,1,0:T(8,128)(2,1)S(1)} %copy-done.1), custom_call_target="tpu_custom_call" | custom-call | tf_op jit(solution)/shard_map/pallas_call | solution.py:216
  10.5 1.2 %collective-permute-done = bf16[4,8,4096]{2,1,0:T(8,128)(2,1)S(1)} collective-permute-done((bf16[4,8,4096]{2,1,0:T(8,128)(2,1)S(1)}, bf16[4,8,4096]{2,1,0:T(8,128)(2,1)S(1)}, u32[]{:S(2)}, u32[]{:S(2)}) %collective-permute-start) | collective-permute-done | bytes 262176 | tf_op jit(solution)/shard_map/ppermute | solution.py:197
  11.8 2.9 %collective-permute-start.1 = (bf16[2,8,4096]{2,1,0:T(8,128)(2,1)S(1)}, bf16[2,8,4096]{2,1,0:T(8,128)(2,1)S(1)}, u32[]{:S(2)}, u32[]{:S(2)}) collective-permute-start(bf16[2,8,4096]{2,1,0:T(8,128)(2,1)S(1)} %get-tuple-element.13), channel_id=1, source_target_pairs={{0,8},{4,12},{8,0},{12,4},{16,24},{20,28},{24,16},{28,20},{1,9},{5... | collective-permute-start | bytes 393224 | tf_op jit(solution)/shard_map/ppermute | solution.py:197
  14.7 1.5 %collective-permute-start.3 = (bf16[2,8,4096]{2,1,0:T(8,128)(2,1)S(1)}, bf16[2,8,4096]{2,1,0:T(8,128)(2,1)S(1)}, u32[]{:S(2)}, u32[]{:S(2)}) collective-permute-start(bf16[2,8,4096]{2,1,0:T(8,128)(2,1)S(1)} %get-tuple-element.14), channel_id=1, source_target_pairs={{0,16},{4,20},{8,24},{12,28},{16,0},{20,4},{24,8},{28,12},{1,17},{... | collective-permute-start | bytes 393224 | tf_op jit(solution)/shard_map/ppermute | solution.py:197
  16.2 2.3 %collective-permute-done.1 = bf16[2,8,4096]{2,1,0:T(8,128)(2,1)S(1)} collective-permute-done((bf16[2,8,4096]{2,1,0:T(8,128)(2,1)S(1)}, bf16[2,8,4096]{2,1,0:T(8,128)(2,1)S(1)}, u32[]{:S(2)}, u32[]{:S(2)}) %collective-permute-start.1) | collective-permute-done | bytes 131104 | tf_op jit(solution)/shard_map/ppermute | solution.py:197
  18.5 1.5 %collective-permute-done.3 = bf16[2,8,4096]{2,1,0:T(8,128)(2,1)S(1)} collective-permute-done((bf16[2,8,4096]{2,1,0:T(8,128)(2,1)S(1)}, bf16[2,8,4096]{2,1,0:T(8,128)(2,1)S(1)}, u32[]{:S(2)}, u32[]{:S(2)}) %collective-permute-start.3) | collective-permute-done | bytes 131104 | tf_op jit(solution)/shard_map/ppermute | solution.py:197
  20.0 1.6 %collective-permute-start.2 = (bf16[2,8,4096]{2,1,0:T(8,128)(2,1)S(1)}, bf16[2,8,4096]{2,1,0:T(8,128)(2,1)S(1)}, u32[]{:S(2)}, u32[]{:S(2)}) collective-permute-start(bf16[2,8,4096]{2,1,0:T(8,128)(2,1)S(1)} %get-tuple-element.11), channel_id=1, source_target_pairs={{0,16},{4,20},{8,24},{12,28},{16,0},{20,4},{24,8},{28,12},{1,17},{... | collective-permute-start | bytes 393224 | tf_op jit(solution)/shard_map/ppermute | solution.py:197
  22.1 2.9 %collective-permute-done.2 = bf16[2,8,4096]{2,1,0:T(8,128)(2,1)S(1)} collective-permute-done((bf16[2,8,4096]{2,1,0:T(8,128)(2,1)S(1)}, bf16[2,8,4096]{2,1,0:T(8,128)(2,1)S(1)}, u32[]{:S(2)}, u32[]{:S(2)}) %collective-permute-start.2) | collective-permute-done | bytes 131104 | tf_op jit(solution)/shard_map/ppermute | solution.py:197
  25.1 1.5 %collective-permute-done.4 = bf16[2,8,4096]{2,1,0:T(8,128)(2,1)S(1)} collective-permute-done((bf16[2,8,4096]{2,1,0:T(8,128)(2,1)S(1)}, bf16[2,8,4096]{2,1,0:T(8,128)(2,1)S(1)}, u32[]{:S(2)}, u32[]{:S(2)}) %collective-permute-start.4) | collective-permute-done | bytes 131104 | tf_op jit(solution)/shard_map/ppermute | solution.py:197
  26.7 1.1 %shard_map.38.receivers = f32[4,4,8,4096]{3,2,1,0:T(8,128)S(1)} custom-call(s32[32]{0:T(128)S(1)} %copy-done.4, bf16[4,32,4096]{2,1,0:T(8,128)(2,1)S(1)} %copy-done.2), custom_call_target="tpu_custom_call" | custom-call | tf_op jit(solution)/shard_map/pallas_call | solution.py:224
  27.8 2.1 %shard_map.39.table = bf16[4096,512]{1,0:T(8,128)(2,1)S(1)} custom-call(), custom_call_target="tpu_custom_call" | custom-call | tf_op jit(solution)/shard_map/pallas_call | solution.py:231
  29.9 1.9 %copy-done = bf16[4096,512]{1,0:T(8,128)(2,1)} copy-done((bf16[4096,512]{1,0:T(8,128)(2,1)}, bf16[4096,512]{1,0:T(8,128)(2,1)S(1)}, u32[]{:S(2)}) %copy-start) | copy-done | bytes 4194328
  31.9 4.4 %shard_map.41 = bf16[8,16,512]{2,1,0:T(8,128)(2,1)S(1)} custom-call(s32[1]{0:T(128)} %bitcast.2.owners, bf16[4,8,4096]{2,1,0:T(8,128)(2,1)S(1)} %pad_maximum_fusion.mine, bf16[4,8,4096]{2,1,0:T(8,128)(2,1)S(1)} %collective-permute-done.5.other, f32[4,4,8,4096]{3,2,1,0:T(8,128)S(1)} %shard_map.38.receivers, bf16[4096,512]{1,0:T(8,128)(2,1)} %copy-done), custom_call_target="tpu_custom_call" | custom-call | flops 536870912 | bytes 4194304 | tf_op jit(solution)/shard_map/pallas_call | solution.py:178
  36.3 2.7 %collective-permute-start.6 = (bf16[8,16,512]{2,1,0:T(8,128)(2,1)S(1)}, bf16[8,16,512]{2,1,0:T(8,128)(2,1)S(1)}, u32[]{:S(2)}, u32[]{:S(2)}) collective-permute-start(bf16[8,16,512]{2,1,0:T(8,128)(2,1)S(1)} %shard_map.41), channel_id=1, source_target_pairs={{0,2},{1,3},{2,0},{3,1},{4,6},{5,7},{6,4},{7,5},{8,10},{9,11},{10,... | collective-permute-start | bytes 393224 | tf_op jit(solution)/shard_map/ppermute | solution.py:197
  39.0 4.4 %shard_map.42 = bf16[8,16,512]{2,1,0:T(8,128)(2,1)S(1)} custom-call(s32[1]{0:T(128)} %bitcast.3.owners, bf16[4,8,4096]{2,1,0:T(8,128)(2,1)S(1)} %pad_maximum_fusion.mine, bf16[4,8,4096]{2,1,0:T(8,128)(2,1)S(1)} %collective-permute-done.5.other, f32[4,4,8,4096]{3,2,1,0:T(8,128)S(1)} %shard_map.38.receivers, bf16[4096,512]{1,0:T(8,128)(2,1)} %copy-done), custom_call_target="tpu_custom_call" | custom-call | flops 536870912 | bytes 4194304 | tf_op jit(solution)/shard_map/pallas_call | solution.py:178
  43.4 1.4 %collective-permute-start.7 = (bf16[8,16,512]{2,1,0:T(8,128)(2,1)S(1)}, bf16[8,16,512]{2,1,0:T(8,128)(2,1)S(1)}, u32[]{:S(2)}, u32[]{:S(2)}) collective-permute-start(bf16[8,16,512]{2,1,0:T(8,128)(2,1)S(1)} %shard_map.42), channel_id=1, source_target_pairs={{0,3},{1,2},{2,1},{3,0},{4,7},{5,6},{6,5},{7,4},{8,11},{9,10},{10,... | collective-permute-start | bytes 393224 | tf_op jit(solution)/shard_map/ppermute | solution.py:197
  44.8 4.4 %shard_map.43 = bf16[8,16,512]{2,1,0:T(8,128)(2,1)S(1)} custom-call(s32[1]{0:T(128)} %bitcast.4.owners, bf16[4,8,4096]{2,1,0:T(8,128)(2,1)S(1)} %pad_maximum_fusion.mine, bf16[4,8,4096]{2,1,0:T(8,128)(2,1)S(1)} %collective-permute-done.5.other, f32[4,4,8,4096]{3,2,1,0:T(8,128)S(1)} %shard_map.38.receivers, bf16[4096,512]{1,0:T(8,128)(2,1)} %copy-done), custom_call_target="tpu_custom_call" | custom-call | flops 536870912 | bytes 4194304 | tf_op jit(solution)/shard_map/pallas_call | solution.py:178
  49.6 4.4 %shard_map.40.own = f32[8,16,512]{2,1,0:T(8,128)S(1)} custom-call(s32[1]{0:T(128)} %bitcast.1.owners, bf16[4,8,4096]{2,1,0:T(8,128)(2,1)S(1)} %pad_maximum_fusion.mine, bf16[4,8,4096]{2,1,0:T(8,128)(2,1)S(1)} %collective-permute-done.5.other, f32[4,4,8,4096]{3,2,1,0:T(8,128)S(1)} %shard_map.38.receivers, bf16[4096,512]{1,0:T(8,128)(2,1)} %copy-done), custom_call_target="tpu_custom_call" | custom-call | flops 536870912 | bytes 4194304 | tf_op jit(solution)/shard_map/pallas_call | solution.py:178
  54.6 1.3 %shard_map.44 = bf16[2,8,8,512]{3,2,1,0:T(8,128)(2,1)} custom-call(s32[5]{0:T(128)S(1)} %stack.11.scalars, f32[8,16,512]{2,1,0:T(8,128)S(1)} %shard_map.40.own, bf16[8,16,512]{2,1,0:T(8,128)(2,1)S(1)} %collective-permute-done.6.rest_0_, bf16[8,16,512]{2,1,0:T(8,128)(2,1)S(1)} %collective-permute-done.7.rest_1_, ...), custom_call_target="tpu_custom_call" | custom-call | tf_op jit(solution)/shard_map/pallas_call | solution.py:257
  (23 shorter events, 3.6 us)
Async XLA Ops:
  0.0 26.7 %copy-start.4 = (s32[32]{0:T(128)S(1)}, s32[32]{0:T(128)}, u32[]{:S(2)}) copy-start(s32[32]{0:T(128)} %quality.3) | copy-start | bytes 388
  7.3 1.2 %copy-start.1 = (bf16[4,32,4096]{2,1,0:T(8,128)(2,1)S(1)}, bf16[4,32,4096]{2,1,0:T(8,128)(2,1)}, u32[]{:S(2)}) copy-start(bf16[4,32,4096]{2,1,0:T(8,128)(2,1)} %spectra.3) | copy-start | bytes 3145732
  8.5 0.7 %copy-start.3 = (s32[32]{0:T(128)S(1)}, s32[32]{0:T(128)}, u32[]{:S(2)}) copy-start(s32[32]{0:T(128)} %quality.3) | copy-start | bytes 388
  9.2 17.6 %copy-start.2 = (bf16[4,32,4096]{2,1,0:T(8,128)(2,1)S(1)}, bf16[4,32,4096]{2,1,0:T(8,128)(2,1)}, u32[]{:S(2)}) copy-start(bf16[4,32,4096]{2,1,0:T(8,128)(2,1)} %spectra.3) | copy-start | bytes 3145732
  10.0 1.7 %collective-permute-start = (bf16[4,8,4096]{2,1,0:T(8,128)(2,1)S(1)}, bf16[4,8,4096]{2,1,0:T(8,128)(2,1)S(1)}, u32[]{:S(2)}, u32[]{:S(2)}) collective-permute-start(bf16[4,8,4096]{2,1,0:T(8,128)(2,1)S(1)} %get-tuple-element.8), channel_id=1, source_target_pairs={{0,4},{4,0},{8,12},{12,8},{16,20},{20,16},{24,28},{28,24},{1,5},{5... | collective-permute-start | bytes 786440 | tf_op jit(solution)/shard_map/ppermute | solution.py:197
  11.8 6.7 %collective-permute-start.1 = (bf16[2,8,4096]{2,1,0:T(8,128)(2,1)S(1)}, bf16[2,8,4096]{2,1,0:T(8,128)(2,1)S(1)}, u32[]{:S(2)}, u32[]{:S(2)}) collective-permute-start(bf16[2,8,4096]{2,1,0:T(8,128)(2,1)S(1)} %get-tuple-element.13), channel_id=1, source_target_pairs={{0,8},{4,12},{8,0},{12,4},{16,24},{20,28},{24,16},{28,20},{1,9},{5... | collective-permute-start | bytes 393224 | tf_op jit(solution)/shard_map/ppermute | solution.py:197
  14.7 5.3 %collective-permute-start.3 = (bf16[2,8,4096]{2,1,0:T(8,128)(2,1)S(1)}, bf16[2,8,4096]{2,1,0:T(8,128)(2,1)S(1)}, u32[]{:S(2)}, u32[]{:S(2)}) collective-permute-start(bf16[2,8,4096]{2,1,0:T(8,128)(2,1)S(1)} %get-tuple-element.14), channel_id=1, source_target_pairs={{0,16},{4,20},{8,24},{12,28},{16,0},{20,4},{24,8},{28,12},{1,17},{... | collective-permute-start | bytes 393224 | tf_op jit(solution)/shard_map/ppermute | solution.py:197
  20.0 5.0 %collective-permute-start.2 = (bf16[2,8,4096]{2,1,0:T(8,128)(2,1)S(1)}, bf16[2,8,4096]{2,1,0:T(8,128)(2,1)S(1)}, u32[]{:S(2)}, u32[]{:S(2)}) collective-permute-start(bf16[2,8,4096]{2,1,0:T(8,128)(2,1)S(1)} %get-tuple-element.11), channel_id=1, source_target_pairs={{0,16},{4,20},{8,24},{12,28},{16,0},{20,4},{24,8},{28,12},{1,17},{... | collective-permute-start | bytes 393224 | tf_op jit(solution)/shard_map/ppermute | solution.py:197
  21.6 5.0 %collective-permute-start.4 = (bf16[2,8,4096]{2,1,0:T(8,128)(2,1)S(1)}, bf16[2,8,4096]{2,1,0:T(8,128)(2,1)S(1)}, u32[]{:S(2)}, u32[]{:S(2)}) collective-permute-start(bf16[2,8,4096]{2,1,0:T(8,128)(2,1)S(1)} %get-tuple-element.12), channel_id=1, source_target_pairs={{0,8},{4,12},{8,0},{12,4},{16,24},{20,28},{24,16},{28,20},{1,9},{5... | collective-permute-start | bytes 393224 | tf_op jit(solution)/shard_map/ppermute | solution.py:197
  26.6 5.2 %collective-permute-start.5 = (bf16[4,8,4096]{2,1,0:T(8,128)(2,1)S(1)}, bf16[4,8,4096]{2,1,0:T(8,128)(2,1)S(1)}, u32[]{:S(2)}, u32[]{:S(2)}) collective-permute-start(bf16[4,8,4096]{2,1,0:T(8,128)(2,1)S(1)} %pad_maximum_fusion.mine), channel_id=1, source_target_pairs={{0,4},{4,0},{8,12},{12,8},{16,20},{20,16},{24,28},{28,24},{1,5},{5... | collective-permute-start | bytes 786440 | tf_op jit(solution)/shard_map/ppermute | solution.py:197
  29.9 2.0 %copy-start = (bf16[4096,512]{1,0:T(8,128)(2,1)}, bf16[4096,512]{1,0:T(8,128)(2,1)S(1)}, u32[]{:S(2)}) copy-start(bf16[4096,512]{1,0:T(8,128)(2,1)S(1)} %shard_map.39.table) | copy-start | bytes 12582916
  36.3 17.7 %collective-permute-start.6 = (bf16[8,16,512]{2,1,0:T(8,128)(2,1)S(1)}, bf16[8,16,512]{2,1,0:T(8,128)(2,1)S(1)}, u32[]{:S(2)}, u32[]{:S(2)}) collective-permute-start(bf16[8,16,512]{2,1,0:T(8,128)(2,1)S(1)} %shard_map.41), channel_id=1, source_target_pairs={{0,2},{1,3},{2,0},{3,1},{4,6},{5,7},{6,4},{7,5},{8,10},{9,11},{10,... | collective-permute-start | bytes 393224 | tf_op jit(solution)/shard_map/ppermute | solution.py:197
  43.4 10.6 %collective-permute-start.7 = (bf16[8,16,512]{2,1,0:T(8,128)(2,1)S(1)}, bf16[8,16,512]{2,1,0:T(8,128)(2,1)S(1)}, u32[]{:S(2)}, u32[]{:S(2)}) collective-permute-start(bf16[8,16,512]{2,1,0:T(8,128)(2,1)S(1)} %shard_map.42), channel_id=1, source_target_pairs={{0,3},{1,2},{2,1},{3,0},{4,7},{5,6},{6,5},{7,4},{8,11},{9,10},{10,... | collective-permute-start | bytes 393224 | tf_op jit(solution)/shard_map/ppermute | solution.py:197
  49.2 5.4 %collective-permute-start.8 = (bf16[8,16,512]{2,1,0:T(8,128)(2,1)S(1)}, bf16[8,16,512]{2,1,0:T(8,128)(2,1)S(1)}, u32[]{:S(2)}, u32[]{:S(2)}) collective-permute-start(bf16[8,16,512]{2,1,0:T(8,128)(2,1)S(1)} %shard_map.43), channel_id=1, source_target_pairs={{0,1},{1,0},{2,3},{3,2},{4,5},{5,4},{6,7},{7,6},{8,9},{9,8},{10,11... | collective-permute-start | bytes 393224 | tf_op jit(solution)/shard_map/ppermute | solution.py:197

commit v2 on v1

--- a/solution.py
+++ b/solution.py
@@ -17,7 +17,7 @@
 EPS = 1e-06
 F32 = jnp.float32
 BF16 = jnp.bfloat16
-VMEM_LIMIT = 48 * 1024 * 1024
+VMEM_LIMIT = 16 * 1024 * 1024
 
 
 def smem():
@@ -45,9 +45,13 @@
     return (values * (quality / jnp.sqrt(energy + EPS))).astype(BF16)
 
 
-def sources_kernel(scalars, quality, spectra, mine, other):
+def sources_kernel(blocks, quality, spectra, mine, other):
+    group = lax.axis_index("chan")
+    per_group = spectra.shape[1] // SRC
     for place, out in enumerate((mine, other)):
-        held, base = scalars[1 + 2 * place], scalars[2 + 2 * place]
+        block = blocks[(group + place) % 2]
+        held = (block // per_group == group).astype(jnp.int32)
+        base = block % per_group * SRC
         aligned = pl.multiple_of(base // 16 * 16, 16)
         upper = base % 16 != 0
         flags = column(SRC, lambda row: (quality[base + row] * held).astype(F32))
@@ -94,7 +98,8 @@
         ).astype(BF16)
 
 
-def lagged_kernel(owners, mine, other, receivers, table, *rest):
+def lagged_kernel(distances, mine, other, receivers, table, *rest):
+    owners = [lax.axis_index("win") ^ distance for distance in distances]
     outs, (even, odd, total) = rest[:-3], rest[-3:]
     _, windows, rows, width = receivers.shape
     bins = width // 2
@@ -159,9 +164,9 @@
             out[row] = total[start : start + 2 * SRC, :].astype(out.dtype)
 
 
-def stack_kernel(scalars, own, *rest):
+def stack_kernel(own, *rest):
     received, out = rest[:-1], rest[-1]
-    step = scalars[0]
+    step = lax.axis_index("chan") % 2
     for row in range(own.shape[0]):
         total = own[row]
         for ref in received:
@@ -170,15 +175,15 @@
         out[1 - step, row] = total[SRC:].astype(BF16)
 
 
-def lagged_call(owners, mine, other, receivers, table, dtype):
-    count = owners.shape[0]
+def lagged_call(distances, mine, other, receivers, table, dtype):
+    count = len(distances)
     _, windows, rows, width = receivers.shape
     lines = count * rows * 2 * SRC
     shape = jax.ShapeDtypeStruct((rows, 2 * SRC, L), dtype)
     return pl.pallas_call(
-        lagged_kernel,
+        functools.partial(lagged_kernel, distances),
         out_shape=[shape] * count,
-        in_specs=[smem(), vmem(), vmem(), vmem(), vmem()],
+        in_specs=[vmem()] * 4,
         out_specs=[vmem()] * count,
         scratch_shapes=[
             pltpu.VMEM((lines, 2 * BINS_PER_CHUNK), BF16),
@@ -189,7 +194,7 @@
         cost_estimate=pl.CostEstimate(
             flops=2 * lines * width * L, bytes_accessed=2 * width * L, transcendentals=0
         ),
-    )(owners, mine, other, receivers, table)
+    )(mine, other, receivers, table)
 
 
 def exchange(value, axis, distance):
@@ -199,18 +204,10 @@
 
 def body(spectra, quality, source_block):
     windows, channels, width = spectra.shape
-    group, groups = lax.axis_index("chan"), lax.axis_size("chan")
-    place, places = lax.axis_index("win"), lax.axis_size("win")
+    groups, places = lax.axis_size("chan"), lax.axis_size("win")
     bins = width // 2
     rows = channels // places
     factor = 1.0 / math.sqrt(width * windows * places)
-
-    core = group % 2
-    blocks = jnp.stack([source_block[core], source_block[1 - core]]).astype(jnp.int32)
-    per_group = channels // SRC
-    held = (blocks // per_group == group).astype(jnp.int32)
-    base = blocks % per_group * SRC
-    scalars = jnp.stack([core, held[0], base[0], held[1], base[1]]).astype(jnp.int32)
 
     candidate = jax.ShapeDtypeStruct((windows, SRC, width), BF16)
     mine, other = pl.pallas_call(
@@ -219,8 +216,11 @@
         in_specs=[smem(), smem(), vmem()],
         out_specs=[vmem(), vmem()],
         compiler_params=params(),
-    )(scalars, quality, spectra)
-
+    )(source_block, quality, spectra)
+
+    both = mine + exchange(other, "chan", 1)
+    both, spectra = lax.optimization_barrier((both, spectra))
+    halves = [both[: windows // 2], both[windows // 2 :]]
     receivers = pl.pallas_call(
         receivers_kernel,
         out_shape=jax.ShapeDtypeStruct((places, windows, rows, width), F32),
@@ -237,10 +237,10 @@
         compiler_params=params(),
     )()
 
-    both = mine + exchange(other, "chan", 1)
-    halves = [both[: windows // 2], both[windows // 2 :]]
     distances = [1 << bit for bit in range(1, (groups - 1).bit_length())]
-    for one, two in zip(distances, reversed(distances), strict=True):
+    for index, (one, two) in enumerate(zip(distances, reversed(distances), strict=True)):
+        if index == 1:
+            halves, receivers, table = lax.optimization_barrier((halves, receivers, table))
         halves = [halves[0] + exchange(halves[0], "chan", one), halves[1] + exchange(halves[1], "chan", two)]
     mine = jnp.concatenate(halves)
     other = exchange(mine, "chan", 1)
@@ -248,19 +248,17 @@
     far_first = sorted(range(1, places), key=lambda d: (-(d.bit_length()), d))
     received = []
     for distance in far_first:
-        owners = jnp.reshape(place ^ distance, (1,)).astype(jnp.int32)
-        (partial,) = lagged_call(owners, mine, other, receivers, table, BF16)
+        (partial,) = lagged_call([distance], mine, other, receivers, table, BF16)
         received.append(exchange(partial, "win", distance))
-    owners = jnp.reshape(place, (1,)).astype(jnp.int32)
-    (own,) = lagged_call(owners, mine, other, receivers, table, F32)
+    (own,) = lagged_call([0], mine, other, receivers, table, F32)
 
     return pl.pallas_call(
         stack_kernel,
         out_shape=jax.ShapeDtypeStruct((STEPS, rows, SRC, L), BF16),
-        in_specs=[smem(), vmem()] + [vmem()] * len(received),
+        in_specs=[vmem()] * (1 + len(received)),
         out_specs=vmem(),
         compiler_params=params(),
-    )(scalars, own, *received)
+    )(own, *received)
 
 
 def solution(mesh):

time: 56.3 us -> 39 us (0.69)
  Pallas kernels: 22.9 us -> 13.7 us
  local copies, waits for them, and re-layouts: 8.49 us -> 2.55 us
  other arithmetic: 2.84 us -> 0.19 us
  waiting for transfers between devices: 9.92 us -> 10.7 us
    pallas_call x4, Pallas kernels: 17.7 us -> 8.98 us  [lagged_call(): pl.pallas_call(functools.partial(lagged_kernel, distances), out_shape=[sh...]
    another operation x1 -> x0, local copies, waits for them, and re-layouts: 2.58 us -> none  [body(): jnp.stack([core, held[0], base[0], held[1], base[1]]).astype(jnp.int32)]
    dynamic_slice x1 -> x0, local copies, waits for them, and re-layouts: 1.39 us -> none  [body(): source_block[core]]
    convert_element_type x1 -> x0, other arithmetic: 1.33 us -> none  [body(): held = (blocks // per_group == group).astype(jnp.int32)]
    mul x1 -> x0, other arithmetic: 1.33 us -> none  [body(): base = blocks % per_group * SRC]
    unnamed x10 -> x6, local copies, waits for them, and re-layouts: 3.83 us -> 2.53 us
    ppermute x9, waiting for transfers between devices: 9.92 us -> 10.7 us  [exchange(): return lax.ppermute(value, axis, [(i, i ^ distance) for i in range(size)])]
    slice x1 -> x0, local copies, waits for them, and re-layouts: 0.67 us -> none  [body(): base[1]]
  transfers between devices with their start and end apart: 9 -> 9, of which waited for: 6 -> 7; matrix products, arithmetic and copies ran while one was open for 0% -> 0% of each run, Pallas kernels for 29% -> 25%
where the time goes in v2:
time: 39 us; the launch traced here: 38.9 us
  Pallas kernels  13.7 us (35%)
  starting transfers between devices  11.6 us (30%)
  waiting for transfers between devices  10.7 us (27%)
  local copies, waits for them, and re-layouts  2.55 us (7%)
    ppermute x9, starting transfers between devices, exchange(): return lax.ppermute(value, axis, [(i, i ^ distance) for i in range(size)])  11.6 us
    ppermute x9, waiting for transfers between devices, exchange(): return lax.ppermute(value, axis, [(i, i ^ distance) for i in range(size)])  10.7 us
    pallas_call x4, Pallas kernels, lagged_call(): pl.pallas_call(functools.partial(lagged_kernel, distances), out_shape=[sh...  8.98 us
    unnamed x6, local copies, waits for them, and re-layouts  2.53 us
    pallas_call x1, Pallas kernels, body(): pl.pallas_call(functools.partial(table_kernel, factor), out_shape=jax.Sha...  2.08 us
    pallas_call x1, Pallas kernels, body(): pl.pallas_call(receivers_kernel, out_shape=jax.ShapeDtypeStruct((places,...  1.07 us
    pallas_call x1, Pallas kernels, body(): pl.pallas_call(sources_kernel, out_shape=[candidate, candidate], in_specs...  0.85 us
  transfers between devices with their start and end apart: 9, of which 7 were waited for; matrix products, arithmetic and copies ran while one was open for 0% of the time, Pallas kernels for 25%

profile of v2, /device:TPU:0, one launch (start us, length us, event | category | flops | bytes accessed | tf_op | source)
XLA Modules:
  0.0 38.9 jit_solution(13299780790539378095)
XLA Ops:
  0.0 1.2 %copy-done = bf16[4,32,4096]{2,1,0:T(8,128)(2,1)S(1)} copy-done((bf16[4,32,4096]{2,1,0:T(8,128)(2,1)S(1)}, bf16[4,32,4096]{2,1,0:T(8,128)(2,1)}, u32[]{:S(2)}) %copy-start) | copy-done | bytes 1048600
  1.2 0.7 %copy-done.1 = s32[32]{0:T(128)S(1)} copy-done((s32[32]{0:T(128)S(1)}, s32[32]{0:T(128)}, u32[]{:S(2)}) %copy-start.1) | copy-done | bytes 152
  1.9 0.7 %copy-done.2 = s32[2]{0:T(128)S(1)} copy-done((s32[2]{0:T(128)S(1)}, s32[2]{0:T(128)}, u32[]{:S(2)}) %copy-start.2) | copy-done | bytes 32
  2.5 0.9 %shard_map.37 = (bf16[4,8,4096]{2,1,0:T(8,128)(2,1)S(1)}, bf16[4,8,4096]{2,1,0:T(8,128)(2,1)S(1)}) custom-call(s32[2]{0:T(128)S(1)} %copy-done.2, s32[32]{0:T(128)S(1)} %copy-done.1, bf16[4,32,4096]{2,1,0:T(8,128)(2,1)S(1)} %copy-done), custom_call_target="tpu_custom_call" | custom-call | tf_op jit(solution)/shard_map/pallas_call | solution.py:213
  3.4 0.5 %collective-permute-start = (bf16[4,8,4096]{2,1,0:T(8,128)(2,1)S(1)}, bf16[4,8,4096]{2,1,0:T(8,128)(2,1)S(1)}, u32[]{:S(2)}, u32[]{:S(2)}) collective-permute-start(bf16[4,8,4096]{2,1,0:T(8,128)(2,1)S(1)} %get-tuple-element.14), channel_id=1, source_target_pairs={{0,4},{4,0},{8,12},{12,8},{16,20},{20,16},{24,28},{28,24},{1,5},{5... | collective-permute-start | bytes 786440 | tf_op jit(solution)/shard_map/ppermute | solution.py:202
  3.9 1.2 %collective-permute-done = bf16[4,8,4096]{2,1,0:T(8,128)(2,1)S(1)} collective-permute-done((bf16[4,8,4096]{2,1,0:T(8,128)(2,1)S(1)}, bf16[4,8,4096]{2,1,0:T(8,128)(2,1)S(1)}, u32[]{:S(2)}, u32[]{:S(2)}) %collective-permute-start) | collective-permute-done | bytes 262176 | tf_op jit(solution)/shard_map/ppermute | solution.py:202
  5.2 3.0 %collective-permute-start.2 = (bf16[2,8,4096]{2,1,0:T(8,128)(2,1)S(1)}, bf16[2,8,4096]{2,1,0:T(8,128)(2,1)S(1)}, u32[]{:S(2)}, u32[]{:S(2)}) collective-permute-start(bf16[2,8,4096]{2,1,0:T(8,128)(2,1)S(1)} %get-tuple-element.23), channel_id=1, source_target_pairs={{0,16},{4,20},{8,24},{12,28},{16,0},{20,4},{24,8},{28,12},{1,17},{... | collective-permute-start | bytes 393224 | tf_op jit(solution)/shard_map/ppermute | solution.py:202
  8.1 1.5 %collective-permute-start.1 = (bf16[2,8,4096]{2,1,0:T(8,128)(2,1)S(1)}, bf16[2,8,4096]{2,1,0:T(8,128)(2,1)S(1)}, u32[]{:S(2)}, u32[]{:S(2)}) collective-permute-start(bf16[2,8,4096]{2,1,0:T(8,128)(2,1)S(1)} %get-tuple-element.24), channel_id=1, source_target_pairs={{0,8},{4,12},{8,0},{12,4},{16,24},{20,28},{24,16},{28,20},{1,9},{5... | collective-permute-start | bytes 393224 | tf_op jit(solution)/shard_map/ppermute | solution.py:202
  9.6 2.1 %shard_map.39.table = bf16[4096,512]{1,0:T(8,128)(2,1)S(1)} custom-call(), custom_call_target="tpu_custom_call" | custom-call | tf_op jit(solution)/shard_map/pallas_call | solution.py:231
  11.7 1.1 %shard_map.38.receivers = f32[4,4,8,4096]{3,2,1,0:T(8,128)S(1)} custom-call(s32[32]{0:T(128)S(1)} %copy-done.1, bf16[4,32,4096]{2,1,0:T(8,128)(2,1)S(1)} %copy-done), custom_call_target="tpu_custom_call" | custom-call | tf_op jit(solution)/shard_map/pallas_call | solution.py:224
  12.8 0.6 %collective-permute-done.1 = bf16[2,8,4096]{2,1,0:T(8,128)(2,1)S(1)} collective-permute-done((bf16[2,8,4096]{2,1,0:T(8,128)(2,1)S(1)}, bf16[2,8,4096]{2,1,0:T(8,128)(2,1)S(1)}, u32[]{:S(2)}, u32[]{:S(2)}) %collective-permute-start.1) | collective-permute-done | bytes 131104 | tf_op jit(solution)/shard_map/ppermute | solution.py:202
  13.4 0.4 %collective-permute-start.3 = (bf16[2,8,4096]{2,1,0:T(8,128)(2,1)S(1)}, bf16[2,8,4096]{2,1,0:T(8,128)(2,1)S(1)}, u32[]{:S(2)}, u32[]{:S(2)}) collective-permute-start(bf16[2,8,4096]{2,1,0:T(8,128)(2,1)S(1)} %get-tuple-element.17), channel_id=1, source_target_pairs={{0,16},{4,20},{8,24},{12,28},{16,0},{20,4},{24,8},{28,12},{1,17},{... | collective-permute-start | bytes 393224 | tf_op jit(solution)/shard_map/ppermute | solution.py:202
  13.8 1.6 %collective-permute-start.4 = (bf16[2,8,4096]{2,1,0:T(8,128)(2,1)S(1)}, bf16[2,8,4096]{2,1,0:T(8,128)(2,1)S(1)}, u32[]{:S(2)}, u32[]{:S(2)}) collective-permute-start(bf16[2,8,4096]{2,1,0:T(8,128)(2,1)S(1)} %get-tuple-element.18), channel_id=1, source_target_pairs={{0,8},{4,12},{8,0},{12,4},{16,24},{20,28},{24,16},{28,20},{1,9},{5... | collective-permute-start | bytes 393224 | tf_op jit(solution)/shard_map/ppermute | solution.py:202
  15.5 3.0 %collective-permute-done.3 = bf16[2,8,4096]{2,1,0:T(8,128)(2,1)S(1)} collective-permute-done((bf16[2,8,4096]{2,1,0:T(8,128)(2,1)S(1)}, bf16[2,8,4096]{2,1,0:T(8,128)(2,1)S(1)}, u32[]{:S(2)}, u32[]{:S(2)}) %collective-permute-start.3) | collective-permute-done | bytes 131104 | tf_op jit(solution)/shard_map/ppermute | solution.py:202
  19.0 1.5 %collective-permute-done.5.other = bf16[4,8,4096]{2,1,0:T(8,128)(2,1)S(1)} collective-permute-done((bf16[4,8,4096]{2,1,0:T(8,128)(2,1)S(1)}, bf16[4,8,4096]{2,1,0:T(8,128)(2,1)S(1)}, u32[]{:S(2)}, u32[]{:S(2)}) %collective-permute-start.5) | collective-permute-done | bytes 262176 | tf_op jit(solution)/shard_map/ppermute | solution.py:202
  20.5 2.2 %shard_map.41 = bf16[8,16,512]{2,1,0:T(8,128)(2,1)S(1)} custom-call(bf16[4,8,4096]{2,1,0:T(8,128)(2,1)S(1)} %pad_maximum_fusion.mine, bf16[4,8,4096]{2,1,0:T(8,128)(2,1)S(1)} %collective-permute-done.5.other, f32[4,4,8,4096]{3,2,1,0:T(8,128)S(1)} %shard_map.38.receivers, bf16[4096,512]{1,0:T(8,128)(2,1)S(1)} %shard_map.39.table), custom_call_target="tpu_custom_call" | custom-call | flops 536870912 | bytes 4194304 | tf_op jit(solution)/shard_map/pallas_call | solution.py:183
  22.7 2.8 %collective-permute-start.6 = (bf16[8,16,512]{2,1,0:T(8,128)(2,1)S(1)}, bf16[8,16,512]{2,1,0:T(8,128)(2,1)S(1)}, u32[]{:S(2)}, u32[]{:S(2)}) collective-permute-start(bf16[8,16,512]{2,1,0:T(8,128)(2,1)S(1)} %shard_map.41), channel_id=1, source_target_pairs={{0,2},{1,3},{2,0},{3,1},{4,6},{5,7},{6,4},{7,5},{8,10},{9,11},{10,... | collective-permute-start | bytes 393224 | tf_op jit(solution)/shard_map/ppermute | solution.py:202
  25.5 2.2 %shard_map.42 = bf16[8,16,512]{2,1,0:T(8,128)(2,1)S(1)} custom-call(bf16[4,8,4096]{2,1,0:T(8,128)(2,1)S(1)} %pad_maximum_fusion.mine, bf16[4,8,4096]{2,1,0:T(8,128)(2,1)S(1)} %collective-permute-done.5.other, f32[4,4,8,4096]{3,2,1,0:T(8,128)S(1)} %shard_map.38.receivers, bf16[4096,512]{1,0:T(8,128)(2,1)S(1)} %shard_map.39.table), custom_call_target="tpu_custom_call" | custom-call | flops 536870912 | bytes 4194304 | tf_op jit(solution)/shard_map/pallas_call | solution.py:183
  27.8 1.4 %collective-permute-start.7 = (bf16[8,16,512]{2,1,0:T(8,128)(2,1)S(1)}, bf16[8,16,512]{2,1,0:T(8,128)(2,1)S(1)}, u32[]{:S(2)}, u32[]{:S(2)}) collective-permute-start(bf16[8,16,512]{2,1,0:T(8,128)(2,1)S(1)} %shard_map.42), channel_id=1, source_target_pairs={{0,3},{1,2},{2,1},{3,0},{4,7},{5,6},{6,5},{7,4},{8,11},{9,10},{10,... | collective-permute-start | bytes 393224 | tf_op jit(solution)/shard_map/ppermute | solution.py:202
  29.2 2.2 %shard_map.43 = bf16[8,16,512]{2,1,0:T(8,128)(2,1)S(1)} custom-call(bf16[4,8,4096]{2,1,0:T(8,128)(2,1)S(1)} %pad_maximum_fusion.mine, bf16[4,8,4096]{2,1,0:T(8,128)(2,1)S(1)} %collective-permute-done.5.other, f32[4,4,8,4096]{3,2,1,0:T(8,128)S(1)} %shard_map.38.receivers, bf16[4096,512]{1,0:T(8,128)(2,1)S(1)} %shard_map.39.table), custom_call_target="tpu_custom_call" | custom-call | flops 536870912 | bytes 4194304 | tf_op jit(solution)/shard_map/pallas_call | solution.py:183
  31.8 2.2 %shard_map.40.own = f32[8,16,512]{2,1,0:T(8,128)S(1)} custom-call(bf16[4,8,4096]{2,1,0:T(8,128)(2,1)S(1)} %pad_maximum_fusion.mine, bf16[4,8,4096]{2,1,0:T(8,128)(2,1)S(1)} %collective-permute-done.5.other, f32[4,4,8,4096]{3,2,1,0:T(8,128)S(1)} %shard_map.38.receivers, bf16[4096,512]{1,0:T(8,128)(2,1)S(1)} %shard_map.39.table), custom_call_target="tpu_custom_call" | custom-call | flops 536870912 | bytes 4194304 | tf_op jit(solution)/shard_map/pallas_call | solution.py:183
  34.0 1.6 %collective-permute-done.6.rest_0_ = bf16[8,16,512]{2,1,0:T(8,128)(2,1)S(1)} collective-permute-done((bf16[8,16,512]{2,1,0:T(8,128)(2,1)S(1)}, bf16[8,16,512]{2,1,0:T(8,128)(2,1)S(1)}, u32[]{:S(2)}, u32[]{:S(2)}) %collective-permute-start.6) | collective-permute-done | bytes 131104 | tf_op jit(solution)/shard_map/ppermute | solution.py:202
  35.7 2.5 %collective-permute-done.8.rest_2_ = bf16[8,16,512]{2,1,0:T(8,128)(2,1)S(1)} collective-permute-done((bf16[8,16,512]{2,1,0:T(8,128)(2,1)S(1)}, bf16[8,16,512]{2,1,0:T(8,128)(2,1)S(1)}, u32[]{:S(2)}, u32[]{:S(2)}) %collective-permute-start.8) | collective-permute-done | bytes 131104 | tf_op jit(solution)/shard_map/ppermute | solution.py:202
  38.1 0.7 %shard_map.44 = bf16[2,8,8,512]{3,2,1,0:T(8,128)(2,1)} custom-call(f32[8,16,512]{2,1,0:T(8,128)S(1)} %shard_map.40.own, bf16[8,16,512]{2,1,0:T(8,128)(2,1)S(1)} %collective-permute-done.6.rest_0_, bf16[8,16,512]{2,1,0:T(8,128)(2,1)S(1)} %collective-permute-done.7.rest_1_, bf16[8,16,512]{2,1,0:T(8,128)(2,1)S(1)} %collective-permute-done.8.rest_2_), custom_call_target="tpu_custom_call" | custom-call | tf_op jit(solution)/shard_map/pallas_call | solution.py:255
  (14 shorter events, 0.9 us)
Async XLA Ops:
  0.0 1.2 %copy-start = (bf16[4,32,4096]{2,1,0:T(8,128)(2,1)S(1)}, bf16[4,32,4096]{2,1,0:T(8,128)(2,1)}, u32[]{:S(2)}) copy-start(bf16[4,32,4096]{2,1,0:T(8,128)(2,1)} %spectra.2) | copy-start | bytes 3145732
  1.2 0.7 %copy-start.1 = (s32[32]{0:T(128)S(1)}, s32[32]{0:T(128)}, u32[]{:S(2)}) copy-start(s32[32]{0:T(128)} %quality.3) | copy-start | bytes 388
  1.9 0.7 %copy-start.2 = (s32[2]{0:T(128)S(1)}, s32[2]{0:T(128)}, u32[]{:S(2)}) copy-start(s32[2]{0:T(128)} %blocks.1) | copy-start | bytes 28
  3.4 1.7 %collective-permute-start = (bf16[4,8,4096]{2,1,0:T(8,128)(2,1)S(1)}, bf16[4,8,4096]{2,1,0:T(8,128)(2,1)S(1)}, u32[]{:S(2)}, u32[]{:S(2)}) collective-permute-start(bf16[4,8,4096]{2,1,0:T(8,128)(2,1)S(1)} %get-tuple-element.14), channel_id=1, source_target_pairs={{0,4},{4,0},{8,12},{12,8},{16,20},{20,16},{24,28},{28,24},{1,5},{5... | collective-permute-start | bytes 786440 | tf_op jit(solution)/shard_map/ppermute | solution.py:202
  5.2 7.6 %collective-permute-start.2 = (bf16[2,8,4096]{2,1,0:T(8,128)(2,1)S(1)}, bf16[2,8,4096]{2,1,0:T(8,128)(2,1)S(1)}, u32[]{:S(2)}, u32[]{:S(2)}) collective-permute-start(bf16[2,8,4096]{2,1,0:T(8,128)(2,1)S(1)} %get-tuple-element.23), channel_id=1, source_target_pairs={{0,16},{4,20},{8,24},{12,28},{16,0},{20,4},{24,8},{28,12},{1,17},{... | collective-permute-start | bytes 393224 | tf_op jit(solution)/shard_map/ppermute | solution.py:202
  8.1 5.3 %collective-permute-start.1 = (bf16[2,8,4096]{2,1,0:T(8,128)(2,1)S(1)}, bf16[2,8,4096]{2,1,0:T(8,128)(2,1)S(1)}, u32[]{:S(2)}, u32[]{:S(2)}) collective-permute-start(bf16[2,8,4096]{2,1,0:T(8,128)(2,1)S(1)} %get-tuple-element.24), channel_id=1, source_target_pairs={{0,8},{4,12},{8,0},{12,4},{16,24},{20,28},{24,16},{28,20},{1,9},{5... | collective-permute-start | bytes 393224 | tf_op jit(solution)/shard_map/ppermute | solution.py:202
  13.4 5.0 %collective-permute-start.3 = (bf16[2,8,4096]{2,1,0:T(8,128)(2,1)S(1)}, bf16[2,8,4096]{2,1,0:T(8,128)(2,1)S(1)}, u32[]{:S(2)}, u32[]{:S(2)}) collective-permute-start(bf16[2,8,4096]{2,1,0:T(8,128)(2,1)S(1)} %get-tuple-element.17), channel_id=1, source_target_pairs={{0,16},{4,20},{8,24},{12,28},{16,0},{20,4},{24,8},{28,12},{1,17},{... | collective-permute-start | bytes 393224 | tf_op jit(solution)/shard_map/ppermute | solution.py:202
  13.8 5.0 %collective-permute-start.4 = (bf16[2,8,4096]{2,1,0:T(8,128)(2,1)S(1)}, bf16[2,8,4096]{2,1,0:T(8,128)(2,1)S(1)}, u32[]{:S(2)}, u32[]{:S(2)}) collective-permute-start(bf16[2,8,4096]{2,1,0:T(8,128)(2,1)S(1)} %get-tuple-element.18), channel_id=1, source_target_pairs={{0,8},{4,12},{8,0},{12,4},{16,24},{20,28},{24,16},{28,20},{1,9},{5... | collective-permute-start | bytes 393224 | tf_op jit(solution)/shard_map/ppermute | solution.py:202
  18.9 1.6 %collective-permute-start.5 = (bf16[4,8,4096]{2,1,0:T(8,128)(2,1)S(1)}, bf16[4,8,4096]{2,1,0:T(8,128)(2,1)S(1)}, u32[]{:S(2)}, u32[]{:S(2)}) collective-permute-start(bf16[4,8,4096]{2,1,0:T(8,128)(2,1)S(1)} %pad_maximum_fusion.mine), channel_id=1, source_target_pairs={{0,4},{4,0},{8,12},{12,8},{16,20},{20,16},{24,28},{28,24},{1,5},{5... | collective-permute-start | bytes 786440 | tf_op jit(solution)/shard_map/ppermute | solution.py:202
  22.7 12.9 %collective-permute-start.6 = (bf16[8,16,512]{2,1,0:T(8,128)(2,1)S(1)}, bf16[8,16,512]{2,1,0:T(8,128)(2,1)S(1)}, u32[]{:S(2)}, u32[]{:S(2)}) collective-permute-start(bf16[8,16,512]{2,1,0:T(8,128)(2,1)S(1)} %shard_map.41), channel_id=1, source_target_pairs={{0,2},{1,3},{2,0},{3,1},{4,6},{5,7},{6,4},{7,5},{8,10},{9,11},{10,... | collective-permute-start | bytes 393224 | tf_op jit(solution)/shard_map/ppermute | solution.py:202
  27.8 7.9 %collective-permute-start.7 = (bf16[8,16,512]{2,1,0:T(8,128)(2,1)S(1)}, bf16[8,16,512]{2,1,0:T(8,128)(2,1)S(1)}, u32[]{:S(2)}, u32[]{:S(2)}) collective-permute-start(bf16[8,16,512]{2,1,0:T(8,128)(2,1)S(1)} %shard_map.42), channel_id=1, source_target_pairs={{0,3},{1,2},{2,1},{3,0},{4,7},{5,6},{6,5},{7,4},{8,11},{9,10},{10,... | collective-permute-start | bytes 393224 | tf_op jit(solution)/shard_map/ppermute | solution.py:202
  31.5 6.7 %collective-permute-start.8 = (bf16[8,16,512]{2,1,0:T(8,128)(2,1)S(1)}, bf16[8,16,512]{2,1,0:T(8,128)(2,1)S(1)}, u32[]{:S(2)}, u32[]{:S(2)}) collective-permute-start(bf16[8,16,512]{2,1,0:T(8,128)(2,1)S(1)} %shard_map.43), channel_id=1, source_target_pairs={{0,1},{1,0},{2,3},{3,2},{4,5},{5,4},{6,7},{7,6},{8,9},{9,8},{10,11... | collective-permute-start | bytes 393224 | tf_op jit(solution)/shard_map/ppermute | solution.py:202

commit v3 on v2

v3 whole, which is shorter than its diff:
```python
import functools
import math

import jax
import jax.numpy as jnp
from jax import lax
from jax.experimental import pallas as pl
from jax.experimental.pallas import tpu as pltpu
from jax.sharding import PartitionSpec as P

L = 512
SRC = 8
STEPS = 2
LANES = 128
TILES_PER_DOT = 4
TABLE_ROWS = 64
EPS = 1e-06
F32 = jnp.float32
BF16 = jnp.bfloat16
VMEM_LIMIT = 16 * 1024 * 1024


def smem():
    return pl.BlockSpec(memory_space=pltpu.SMEM)


def vmem():
    return pl.BlockSpec(memory_space=pltpu.VMEM)


def params():
    return pltpu.CompilerParams(vmem_limit_bytes=VMEM_LIMIT)


def column(count, read):
    rows = lax.broadcasted_iota(jnp.int32, (count, 1), 0)
    result = jnp.zeros((count, 1), F32)
    for row in range(count):
        result = jnp.where(rows == row, read(row), result)
    return result


def whitened_rows(values, quality):
    energy = jnp.sum(values * values, axis=-1, keepdims=True) / (values.shape[-1] // 2)
    return (values * (quality / jnp.sqrt(energy + EPS))).astype(BF16).astype(F32)


def sources_kernel(blocks_in, quality_in, spectra_in, *rest):
    outs, (blocks, quality, spectra, sems) = rest[:-4], rest[-4:]
    windows, channels, width = spectra.shape
    bins, part = width // 2, width // 4
    copies = [
        pltpu.make_async_copy(blocks_in, blocks, sems.at[windows]),
        pltpu.make_async_copy(quality_in, quality, sems.at[windows + 1]),
    ] + [
        pltpu.make_async_copy(spectra_in.at[window], spectra.at[window], sems.at[window])
        for window in range(windows)
    ]
    for copy in copies:
        copy.start()
    copies[0].wait()
    copies[1].wait()
    group = lax.axis_index("chan")
    even = group % 2 == 0
    per_group = channels // SRC
    chosen = []
    for step in range(STEPS):
        block = blocks[step]
        held = (block // per_group == group).astype(jnp.int32)
        base = block % per_group * SRC
        flags = column(SRC, lambda row: (quality[base + row] * held).astype(F32))
        chosen.append((pl.multiple_of(base // 16 * 16, 16), base % 16 != 0, flags))
    for window in range(windows):
        copies[2 + window].wait()
        for step, (aligned, upper, flags) in enumerate(chosen):
            rows = spectra[window, pl.ds(aligned, 16), :].astype(F32)
            values = whitened_rows(jnp.where(upper, rows[SRC:], rows[:SRC]), flags)
            low = jnp.concatenate([values[:, :part], values[:, bins : bins + part]], axis=1)
            high = jnp.concatenate([values[:, part:bins], values[:, bins + part :]], axis=1)
            outs[step][window] = jnp.where(even, low, high).astype(BF16)
            outs[STEPS + step][window] = jnp.where(even, high, low).astype(BF16)


def receivers_kernel(quality, spectra, out):
    owners, windows, rows, _ = out.shape
    flags = column(owners * rows, lambda row: quality[row].astype(F32))
    for window in range(windows):
        values = whitened_rows(spectra[window].astype(F32), flags)
        for owner in range(owners):
            out[owner, window] = values[owner * rows : (owner + 1) * rows]


def table_kernel(factor, out, turn_cos, turn_sin, base_cos, base_sin):
    bins, lags = out.shape[0] // 2, out.shape[1]

    def angles(count, stride):
        rows = lax.broadcasted_iota(jnp.int32, (count, lags), 0) * stride
        shifts = lax.broadcasted_iota(jnp.int32, (count, lags), 1) - lags // 2
        residue = (rows * shifts) & (2 * bins - 1)
        residue = jnp.where(residue >= bins, residue - 2 * bins, residue)
        return residue.astype(F32) * (2.0 * math.pi / (2 * bins))

    turns = angles(bins // TABLE_ROWS, TABLE_ROWS)
    turn_cos[...] = jnp.cos(turns) * factor
    turn_sin[...] = jnp.sin(turns) * factor
    base = angles(TABLE_ROWS, 1)
    base_cos[...] = jnp.cos(base)
    base_sin[...] = jnp.sin(base)

    @pl.loop(0, bins // TABLE_ROWS)
    def _(turn):
        far_cos, far_sin = turn_cos[pl.ds(turn, 1), :], turn_sin[pl.ds(turn, 1), :]
        near_cos, near_sin = base_cos[...], base_sin[...]
        start = pl.multiple_of(turn * TABLE_ROWS, TABLE_ROWS)
        out[pl.ds(start, TABLE_ROWS), :] = (near_cos * far_cos - near_sin * far_sin).astype(BF16)
        out[pl.ds(bins + start, TABLE_ROWS), :] = (
            -(near_sin * far_cos + near_cos * far_sin)
        ).astype(BF16)


def lagged_kernel(distances, plan, carried, zeros, *refs):
    steps = sorted({step for _, present in plan for step in present})
    count = sum(len(present) for _, present in plan)
    sources, (receivers, table), refs = list(refs[:count]), refs[count : count + 2], refs[count + 2 :]
    carry = refs[: len(carried)]
    if zeros:
        refs, out = refs[:-1], refs[-1]
        out[...] = jnp.zeros_like(out)
    outs = refs[len(refs) - len(steps) :]
    core = lax.axis_index("chan") % 2
    _, windows, rows, width = receivers.shape
    bins, part = width // 2, width // 4
    lines = rows * SRC
    depth = TILES_PER_DOT * LANES

    def cross_tile(pair, start, at):
        real, imag = pl.ds(at, LANES), pl.ds(part + at, LANES)
        src = [
            [(ref[w, :, real].astype(F32), ref[w, :, imag].astype(F32)) for w in range(windows)]
            for ref in pair
        ]
        real = pl.ds(pl.multiple_of(start + at, LANES), LANES)
        imag = pl.ds(pl.multiple_of(bins + start + at, LANES), LANES)
        found = [[[], []] for _ in pair]
        for distance in distances:
            owner = lax.axis_index("win") ^ distance
            for row in range(rows):
                sums = [[None, None] for _ in pair]
                for w in range(windows):
                    rec_real = receivers[owner, w, pl.ds(row, 1), real]
                    rec_imag = receivers[owner, w, pl.ds(row, 1), imag]
                    for s in range(len(pair)):
                        src_real, src_imag = src[s][w]
                        re = src_real * rec_real + src_imag * rec_imag
                        im = src_real * rec_imag - src_imag * rec_real
                        sums[s][0] = re if w == 0 else sums[s][0] + re
                        sums[s][1] = im if w == 0 else sums[s][1] + im
                for s in range(len(pair)):
                    for p in range(2):
                        found[s][p].append(sums[s][p])
        return [
            jnp.concatenate(
                [
                    jnp.concatenate(one[p][row : row + 2], axis=0).astype(BF16)
                    for one in found
                    for row in range(0, len(one[p]), 2)
                ],
                axis=0,
            )
            for p in range(2)
        ]

    totals = {}
    for ref, step in zip(carry, carried, strict=True):
        held = [ref[distance * rows // 2 + pair] for distance in distances for pair in range(rows // 2)]
        totals[step] = jnp.concatenate(held, axis=0)
    for other, present in plan:
        pair, sources = sources[: len(present)], sources[len(present) :]
        start = (1 - core if other else core) * part
        for chunk in range(part // depth):
            at = chunk * depth
            tiles = [cross_tile(pair, start, at + tile * LANES) for tile in range(TILES_PER_DOT)]
            for p in range(2):
                cross = jnp.concatenate([tile[p] for tile in tiles], axis=1)
                where = pl.ds(pl.multiple_of(p * bins + start + at, depth), depth)
                product = jnp.dot(cross, table[where, :], preferred_element_type=F32)
                for place, step in enumerate(present):
                    height = lines * len(distances)
                    piece = product[place * height : (place + 1) * height]
                    totals[step] = totals[step] + piece if step in totals else piece
    for out, step in zip(outs, steps, strict=True):
        for pair in range(out.shape[0]):
            out[pair] = totals[step][pair * 2 * SRC : (pair + 1) * 2 * SRC].astype(out.dtype)


def stack_kernel(firsts, *refs):
    refs, out = refs[:-1], refs[-1]
    for step in range(STEPS):
        for pair in range(out.shape[1] // 2):
            terms = zip(refs[step::STEPS], firsts, strict=True)
            total = sum(ref[first + pair].astype(F32) for ref, first in terms)
            out[step, 2 * pair] = total[:SRC].astype(BF16)
            out[step, 2 * pair + 1] = total[SRC:].astype(BF16)


def lagged_call(distances, plan, sources, receivers, table, dtype, carry=None, after=(), zeros=None):
    _, windows, rows, width = receivers.shape
    carry = carry or {}
    carried = sorted(carry)
    count = len({step for _, present in plan for step in present})
    operands = [*sources, receivers, table, *(carry[step] for step in carried)]
    shapes = [jax.ShapeDtypeStruct((len(distances) * rows // 2, 2 * SRC, L), dtype)] * count
    if zeros is not None:
        shapes.append(jax.ShapeDtypeStruct(zeros, BF16))
    return pl.pallas_call(
        functools.partial(lagged_kernel, distances, plan, carried, zeros is not None),
        out_shape=shapes,
        in_specs=[vmem()] * len(operands) + [pl.BlockSpec(memory_space=pl.ANY)] * len(after),
        out_specs=[vmem()] * len(shapes),
        compiler_params=params(),
        cost_estimate=pl.CostEstimate(
            flops=len(distances) * len(sources) * rows * SRC * width * L,
            bytes_accessed=2 * width * L,
            transcendentals=0,
        ),
    )(*operands, *after)


def exchange(value, axis, *distances):
    size = lax.axis_size(axis)
    return lax.ppermute(value, axis, [(i, i ^ distances[i % len(distances)]) for i in range(size)])


def body(spectra, quality, source_block):
    windows, channels, width = spectra.shape
    groups, places = lax.axis_size("chan"), lax.axis_size("win")
    bins = width // 2
    rows = channels // places
    factor = 1.0 / math.sqrt(width * windows * places)

    hbm = pl.BlockSpec(memory_space=pltpu.HBM)
    inputs = [pltpu.with_memory_space_constraint(x, pltpu.HBM) for x in (source_block, quality, spectra)]
    candidates = pl.pallas_call(
        sources_kernel,
        out_shape=[jax.ShapeDtypeStruct((windows, SRC, width // 2), BF16)] * (2 * STEPS),
        in_specs=[hbm] * 3,
        out_specs=[vmem()] * (2 * STEPS),
        scratch_shapes=[
            pltpu.SMEM(source_block.shape, jnp.int32),
            pltpu.SMEM(quality.shape, jnp.int32),
            pltpu.VMEM(spectra.shape, BF16),
            pltpu.SemaphoreType.DMA((windows + 2,)),
        ],
        compiler_params=params(),
    )(*inputs)

    table = pl.pallas_call(
        functools.partial(table_kernel, factor),
        out_shape=jax.ShapeDtypeStruct((width, L), BF16),
        out_specs=vmem(),
        scratch_shapes=[pltpu.VMEM((bins // TABLE_ROWS, L), F32)] * 2
        + [pltpu.VMEM((TABLE_ROWS, L), F32)] * 2,
        compiler_params=params(),
    )()
    mine = [candidates[step] + exchange(candidates[STEPS + step], "chan", 1) for step in range(STEPS)]
    distances = [1 << bit for bit in range(1, (groups - 1).bit_length())]
    hops = list(zip(distances, reversed(distances), strict=True))
    for index, (even, odd) in enumerate(hops):
        if index == 1:
            mine[0], table, spectra = lax.optimization_barrier((mine[0], table, spectra))
        arrived = [exchange(part, "chan", even, odd) for part in mine]
        if index < len(hops) - 1:
            mine = [part + new for part, new in zip(mine, arrived, strict=True)]
    receivers = pl.pallas_call(
        receivers_kernel,
        out_shape=jax.ShapeDtypeStruct((places, windows, rows, width), F32),
        in_specs=[smem(), vmem()],
        out_specs=vmem(),
        compiler_params=params(),
    )(quality, spectra)

    odd = [distance for distance in reversed(range(places)) if distance & 1]
    mine[0] = mine[0] + arrived[0]
    mine[0], receivers = lax.optimization_barrier((mine[0], receivers))
    other = [exchange(mine[0], "chan", 1)]
    halves = [(False, (0,)), (True, (0,))]
    (first,) = lagged_call(odd, halves, [mine[0], other[0]], receivers, table, BF16)
    mine[1] = mine[1] + arrived[1]
    other.append(exchange(mine[1], "chan", 1))
    halves = [(False, (1,)), (True, (1,))]
    (second,) = lagged_call(odd, halves, [mine[1], other[1]], receivers, table, BF16, after=[first])

    def lagged(distances, after=()):
        plan = [(True, (0, 1)), (False, (0, 1))]
        return lagged_call(distances, plan, [*other, *mine], receivers, table, F32, after=after)

    pairs = rows // 2
    received = [([distance ^ 1 for distance in odd], [exchange(part, "win", 1) for part in (first, second)])]
    last = ()
    for bit in range(1, (places - 1).bit_length()):
        group = [distance for distance in reversed(range(0, places, 1 << bit)) if distance >> bit & 1]
        sums = list(lagged(group, last))
        for order, parts in received:
            here = [order.index(distance) * pairs for distance in group]
            for step in range(STEPS):
                new = jnp.concatenate([parts[step][at : at + pairs] for at in here])
                sums[step] = sums[step] + new.astype(F32)
        sums = [part.astype(BF16) for part in sums]
        last = sums[1:]
        received.append(([distance ^ 1 << bit for distance in group], [exchange(part, "win", 1 << bit) for part in sums]))
    own = lagged([0], last)
    terms = [*own, *(part for _, parts in received for part in parts)]

    return pl.pallas_call(
        functools.partial(stack_kernel, [0, *(order.index(0) * pairs for order, _ in received)]),
        out_shape=jax.ShapeDtypeStruct((STEPS, rows, SRC, L), BF16),
        in_specs=[vmem()] * len(terms),
        out_specs=vmem(),
        compiler_params=params(),
    )(*terms)


def solution(mesh):
    return jax.shard_map(
        body,
        mesh=mesh,
        in_specs=(P("win", "chan", None), P("chan"), P()),
        out_specs=P(None, ("chan", "win"), None, None),
        check_vma=False,
    )
```

time: 39 us -> 33.4 us (0.86)
  waiting for transfers between devices: 10.7 us -> 6.21 us
  starting transfers between devices: 11.6 us -> 15.4 us
  local copies, waits for them, and re-layouts: 2.55 us -> 0.01 us
  Pallas kernels: 13.7 us -> 11.3 us
    ppermute x9 -> x12, waiting for transfers between devices: 10.7 us -> 6.21 us  [exchange(): lax.ppermute(value, axis, [(i, i ^ distances[i % len(distances)]) for i i...]
    ppermute x9 -> x12, starting transfers between devices: 11.6 us -> 15.4 us  [exchange(): lax.ppermute(value, axis, [(i, i ^ distances[i % len(distances)]) for i i...]
    unnamed x6 -> x4, local copies, waits for them, and re-layouts: 2.53 us -> 0.01 us
    pallas_call x6, Pallas kernels: 10.5 us -> 8.13 us  [the longest x4 5.67 us: lagged_call(): pl.pallas_call(functools.partial(lagged_kernel, distances, plan, carried,...]
  transfers between devices with their start and end apart: 9 -> 12, of which waited for: 7 -> 7; matrix products, arithmetic and copies ran while one was open for 0% -> 1% of each run, Pallas kernels for 25% -> 27%
where the time goes in v3:
time: 33.4 us; the launch traced here: 33.2 us
  starting transfers between devices  15.4 us (46%)
  Pallas kernels  11.3 us (34%)
  waiting for transfers between devices  6.21 us (19%)
    ppermute x12, starting transfers between devices, exchange(): lax.ppermute(value, axis, [(i, i ^ distances[i % len(distances)]) for i i...  15.4 us
    ppermute x12, waiting for transfers between devices, exchange(): lax.ppermute(value, axis, [(i, i ^ distances[i % len(distances)]) for i i...  6.21 us
    pallas_call x4, Pallas kernels, lagged_call(): pl.pallas_call(functools.partial(lagged_kernel, distances, plan, carried,...  5.67 us
    pallas_call x1, Pallas kernels, body(): pl.pallas_call(functools.partial(table_kernel, factor), out_shape=jax.Sha...  2.08 us
    pallas_call x1, Pallas kernels, body(): pl.pallas_call(sources_kernel, out_shape=[jax.ShapeDtypeStruct((windows,...  1.77 us
    pallas_call x1, Pallas kernels, body(): pl.pallas_call(receivers_kernel, out_shape=jax.ShapeDtypeStruct((places,...  1.07 us
    pallas_call x1, Pallas kernels, body(): pl.pallas_call(functools.partial(stack_kernel, [0, *(order.index(0) * pai...  0.7 us
  transfers between devices with their start and end apart: 12, of which 7 were waited for; matrix products, arithmetic and copies ran while one was open for 1% of the time, Pallas kernels for 27%

profile of v3, /device:TPU:0, one launch (start us, length us, event | category | flops | bytes accessed | tf_op | source)
XLA Modules:
  0.0 33.2 jit_solution(891189736313448712)
XLA Ops:
  0.0 1.8 %shard_map.37 = (bf16[4,8,2048]{2,1,0:T(8,128)(2,1)S(1)}, bf16[4,8,2048]{2,1,0:T(8,128)(2,1)S(1)}, bf16[4,8,2048]{2,1,0:T(8,128)(2,1)S(1)}, bf16[4,8,2048]{2,1,0:T(8,128)(2,1)S(1)}) custom-call(s32[2]{0:T(128)} %blocks_in.1, s32[32]{0:T(128)} %quality.1, bf16[4,32,4096]{2,1,0:T(8,128)(2,1)} %spectra), custom_call_target="tpu_custom_call" | custom-call | tf_op jit(solution)/shard_map/pallas_call | solution.py:243
  1.8 0.5 %collective-permute-start = (bf16[4,8,2048]{2,1,0:T(8,128)(2,1)S(1)}, bf16[4,8,2048]{2,1,0:T(8,128)(2,1)S(1)}, u32[]{:S(2)}, u32[]{:S(2)}) collective-permute-start(bf16[4,8,2048]{2,1,0:T(8,128)(2,1)S(1)} %get-tuple-element.19), channel_id=1, source_target_pairs={{0,4},{4,0},{8,12},{12,8},{16,20},{20,16},{24,28},{28,24},{1,5},{5... | collective-permute-start | bytes 393224 | tf_op jit(solution)/shard_map/ppermute | solution.py:231
  2.4 0.9 %collective-permute-done = bf16[4,8,2048]{2,1,0:T(8,128)(2,1)S(1)} collective-permute-done((bf16[4,8,2048]{2,1,0:T(8,128)(2,1)S(1)}, bf16[4,8,2048]{2,1,0:T(8,128)(2,1)S(1)}, u32[]{:S(2)}, u32[]{:S(2)}) %collective-permute-start) | collective-permute-done | bytes 131104 | tf_op jit(solution)/shard_map/ppermute | solution.py:231
  3.3 2.9 %collective-permute-start.1 = (bf16[4,8,2048]{2,1,0:T(8,128)(2,1)S(1)}, bf16[4,8,2048]{2,1,0:T(8,128)(2,1)S(1)}, u32[]{:S(2)}, u32[]{:S(2)}) collective-permute-start(bf16[4,8,2048]{2,1,0:T(8,128)(2,1)S(1)} %add.24), channel_id=1, source_target_pairs={{0,8},{4,20},{8,0},{12,28},{16,24},{20,4},{24,16},{28,12},{1,9},{5... | collective-permute-start | bytes 393224 | tf_op jit(solution)/shard_map/ppermute | solution.py:231
  6.3 0.1 collective-permute-start.5
  6.4 2.1 %shard_map.38.refs_5_.refs_3_ = bf16[4096,512]{1,0:T(8,128)(2,1)S(1)} custom-call(), custom_call_target="tpu_custom_call" | custom-call | tf_op jit(solution)/shard_map/pallas_call | solution.py:257
  8.5 0.7 %collective-permute-done.1 = bf16[4,8,2048]{2,1,0:T(8,128)(2,1)S(1)} collective-permute-done((bf16[4,8,2048]{2,1,0:T(8,128)(2,1)S(1)}, bf16[4,8,2048]{2,1,0:T(8,128)(2,1)S(1)}, u32[]{:S(2)}, u32[]{:S(2)}) %collective-permute-start.1) | collective-permute-done | bytes 131104 | tf_op jit(solution)/shard_map/ppermute | solution.py:231
  9.2 2.1 %collective-permute-start.2 = (bf16[4,8,2048]{2,1,0:T(8,128)(2,1)S(1)}, bf16[4,8,2048]{2,1,0:T(8,128)(2,1)S(1)}, u32[]{:S(2)}, u32[]{:S(2)}) collective-permute-start(bf16[4,8,2048]{2,1,0:T(8,128)(2,1)S(1)} %add.25), channel_id=1, source_target_pairs={{0,16},{4,12},{8,24},{12,4},{16,0},{20,28},{24,8},{28,20},{1,17},{... | collective-permute-start | bytes 393224 | tf_op jit(solution)/shard_map/ppermute | solution.py:231
  11.4 1.6 %collective-permute-start.6 = (bf16[4,8,2048]{2,1,0:T(8,128)(2,1)S(1)}, bf16[4,8,2048]{2,1,0:T(8,128)(2,1)S(1)}, u32[]{:S(2)}, u32[]{:S(2)}) collective-permute-start(bf16[4,8,2048]{2,1,0:T(8,128)(2,1)S(1)} %add.28), channel_id=1, source_target_pairs={{0,16},{4,12},{8,24},{12,4},{16,0},{20,28},{24,8},{28,20},{1,17},{... | collective-permute-start | bytes 393224 | tf_op jit(solution)/shard_map/ppermute | solution.py:231
  12.9 1.1 %shard_map.39.refs_4_.refs_2_ = f32[4,4,8,4096]{3,2,1,0:T(8,128)S(1)} custom-call(s32[32]{0:T(128)S(1)} %copy-done.1, bf16[4,32,4096]{2,1,0:T(8,128)(2,1)S(1)} %copy-done), custom_call_target="tpu_custom_call" | custom-call | tf_op jit(solution)/shard_map/pallas_call | solution.py:274
  14.0 0.3 collective-permute-done.2
  14.4 2.0 %collective-permute-done.6 = bf16[4,8,2048]{2,1,0:T(8,128)(2,1)S(1)} collective-permute-done((bf16[4,8,2048]{2,1,0:T(8,128)(2,1)S(1)}, bf16[4,8,2048]{2,1,0:T(8,128)(2,1)S(1)}, u32[]{:S(2)}, u32[]{:S(2)}) %collective-permute-start.6) | collective-permute-done | bytes 131104 | tf_op jit(solution)/shard_map/ppermute | solution.py:231
  16.5 1.4 %shard_map.41.refs_4_ = bf16[8,16,512]{2,1,0:T(8,128)(2,1)S(1)} custom-call(bf16[4,8,2048]{2,1,0:T(8,128)(2,1)S(1)} %add.26.refs_2_.refs_0_, bf16[4,8,2048]{2,1,0:T(8,128)(2,1)S(1)} %collective-permute-done.3.refs_0_.refs_1_, f32[4,4,8,4096]{3,2,1,0:T(8,128)S(1)} %shard_map.39.refs_4_.refs_2_, bf16[4096,512]{1,0:T(8,128)(2,1)S(1)} %shard_map.38.refs_5_.refs_3_), custom_call_target="tpu_custom_call" | custom-call | flops 536870912 | bytes 4194304 | tf_op jit(solution)/shard_map/pallas_call | solution.py:215
  17.9 1.6 %collective-permute-start.9 = (bf16[8,16,512]{2,1,0:T(8,128)(2,1)S(1)}, bf16[8,16,512]{2,1,0:T(8,128)(2,1)S(1)}, u32[]{:S(2)}, u32[]{:S(2)}) collective-permute-start(bf16[8,16,512]{2,1,0:T(8,128)(2,1)S(1)} %shard_map.41.refs_4_), channel_id=1, source_target_pairs={{0,1},{1,0},{2,3},{3,2},{4,5},{5,4},{6,7},{7,6},{8,9},{9,8},{10,11... | collective-permute-start | bytes 393224 | tf_op jit(solution)/shard_map/ppermute | solution.py:231
  19.6 1.4 %shard_map.42 = bf16[8,16,512]{2,1,0:T(8,128)(2,1)S(1)} custom-call(bf16[4,8,2048]{2,1,0:T(8,128)(2,1)S(1)} %add.29.refs_3_.refs_0_, bf16[4,8,2048]{2,1,0:T(8,128)(2,1)S(1)} %collective-permute-done.7.refs_1_, f32[4,4,8,4096]{3,2,1,0:T(8,128)S(1)} %shard_map.39.refs_4_.refs_2_, bf16[4096,512]{1,0:T(8,128)(2,1)S(1)} %shard_map.38.refs_5_.refs_3_, ...), custom_call_target="tpu_custom_call" | custom-call | flops 536870912 | bytes 4194304 | tf_op jit(solution)/shard_map/pallas_call | solution.py:215
  20.9 0.5 %collective-permute-start.8 = (bf16[8,16,512]{2,1,0:T(8,128)(2,1)S(1)}, bf16[8,16,512]{2,1,0:T(8,128)(2,1)S(1)}, u32[]{:S(2)}, u32[]{:S(2)}) collective-permute-start(bf16[8,16,512]{2,1,0:T(8,128)(2,1)S(1)} %shard_map.42), channel_id=1, source_target_pairs={{0,1},{1,0},{2,3},{3,2},{4,5},{5,4},{6,7},{7,6},{8,9},{9,8},{10,11... | collective-permute-start | bytes 393224 | tf_op jit(solution)/shard_map/ppermute | solution.py:231
  21.5 1.5 %shard_map.40 = (f32[4,16,512]{2,1,0:T(8,128)S(1)}, f32[4,16,512]{2,1,0:T(8,128)S(1)}) custom-call(bf16[4,8,2048]{2,1,0:T(8,128)(2,1)S(1)} %collective-permute-done.3.refs_0_.refs_1_, bf16[4,8,2048]{2,1,0:T(8,128)(2,1)S(1)} %collective-permute-done.7.refs_1_, bf16[4,8,2048]{2,1,0:T(8,128)(2,1)S(1)} %add.26.refs_2_.refs_0_, ...), custom_call_target="tpu_custom_call" | custom-call | flops 536870912 | bytes 4194304 | tf_op jit(solution)/shard_map/pallas_call | solution.py:215
  22.9 1.0 %collective-permute-done.9.refs_2_ = bf16[8,16,512]{2,1,0:T(8,128)(2,1)S(1)} collective-permute-done((bf16[8,16,512]{2,1,0:T(8,128)(2,1)S(1)}, bf16[8,16,512]{2,1,0:T(8,128)(2,1)S(1)}, u32[]{:S(2)}, u32[]{:S(2)}) %collective-permute-start.9) | collective-permute-done | bytes 131104 | tf_op jit(solution)/shard_map/ppermute | solution.py:231
  23.9 2.7 %collective-permute-start.10 = (bf16[4,16,512]{2,1,0:T(8,128)(2,1)S(1)}, bf16[4,16,512]{2,1,0:T(8,128)(2,1)S(1)}, u32[]{:S(2)}, u32[]{:S(2)}) collective-permute-start(bf16[4,16,512]{2,1,0:T(8,128)(2,1)S(1)} %add_convert_fusion), channel_id=1, source_target_pairs={{0,2},{1,3},{2,0},{3,1},{4,6},{5,7},{6,4},{7,5},{8,10},{9,11},{10,... | collective-permute-start | bytes 196616 | tf_op jit(solution)/shard_map/ppermute | solution.py:231
  26.5 0.1 collective-permute-done.8.refs_3_
  26.7 3.1 %collective-permute-start.11 = (bf16[4,16,512]{2,1,0:T(8,128)(2,1)S(1)}, bf16[4,16,512]{2,1,0:T(8,128)(2,1)S(1)}, u32[]{:S(2)}, u32[]{:S(2)}) collective-permute-start(bf16[4,16,512]{2,1,0:T(8,128)(2,1)S(1)} %add_convert_fusion.1.refs_6_), channel_id=1, source_target_pairs={{0,2},{1,3},{2,0},{3,1},{4,6},{5,7},{6,4},{7,5},{8,10},{9,11},{10,... | collective-permute-start | bytes 196616 | tf_op jit(solution)/shard_map/ppermute | solution.py:231
  29.8 1.5 %shard_map.43 = (f32[4,16,512]{2,1,0:T(8,128)S(1)}, f32[4,16,512]{2,1,0:T(8,128)S(1)}) custom-call(bf16[4,8,2048]{2,1,0:T(8,128)(2,1)S(1)} %collective-permute-done.3.refs_0_.refs_1_, bf16[4,8,2048]{2,1,0:T(8,128)(2,1)S(1)} %collective-permute-done.7.refs_1_, bf16[4,8,2048]{2,1,0:T(8,128)(2,1)S(1)} %add.26.refs_2_.refs_0_, ...), custom_call_target="tpu_custom_call" | custom-call | flops 536870912 | bytes 4194304 | tf_op jit(solution)/shard_map/pallas_call | solution.py:215
  31.3 1.2 %collective-permute-done.11.refs_5_ = bf16[4,16,512]{2,1,0:T(8,128)(2,1)S(1)} collective-permute-done((bf16[4,16,512]{2,1,0:T(8,128)(2,1)S(1)}, bf16[4,16,512]{2,1,0:T(8,128)(2,1)S(1)}, u32[]{:S(2)}, u32[]{:S(2)}) %collective-permute-start.11) | collective-permute-done | bytes 65568 | tf_op jit(solution)/shard_map/ppermute | solution.py:231
  32.5 0.7 %shard_map.44 = bf16[2,8,8,512]{3,2,1,0:T(8,128)(2,1)} custom-call(f32[4,16,512]{2,1,0:T(8,128)S(1)} %get-tuple-element.28.refs_0_, f32[4,16,512]{2,1,0:T(8,128)S(1)} %get-tuple-element.29.refs_1_, bf16[8,16,512]{2,1,0:T(8,128)(2,1)S(1)} %collective-permute-done.9.refs_2_, bf16[8,16,512]{2,1,0:T(8,128)(2,1)S(1)} %collective-permute-done.8.refs_3_, ...), custom_call_target="tpu_custom_call" | custom-call | tf_op jit(solution)/shard_map/pallas_call | solution.py:314
  (20 shorter events, 0.5 us)
Async XLA Ops:
  0.0 12.9 %copy-start = (bf16[4,32,4096]{2,1,0:T(8,128)(2,1)S(1)}, bf16[4,32,4096]{2,1,0:T(8,128)(2,1)}, u32[]{:S(2)}) copy-start(bf16[4,32,4096]{2,1,0:T(8,128)(2,1)} %spectra) | copy-start | bytes 3145732
  0.0 12.9 %copy-start.1 = (s32[32]{0:T(128)S(1)}, s32[32]{0:T(128)}, u32[]{:S(2)}) copy-start(s32[32]{0:T(128)} %quality.1) | copy-start | bytes 388
  1.8 1.5 %collective-permute-start = (bf16[4,8,2048]{2,1,0:T(8,128)(2,1)S(1)}, bf16[4,8,2048]{2,1,0:T(8,128)(2,1)S(1)}, u32[]{:S(2)}, u32[]{:S(2)}) collective-permute-start(bf16[4,8,2048]{2,1,0:T(8,128)(2,1)S(1)} %get-tuple-element.19), channel_id=1, source_target_pairs={{0,4},{4,0},{8,12},{12,8},{16,20},{20,16},{24,28},{28,24},{1,5},{5... | collective-permute-start | bytes 393224 | tf_op jit(solution)/shard_map/ppermute | solution.py:231
  2.3 3.9 %collective-permute-start.4 = (bf16[4,8,2048]{2,1,0:T(8,128)(2,1)S(1)}, bf16[4,8,2048]{2,1,0:T(8,128)(2,1)S(1)}, u32[]{:S(2)}, u32[]{:S(2)}) collective-permute-start(bf16[4,8,2048]{2,1,0:T(8,128)(2,1)S(1)} %get-tuple-element.24), channel_id=1, source_target_pairs={{0,4},{4,0},{8,12},{12,8},{16,20},{20,16},{24,28},{28,24},{1,5},{5... | collective-permute-start | bytes 393224 | tf_op jit(solution)/shard_map/ppermute | solution.py:231
  3.3 5.9 %collective-permute-start.1 = (bf16[4,8,2048]{2,1,0:T(8,128)(2,1)S(1)}, bf16[4,8,2048]{2,1,0:T(8,128)(2,1)S(1)}, u32[]{:S(2)}, u32[]{:S(2)}) collective-permute-start(bf16[4,8,2048]{2,1,0:T(8,128)(2,1)S(1)} %add.24), channel_id=1, source_target_pairs={{0,8},{4,20},{8,0},{12,28},{16,24},{20,4},{24,16},{28,12},{1,9},{5... | collective-permute-start | bytes 393224 | tf_op jit(solution)/shard_map/ppermute | solution.py:231
  6.3 5.1 %collective-permute-start.5 = (bf16[4,8,2048]{2,1,0:T(8,128)(2,1)S(1)}, bf16[4,8,2048]{2,1,0:T(8,128)(2,1)S(1)}, u32[]{:S(2)}, u32[]{:S(2)}) collective-permute-start(bf16[4,8,2048]{2,1,0:T(8,128)(2,1)S(1)} %add.27), channel_id=1, source_target_pairs={{0,8},{4,20},{8,0},{12,28},{16,24},{20,4},{24,16},{28,12},{1,9},{5... | collective-permute-start | bytes 393224 | tf_op jit(solution)/shard_map/ppermute | solution.py:231
  9.2 5.1 %collective-permute-start.2 = (bf16[4,8,2048]{2,1,0:T(8,128)(2,1)S(1)}, bf16[4,8,2048]{2,1,0:T(8,128)(2,1)S(1)}, u32[]{:S(2)}, u32[]{:S(2)}) collective-permute-start(bf16[4,8,2048]{2,1,0:T(8,128)(2,1)S(1)} %add.25), channel_id=1, source_target_pairs={{0,16},{4,12},{8,24},{12,4},{16,0},{20,28},{24,8},{28,20},{1,17},{... | collective-permute-start | bytes 393224 | tf_op jit(solution)/shard_map/ppermute | solution.py:231
  11.4 5.0 %collective-permute-start.6 = (bf16[4,8,2048]{2,1,0:T(8,128)(2,1)S(1)}, bf16[4,8,2048]{2,1,0:T(8,128)(2,1)S(1)}, u32[]{:S(2)}, u32[]{:S(2)}) collective-permute-start(bf16[4,8,2048]{2,1,0:T(8,128)(2,1)S(1)} %add.28), channel_id=1, source_target_pairs={{0,16},{4,12},{8,24},{12,4},{16,0},{20,28},{24,8},{28,20},{1,17},{... | collective-permute-start | bytes 393224 | tf_op jit(solution)/shard_map/ppermute | solution.py:231
  14.3 2.2 %collective-permute-start.3 = (bf16[4,8,2048]{2,1,0:T(8,128)(2,1)S(1)}, bf16[4,8,2048]{2,1,0:T(8,128)(2,1)S(1)}, u32[]{:S(2)}, u32[]{:S(2)}) collective-permute-start(bf16[4,8,2048]{2,1,0:T(8,128)(2,1)S(1)} %add.26.refs_2_.refs_0_), channel_id=1, source_target_pairs={{0,4},{4,0},{8,12},{12,8},{16,20},{20,16},{24,28},{28,24},{1,5},{5... | collective-permute-start | bytes 393224 | tf_op jit(solution)/shard_map/ppermute | solution.py:231
  16.4 3.1 %collective-permute-start.7 = (bf16[4,8,2048]{2,1,0:T(8,128)(2,1)S(1)}, bf16[4,8,2048]{2,1,0:T(8,128)(2,1)S(1)}, u32[]{:S(2)}, u32[]{:S(2)}) collective-permute-start(bf16[4,8,2048]{2,1,0:T(8,128)(2,1)S(1)} %add.29.refs_3_.refs_0_), channel_id=1, source_target_pairs={{0,4},{4,0},{8,12},{12,8},{16,20},{20,16},{24,28},{28,24},{1,5},{5... | collective-permute-start | bytes 393224 | tf_op jit(solution)/shard_map/ppermute | solution.py:231
  17.9 6.0 %collective-permute-start.9 = (bf16[8,16,512]{2,1,0:T(8,128)(2,1)S(1)}, bf16[8,16,512]{2,1,0:T(8,128)(2,1)S(1)}, u32[]{:S(2)}, u32[]{:S(2)}) collective-permute-start(bf16[8,16,512]{2,1,0:T(8,128)(2,1)S(1)} %shard_map.41.refs_4_), channel_id=1, source_target_pairs={{0,1},{1,0},{2,3},{3,2},{4,5},{5,4},{6,7},{7,6},{8,9},{9,8},{10,11... | collective-permute-start | bytes 393224 | tf_op jit(solution)/shard_map/ppermute | solution.py:231
  20.9 5.7 %collective-permute-start.8 = (bf16[8,16,512]{2,1,0:T(8,128)(2,1)S(1)}, bf16[8,16,512]{2,1,0:T(8,128)(2,1)S(1)}, u32[]{:S(2)}, u32[]{:S(2)}) collective-permute-start(bf16[8,16,512]{2,1,0:T(8,128)(2,1)S(1)} %shard_map.42), channel_id=1, source_target_pairs={{0,1},{1,0},{2,3},{3,2},{4,5},{5,4},{6,7},{7,6},{8,9},{9,8},{10,11... | collective-permute-start | bytes 393224 | tf_op jit(solution)/shard_map/ppermute | solution.py:231
  23.9 7.4 %collective-permute-start.10 = (bf16[4,16,512]{2,1,0:T(8,128)(2,1)S(1)}, bf16[4,16,512]{2,1,0:T(8,128)(2,1)S(1)}, u32[]{:S(2)}, u32[]{:S(2)}) collective-permute-start(bf16[4,16,512]{2,1,0:T(8,128)(2,1)S(1)} %add_convert_fusion), channel_id=1, source_target_pairs={{0,2},{1,3},{2,0},{3,1},{4,6},{5,7},{6,4},{7,5},{8,10},{9,11},{10,... | collective-permute-start | bytes 196616 | tf_op jit(solution)/shard_map/ppermute | solution.py:231
  26.7 5.8 %collective-permute-start.11 = (bf16[4,16,512]{2,1,0:T(8,128)(2,1)S(1)}, bf16[4,16,512]{2,1,0:T(8,128)(2,1)S(1)}, u32[]{:S(2)}, u32[]{:S(2)}) collective-permute-start(bf16[4,16,512]{2,1,0:T(8,128)(2,1)S(1)} %add_convert_fusion.1.refs_6_), channel_id=1, source_target_pairs={{0,2},{1,3},{2,0},{3,1},{4,6},{5,7},{6,4},{7,5},{8,10},{9,11},{10,... | collective-permute-start | bytes 196616 | tf_op jit(solution)/shard_map/ppermute | solution.py:231

commit v4 on v3

--- a/solution.py
+++ b/solution.py
@@ -70,8 +70,9 @@
         base = block % per_group * SRC
         flags = column(SRC, lambda row: (quality[base + row] * held).astype(F32))
         chosen.append((pl.multiple_of(base // 16 * 16, 16), base % 16 != 0, flags))
+    for copy in copies[2:]:
+        copy.wait()
     for window in range(windows):
-        copies[2 + window].wait()
         for step, (aligned, upper, flags) in enumerate(chosen):
             rows = spectra[window, pl.ds(aligned, 16), :].astype(F32)
             values = whitened_rows(jnp.where(upper, rows[SRC:], rows[:SRC]), flags)
@@ -118,19 +119,14 @@
         ).astype(BF16)
 
 
-def lagged_kernel(distances, plan, carried, zeros, *refs):
+def lagged_kernel(distances, plan, *refs):
     steps = sorted({step for _, present in plan for step in present})
     count = sum(len(present) for _, present in plan)
     sources, (receivers, table), refs = list(refs[:count]), refs[count : count + 2], refs[count + 2 :]
-    carry = refs[: len(carried)]
-    if zeros:
-        refs, out = refs[:-1], refs[-1]
-        out[...] = jnp.zeros_like(out)
     outs = refs[len(refs) - len(steps) :]
     core = lax.axis_index("chan") % 2
     _, windows, rows, width = receivers.shape
     bins, part = width // 2, width // 4
-    lines = rows * SRC
     depth = TILES_PER_DOT * LANES
 
     def cross_tile(pair, start, at):
@@ -141,39 +137,29 @@
         ]
         real = pl.ds(pl.multiple_of(start + at, LANES), LANES)
         imag = pl.ds(pl.multiple_of(bins + start + at, LANES), LANES)
-        found = [[[], []] for _ in pair]
+        found = [[], []]
         for distance in distances:
             owner = lax.axis_index("win") ^ distance
+            held = []
             for row in range(rows):
                 sums = [[None, None] for _ in pair]
                 for w in range(windows):
                     rec_real = receivers[owner, w, pl.ds(row, 1), real]
                     rec_imag = receivers[owner, w, pl.ds(row, 1), imag]
-                    for s in range(len(pair)):
-                        src_real, src_imag = src[s][w]
+                    for total, one in zip(sums, src, strict=True):
+                        src_real, src_imag = one[w]
                         re = src_real * rec_real + src_imag * rec_imag
                         im = src_real * rec_imag - src_imag * rec_real
-                        sums[s][0] = re if w == 0 else sums[s][0] + re
-                        sums[s][1] = im if w == 0 else sums[s][1] + im
-                for s in range(len(pair)):
+                        total[0] = re if w == 0 else total[0] + re
+                        total[1] = im if w == 0 else total[1] + im
+                held += sums
+                if len(held) == 2:
                     for p in range(2):
-                        found[s][p].append(sums[s][p])
-        return [
-            jnp.concatenate(
-                [
-                    jnp.concatenate(one[p][row : row + 2], axis=0).astype(BF16)
-                    for one in found
-                    for row in range(0, len(one[p]), 2)
-                ],
-                axis=0,
-            )
-            for p in range(2)
-        ]
-
-    totals = {}
-    for ref, step in zip(carry, carried, strict=True):
-        held = [ref[distance * rows // 2 + pair] for distance in distances for pair in range(rows // 2)]
-        totals[step] = jnp.concatenate(held, axis=0)
+                        found[p].append(jnp.concatenate([total[p] for total in held], axis=0).astype(BF16))
+                    held = []
+        return [jnp.concatenate(found[p], axis=0) for p in range(2)]
+
+    total = None
     for other, present in plan:
         pair, sources = sources[: len(present)], sources[len(present) :]
         start = (1 - core if other else core) * part
@@ -184,39 +170,34 @@
                 cross = jnp.concatenate([tile[p] for tile in tiles], axis=1)
                 where = pl.ds(pl.multiple_of(p * bins + start + at, depth), depth)
                 product = jnp.dot(cross, table[where, :], preferred_element_type=F32)
-                for place, step in enumerate(present):
-                    height = lines * len(distances)
-                    piece = product[place * height : (place + 1) * height]
-                    totals[step] = totals[step] + piece if step in totals else piece
-    for out, step in zip(outs, steps, strict=True):
+                total = product if total is None else total + product
+    for place, out in enumerate(outs):
         for pair in range(out.shape[0]):
-            out[pair] = totals[step][pair * 2 * SRC : (pair + 1) * 2 * SRC].astype(out.dtype)
+            lines = [((2 * pair + row) * len(steps) + place) * SRC for row in range(2)]
+            out[pair] = jnp.concatenate([total[line : line + SRC] for line in lines], axis=0).astype(out.dtype)
 
 
 def stack_kernel(firsts, *refs):
-    refs, out = refs[:-1], refs[-1]
+    refs, out = list(refs[:-1]), refs[-1]
     for step in range(STEPS):
+        terms = list(zip(refs, firsts[step], strict=False))
+        refs = refs[len(terms) :]
         for pair in range(out.shape[1] // 2):
-            terms = zip(refs[step::STEPS], firsts, strict=True)
             total = sum(ref[first + pair].astype(F32) for ref, first in terms)
             out[step, 2 * pair] = total[:SRC].astype(BF16)
             out[step, 2 * pair + 1] = total[SRC:].astype(BF16)
 
 
-def lagged_call(distances, plan, sources, receivers, table, dtype, carry=None, after=(), zeros=None):
+def lagged_call(distances, plan, sources, receivers, table, dtype, after=()):
     _, windows, rows, width = receivers.shape
-    carry = carry or {}
-    carried = sorted(carry)
+    operands = [*sources, receivers, table]
     count = len({step for _, present in plan for step in present})
-    operands = [*sources, receivers, table, *(carry[step] for step in carried)]
-    shapes = [jax.ShapeDtypeStruct((len(distances) * rows // 2, 2 * SRC, L), dtype)] * count
-    if zeros is not None:
-        shapes.append(jax.ShapeDtypeStruct(zeros, BF16))
+    shape = jax.ShapeDtypeStruct((len(distances) * rows // 2, 2 * SRC, L), dtype)
     return pl.pallas_call(
-        functools.partial(lagged_kernel, distances, plan, carried, zeros is not None),
-        out_shape=shapes,
+        functools.partial(lagged_kernel, distances, plan),
+        out_shape=[shape] * count,
         in_specs=[vmem()] * len(operands) + [pl.BlockSpec(memory_space=pl.ANY)] * len(after),
-        out_specs=[vmem()] * len(shapes),
+        out_specs=[vmem()] * count,
         compiler_params=params(),
         cost_estimate=pl.CostEstimate(
             flops=len(distances) * len(sources) * rows * SRC * width * L,
@@ -279,45 +260,50 @@
         compiler_params=params(),
     )(quality, spectra)
 
-    odd = [distance for distance in reversed(range(places)) if distance & 1]
     mine[0] = mine[0] + arrived[0]
     mine[0], receivers = lax.optimization_barrier((mine[0], receivers))
-    other = [exchange(mine[0], "chan", 1)]
-    halves = [(False, (0,)), (True, (0,))]
-    (first,) = lagged_call(odd, halves, [mine[0], other[0]], receivers, table, BF16)
+
+    def lagged(distances, steps, dtype, after=()):
+        plan = [(False, steps), (True, steps)]
+        operands = [sources[step][half] for half in range(2) for step in steps]
+        return lagged_call(distances, plan, operands, receivers, table, dtype, after)
+
+    pairs = rows // 2
+    received = [[] for _ in range(STEPS)]
+    odd = list(reversed(range(1, places, 2)))
+    sources = [(mine[0], exchange(mine[0], "chan", 1))]
     mine[1] = mine[1] + arrived[1]
-    other.append(exchange(mine[1], "chan", 1))
-    halves = [(False, (1,)), (True, (1,))]
-    (second,) = lagged_call(odd, halves, [mine[1], other[1]], receivers, table, BF16, after=[first])
-
-    def lagged(distances, after=()):
-        plan = [(True, (0, 1)), (False, (0, 1))]
-        return lagged_call(distances, plan, [*other, *mine], receivers, table, F32, after=after)
-
-    pairs = rows // 2
-    received = [([distance ^ 1 for distance in odd], [exchange(part, "win", 1) for part in (first, second)])]
-    last = ()
+    sources.append((mine[1], exchange(mine[1], "chan", 1)))
+    (part,) = last = lagged(odd, (0,), BF16)
+    received[0].append(([distance ^ 1 for distance in odd], exchange(part, "win", 1)))
+    (part,) = last = lagged(odd, (1,), BF16, last)
+    received[1].append(([distance ^ 1 for distance in odd], exchange(part, "win", 1)))
     for bit in range(1, (places - 1).bit_length()):
         group = [distance for distance in reversed(range(0, places, 1 << bit)) if distance >> bit & 1]
-        sums = list(lagged(group, last))
-        for order, parts in received:
-            here = [order.index(distance) * pairs for distance in group]
-            for step in range(STEPS):
-                new = jnp.concatenate([parts[step][at : at + pairs] for at in here])
+        sums = list(lagged(group, (0, 1), F32))
+        for step in range(STEPS):
+            for order, part in received[step]:
+                here = [order.index(distance) * pairs for distance in group]
+                new = jnp.concatenate([part[at : at + pairs] for at in here])
                 sums[step] = sums[step] + new.astype(F32)
-        sums = [part.astype(BF16) for part in sums]
-        last = sums[1:]
-        received.append(([distance ^ 1 << bit for distance in group], [exchange(part, "win", 1 << bit) for part in sums]))
-    own = lagged([0], last)
-    terms = [*own, *(part for _, parts in received for part in parts)]
+            sums[step] = sums[step].astype(BF16)
+        last = tuple(sums[1:])
+        for step in range(STEPS):
+            received[step].append(([distance ^ 1 << bit for distance in group], exchange(sums[step], "win", 1 << bit)))
+    own = lagged([0], (0, 1), F32, last)
+    terms = [
+        [(own[step], 0)] + [(part, (len(order) - 1) * pairs) for order, part in received[step] if order[-1] == 0]
+        for step in range(STEPS)
+    ]
+    operands = [part for step in terms for part, _ in step]
 
     return pl.pallas_call(
-        functools.partial(stack_kernel, [0, *(order.index(0) * pairs for order, _ in received)]),
+        functools.partial(stack_kernel, [[first for _, first in step] for step in terms]),
         out_shape=jax.ShapeDtypeStruct((STEPS, rows, SRC, L), BF16),
-        in_specs=[vmem()] * len(terms),
+        in_specs=[vmem()] * len(operands),
         out_specs=vmem(),
         compiler_params=params(),
-    )(*terms)
+    )(*operands)
 
 
 def solution(mesh):

time: 33.4 us -> 33.2 us (level)
  transfers between devices with their start and end apart: 12 -> 12, of which waited for: 7 -> 7; matrix products, arithmetic and copies ran while one was open for 1% -> 1% of each run, Pallas kernels for 27% -> 26%
where the time goes in v4:
time: 33.2 us; the launch traced here: 33.1 us
  starting transfers between devices  15.4 us (46%)
  Pallas kernels  11 us (33%)
  waiting for transfers between devices  6.36 us (19%)
    ppermute x12, starting transfers between devices, exchange(): lax.ppermute(value, axis, [(i, i ^ distances[i % len(distances)]) for i i...  15.4 us
    ppermute x12, waiting for transfers between devices, exchange(): lax.ppermute(value, axis, [(i, i ^ distances[i % len(distances)]) for i i...  6.36 us
    pallas_call x4, Pallas kernels, lagged_call(): pl.pallas_call(functools.partial(lagged_kernel, distances, plan), out_sha...  5.53 us
    pallas_call x1, Pallas kernels, body(): pl.pallas_call(functools.partial(table_kernel, factor), out_shape=jax.Sha...  2.08 us
    pallas_call x1, Pallas kernels, body(): pl.pallas_call(sources_kernel, out_shape=[jax.ShapeDtypeStruct((windows,...  1.63 us
    pallas_call x1, Pallas kernels, body(): pl.pallas_call(receivers_kernel, out_shape=jax.ShapeDtypeStruct((places,...  1.07 us
    pallas_call x1, Pallas kernels, body(): pl.pallas_call(functools.partial(stack_kernel, [[first for _, first in st...  0.7 us
  transfers between devices with their start and end apart: 12, of which 7 were waited for; matrix products, arithmetic and copies ran while one was open for 1% of the time, Pallas kernels for 26%

profile of v4, /device:TPU:0, one launch (start us, length us, event | category | flops | bytes accessed | tf_op | source)
XLA Modules:
  0.0 33.1 jit_solution(154793134856750411)
XLA Ops:
  0.0 1.6 %shard_map.37 = (bf16[4,8,2048]{2,1,0:T(8,128)(2,1)S(1)}, bf16[4,8,2048]{2,1,0:T(8,128)(2,1)S(1)}, bf16[4,8,2048]{2,1,0:T(8,128)(2,1)S(1)}, bf16[4,8,2048]{2,1,0:T(8,128)(2,1)S(1)}) custom-call(s32[2]{0:T(128)} %blocks_in.1, s32[32]{0:T(128)} %quality.1, bf16[4,32,4096]{2,1,0:T(8,128)(2,1)} %spectra), custom_call_target="tpu_custom_call" | custom-call | tf_op jit(solution)/shard_map/pallas_call | solution.py:224
  1.6 0.5 %collective-permute-start = (bf16[4,8,2048]{2,1,0:T(8,128)(2,1)S(1)}, bf16[4,8,2048]{2,1,0:T(8,128)(2,1)S(1)}, u32[]{:S(2)}, u32[]{:S(2)}) collective-permute-start(bf16[4,8,2048]{2,1,0:T(8,128)(2,1)S(1)} %get-tuple-element.19), channel_id=1, source_target_pairs={{0,4},{4,0},{8,12},{12,8},{16,20},{20,16},{24,28},{28,24},{1,5},{5... | collective-permute-start | bytes 393224 | tf_op jit(solution)/shard_map/ppermute | solution.py:212
  2.2 0.9 %collective-permute-done = bf16[4,8,2048]{2,1,0:T(8,128)(2,1)S(1)} collective-permute-done((bf16[4,8,2048]{2,1,0:T(8,128)(2,1)S(1)}, bf16[4,8,2048]{2,1,0:T(8,128)(2,1)S(1)}, u32[]{:S(2)}, u32[]{:S(2)}) %collective-permute-start) | collective-permute-done | bytes 131104 | tf_op jit(solution)/shard_map/ppermute | solution.py:212
  3.2 2.9 %collective-permute-start.1 = (bf16[4,8,2048]{2,1,0:T(8,128)(2,1)S(1)}, bf16[4,8,2048]{2,1,0:T(8,128)(2,1)S(1)}, u32[]{:S(2)}, u32[]{:S(2)}) collective-permute-start(bf16[4,8,2048]{2,1,0:T(8,128)(2,1)S(1)} %add.24), channel_id=1, source_target_pairs={{0,8},{4,20},{8,0},{12,28},{16,24},{20,4},{24,16},{28,12},{1,9},{5... | collective-permute-start | bytes 393224 | tf_op jit(solution)/shard_map/ppermute | solution.py:212
  6.1 0.1 collective-permute-start.4
  6.3 2.1 %shard_map.38.refs_5_.refs_3_ = bf16[4096,512]{1,0:T(8,128)(2,1)S(1)} custom-call(), custom_call_target="tpu_custom_call" | custom-call | tf_op jit(solution)/shard_map/pallas_call | solution.py:238
  8.4 0.7 %collective-permute-done.1 = bf16[4,8,2048]{2,1,0:T(8,128)(2,1)S(1)} collective-permute-done((bf16[4,8,2048]{2,1,0:T(8,128)(2,1)S(1)}, bf16[4,8,2048]{2,1,0:T(8,128)(2,1)S(1)}, u32[]{:S(2)}, u32[]{:S(2)}) %collective-permute-start.1) | collective-permute-done | bytes 131104 | tf_op jit(solution)/shard_map/ppermute | solution.py:212
  9.1 2.1 %collective-permute-start.2 = (bf16[4,8,2048]{2,1,0:T(8,128)(2,1)S(1)}, bf16[4,8,2048]{2,1,0:T(8,128)(2,1)S(1)}, u32[]{:S(2)}, u32[]{:S(2)}) collective-permute-start(bf16[4,8,2048]{2,1,0:T(8,128)(2,1)S(1)} %add.25), channel_id=1, source_target_pairs={{0,16},{4,12},{8,24},{12,4},{16,0},{20,28},{24,8},{28,20},{1,17},{... | collective-permute-start | bytes 393224 | tf_op jit(solution)/shard_map/ppermute | solution.py:212
  11.2 1.6 %collective-permute-start.5 = (bf16[4,8,2048]{2,1,0:T(8,128)(2,1)S(1)}, bf16[4,8,2048]{2,1,0:T(8,128)(2,1)S(1)}, u32[]{:S(2)}, u32[]{:S(2)}) collective-permute-start(bf16[4,8,2048]{2,1,0:T(8,128)(2,1)S(1)} %add.28), channel_id=1, source_target_pairs={{0,16},{4,12},{8,24},{12,4},{16,0},{20,28},{24,8},{28,20},{1,17},{... | collective-permute-start | bytes 393224 | tf_op jit(solution)/shard_map/ppermute | solution.py:212
  12.8 1.1 %shard_map.39.refs_4_.refs_2_ = f32[4,4,8,4096]{3,2,1,0:T(8,128)S(1)} custom-call(s32[32]{0:T(128)S(1)} %copy-done.1, bf16[4,32,4096]{2,1,0:T(8,128)(2,1)S(1)} %copy-done), custom_call_target="tpu_custom_call" | custom-call | tf_op jit(solution)/shard_map/pallas_call | solution.py:255
  13.9 0.3 collective-permute-done.2
  14.3 2.0 %collective-permute-done.5 = bf16[4,8,2048]{2,1,0:T(8,128)(2,1)S(1)} collective-permute-done((bf16[4,8,2048]{2,1,0:T(8,128)(2,1)S(1)}, bf16[4,8,2048]{2,1,0:T(8,128)(2,1)S(1)}, u32[]{:S(2)}, u32[]{:S(2)}) %collective-permute-start.5) | collective-permute-done | bytes 131104 | tf_op jit(solution)/shard_map/ppermute | solution.py:212
  16.4 1.4 %shard_map.41.refs_4_ = bf16[8,16,512]{2,1,0:T(8,128)(2,1)S(1)} custom-call(bf16[4,8,2048]{2,1,0:T(8,128)(2,1)S(1)} %add.26.refs_0_, bf16[4,8,2048]{2,1,0:T(8,128)(2,1)S(1)} %collective-permute-done.6.refs_2_.refs_1_, f32[4,4,8,4096]{3,2,1,0:T(8,128)S(1)} %shard_map.39.refs_4_.refs_2_, bf16[4096,512]{1,0:T(8,128)(2,1)S(1)} %shard_map.38.refs_5_.refs_3_), custom_call_target="tpu_custom_call" | custom-call | flops 536870912 | bytes 4194304 | tf_op jit(solution)/shard_map/pallas_call | solution.py:196
  17.8 1.6 %collective-permute-start.9 = (bf16[8,16,512]{2,1,0:T(8,128)(2,1)S(1)}, bf16[8,16,512]{2,1,0:T(8,128)(2,1)S(1)}, u32[]{:S(2)}, u32[]{:S(2)}) collective-permute-start(bf16[8,16,512]{2,1,0:T(8,128)(2,1)S(1)} %shard_map.41.refs_4_), channel_id=1, source_target_pairs={{0,1},{1,0},{2,3},{3,2},{4,5},{5,4},{6,7},{7,6},{8,9},{9,8},{10,11... | collective-permute-start | bytes 393224 | tf_op jit(solution)/shard_map/ppermute | solution.py:212
  19.4 1.4 %shard_map.42 = bf16[8,16,512]{2,1,0:T(8,128)(2,1)S(1)} custom-call(bf16[4,8,2048]{2,1,0:T(8,128)(2,1)S(1)} %add.29.refs_1_.refs_0_, bf16[4,8,2048]{2,1,0:T(8,128)(2,1)S(1)} %collective-permute-done.7.refs_3_.refs_1_, f32[4,4,8,4096]{3,2,1,0:T(8,128)S(1)} %shard_map.39.refs_4_.refs_2_, bf16[4096,512]{1,0:T(8,128)(2,1)S(1)} %shard_map.38.refs_5_.refs_3_, ...), custom_call_target="tpu_custom_call" | custom-call | flops 536870912 | bytes 4194304 | tf_op jit(solution)/shard_map/pallas_call | solution.py:196
  20.8 0.5 %collective-permute-start.8 = (bf16[8,16,512]{2,1,0:T(8,128)(2,1)S(1)}, bf16[8,16,512]{2,1,0:T(8,128)(2,1)S(1)}, u32[]{:S(2)}, u32[]{:S(2)}) collective-permute-start(bf16[8,16,512]{2,1,0:T(8,128)(2,1)S(1)} %shard_map.42), channel_id=1, source_target_pairs={{0,1},{1,0},{2,3},{3,2},{4,5},{5,4},{6,7},{7,6},{8,9},{9,8},{10,11... | collective-permute-start | bytes 393224 | tf_op jit(solution)/shard_map/ppermute | solution.py:212
  21.3 1.4 %shard_map.40 = (f32[4,16,512]{2,1,0:T(8,128)S(1)}, f32[4,16,512]{2,1,0:T(8,128)S(1)}) custom-call(bf16[4,8,2048]{2,1,0:T(8,128)(2,1)S(1)} %add.26.refs_0_, bf16[4,8,2048]{2,1,0:T(8,128)(2,1)S(1)} %add.29.refs_1_.refs_0_, bf16[4,8,2048]{2,1,0:T(8,128)(2,1)S(1)} %collective-permute-done.6.refs_2_.refs_1_, ...), custom_call_target="tpu_custom_call" | custom-call | flops 536870912 | bytes 4194304 | tf_op jit(solution)/shard_map/pallas_call | solution.py:196
  22.7 1.0 %collective-permute-done.9.refs_1_ = bf16[8,16,512]{2,1,0:T(8,128)(2,1)S(1)} collective-permute-done((bf16[8,16,512]{2,1,0:T(8,128)(2,1)S(1)}, bf16[8,16,512]{2,1,0:T(8,128)(2,1)S(1)}, u32[]{:S(2)}, u32[]{:S(2)}) %collective-permute-start.9) | collective-permute-done | bytes 131104 | tf_op jit(solution)/shard_map/ppermute | solution.py:212
  23.8 2.7 %collective-permute-start.10 = (bf16[4,16,512]{2,1,0:T(8,128)(2,1)S(1)}, bf16[4,16,512]{2,1,0:T(8,128)(2,1)S(1)}, u32[]{:S(2)}, u32[]{:S(2)}) collective-permute-start(bf16[4,16,512]{2,1,0:T(8,128)(2,1)S(1)} %add_convert_fusion), channel_id=1, source_target_pairs={{0,2},{1,3},{2,0},{3,1},{4,6},{5,7},{6,4},{7,5},{8,10},{9,11},{10,... | collective-permute-start | bytes 196616 | tf_op jit(solution)/shard_map/ppermute | solution.py:212
  26.4 0.1 collective-permute-done.8.refs_4_
  26.6 3.1 %collective-permute-start.11 = (bf16[4,16,512]{2,1,0:T(8,128)(2,1)S(1)}, bf16[4,16,512]{2,1,0:T(8,128)(2,1)S(1)}, u32[]{:S(2)}, u32[]{:S(2)}) collective-permute-start(bf16[4,16,512]{2,1,0:T(8,128)(2,1)S(1)} %add_convert_fusion.1.refs_6_), channel_id=1, source_target_pairs={{0,2},{1,3},{2,0},{3,1},{4,6},{5,7},{6,4},{7,5},{8,10},{9,11},{10,... | collective-permute-start | bytes 196616 | tf_op jit(solution)/shard_map/ppermute | solution.py:212
  29.7 1.4 %shard_map.43 = (f32[4,16,512]{2,1,0:T(8,128)S(1)}, f32[4,16,512]{2,1,0:T(8,128)S(1)}) custom-call(bf16[4,8,2048]{2,1,0:T(8,128)(2,1)S(1)} %add.26.refs_0_, bf16[4,8,2048]{2,1,0:T(8,128)(2,1)S(1)} %add.29.refs_1_.refs_0_, bf16[4,8,2048]{2,1,0:T(8,128)(2,1)S(1)} %collective-permute-done.6.refs_2_.refs_1_, ...), custom_call_target="tpu_custom_call" | custom-call | flops 536870912 | bytes 4194304 | tf_op jit(solution)/shard_map/pallas_call | solution.py:196
  31.1 1.3 %collective-permute-done.11.refs_5_ = bf16[4,16,512]{2,1,0:T(8,128)(2,1)S(1)} collective-permute-done((bf16[4,16,512]{2,1,0:T(8,128)(2,1)S(1)}, bf16[4,16,512]{2,1,0:T(8,128)(2,1)S(1)}, u32[]{:S(2)}, u32[]{:S(2)}) %collective-permute-start.11) | collective-permute-done | bytes 65568 | tf_op jit(solution)/shard_map/ppermute | solution.py:212
  32.4 0.7 %shard_map.44 = bf16[2,8,8,512]{3,2,1,0:T(8,128)(2,1)} custom-call(f32[4,16,512]{2,1,0:T(8,128)S(1)} %get-tuple-element.28.refs_0_, bf16[8,16,512]{2,1,0:T(8,128)(2,1)S(1)} %collective-permute-done.9.refs_1_, bf16[4,16,512]{2,1,0:T(8,128)(2,1)S(1)} %collective-permute-done.10.refs_2_, f32[4,16,512]{2,1,0:T(8,128)S(1)} %get-tuple-element.30.refs_3_, ...), custom_call_target="tpu_custom_call" | custom-call | tf_op jit(solution)/shard_map/pallas_call | solution.py:300
  (20 shorter events, 0.5 us)
Async XLA Ops:
  0.0 12.8 %copy-start = (bf16[4,32,4096]{2,1,0:T(8,128)(2,1)S(1)}, bf16[4,32,4096]{2,1,0:T(8,128)(2,1)}, u32[]{:S(2)}) copy-start(bf16[4,32,4096]{2,1,0:T(8,128)(2,1)} %spectra) | copy-start | bytes 3145732
  0.0 12.8 %copy-start.1 = (s32[32]{0:T(128)S(1)}, s32[32]{0:T(128)}, u32[]{:S(2)}) copy-start(s32[32]{0:T(128)} %quality.1) | copy-start | bytes 388
  1.6 1.5 %collective-permute-start = (bf16[4,8,2048]{2,1,0:T(8,128)(2,1)S(1)}, bf16[4,8,2048]{2,1,0:T(8,128)(2,1)S(1)}, u32[]{:S(2)}, u32[]{:S(2)}) collective-permute-start(bf16[4,8,2048]{2,1,0:T(8,128)(2,1)S(1)} %get-tuple-element.19), channel_id=1, source_target_pairs={{0,4},{4,0},{8,12},{12,8},{16,20},{20,16},{24,28},{28,24},{1,5},{5... | collective-permute-start | bytes 393224 | tf_op jit(solution)/shard_map/ppermute | solution.py:212
  2.2 3.9 %collective-permute-start.3 = (bf16[4,8,2048]{2,1,0:T(8,128)(2,1)S(1)}, bf16[4,8,2048]{2,1,0:T(8,128)(2,1)S(1)}, u32[]{:S(2)}, u32[]{:S(2)}) collective-permute-start(bf16[4,8,2048]{2,1,0:T(8,128)(2,1)S(1)} %get-tuple-element.24), channel_id=1, source_target_pairs={{0,4},{4,0},{8,12},{12,8},{16,20},{20,16},{24,28},{28,24},{1,5},{5... | collective-permute-start | bytes 393224 | tf_op jit(solution)/shard_map/ppermute | solution.py:212
  3.2 5.9 %collective-permute-start.1 = (bf16[4,8,2048]{2,1,0:T(8,128)(2,1)S(1)}, bf16[4,8,2048]{2,1,0:T(8,128)(2,1)S(1)}, u32[]{:S(2)}, u32[]{:S(2)}) collective-permute-start(bf16[4,8,2048]{2,1,0:T(8,128)(2,1)S(1)} %add.24), channel_id=1, source_target_pairs={{0,8},{4,20},{8,0},{12,28},{16,24},{20,4},{24,16},{28,12},{1,9},{5... | collective-permute-start | bytes 393224 | tf_op jit(solution)/shard_map/ppermute | solution.py:212
  6.1 5.1 %collective-permute-start.4 = (bf16[4,8,2048]{2,1,0:T(8,128)(2,1)S(1)}, bf16[4,8,2048]{2,1,0:T(8,128)(2,1)S(1)}, u32[]{:S(2)}, u32[]{:S(2)}) collective-permute-start(bf16[4,8,2048]{2,1,0:T(8,128)(2,1)S(1)} %add.27), channel_id=1, source_target_pairs={{0,8},{4,20},{8,0},{12,28},{16,24},{20,4},{24,16},{28,12},{1,9},{5... | collective-permute-start | bytes 393224 | tf_op jit(solution)/shard_map/ppermute | solution.py:212
  9.1 5.1 %collective-permute-start.2 = (bf16[4,8,2048]{2,1,0:T(8,128)(2,1)S(1)}, bf16[4,8,2048]{2,1,0:T(8,128)(2,1)S(1)}, u32[]{:S(2)}, u32[]{:S(2)}) collective-permute-start(bf16[4,8,2048]{2,1,0:T(8,128)(2,1)S(1)} %add.25), channel_id=1, source_target_pairs={{0,16},{4,12},{8,24},{12,4},{16,0},{20,28},{24,8},{28,20},{1,17},{... | collective-permute-start | bytes 393224 | tf_op jit(solution)/shard_map/ppermute | solution.py:212
  11.2 5.0 %collective-permute-start.5 = (bf16[4,8,2048]{2,1,0:T(8,128)(2,1)S(1)}, bf16[4,8,2048]{2,1,0:T(8,128)(2,1)S(1)}, u32[]{:S(2)}, u32[]{:S(2)}) collective-permute-start(bf16[4,8,2048]{2,1,0:T(8,128)(2,1)S(1)} %add.28), channel_id=1, source_target_pairs={{0,16},{4,12},{8,24},{12,4},{16,0},{20,28},{24,8},{28,20},{1,17},{... | collective-permute-start | bytes 393224 | tf_op jit(solution)/shard_map/ppermute | solution.py:212
  14.2 2.2 %collective-permute-start.6 = (bf16[4,8,2048]{2,1,0:T(8,128)(2,1)S(1)}, bf16[4,8,2048]{2,1,0:T(8,128)(2,1)S(1)}, u32[]{:S(2)}, u32[]{:S(2)}) collective-permute-start(bf16[4,8,2048]{2,1,0:T(8,128)(2,1)S(1)} %add.26.refs_0_), channel_id=1, source_target_pairs={{0,4},{4,0},{8,12},{12,8},{16,20},{20,16},{24,28},{28,24},{1,5},{5... | collective-permute-start | bytes 393224 | tf_op jit(solution)/shard_map/ppermute | solution.py:212
  16.3 3.1 %collective-permute-start.7 = (bf16[4,8,2048]{2,1,0:T(8,128)(2,1)S(1)}, bf16[4,8,2048]{2,1,0:T(8,128)(2,1)S(1)}, u32[]{:S(2)}, u32[]{:S(2)}) collective-permute-start(bf16[4,8,2048]{2,1,0:T(8,128)(2,1)S(1)} %add.29.refs_1_.refs_0_), channel_id=1, source_target_pairs={{0,4},{4,0},{8,12},{12,8},{16,20},{20,16},{24,28},{28,24},{1,5},{5... | collective-permute-start | bytes 393224 | tf_op jit(solution)/shard_map/ppermute | solution.py:212
  17.8 6.0 %collective-permute-start.9 = (bf16[8,16,512]{2,1,0:T(8,128)(2,1)S(1)}, bf16[8,16,512]{2,1,0:T(8,128)(2,1)S(1)}, u32[]{:S(2)}, u32[]{:S(2)}) collective-permute-start(bf16[8,16,512]{2,1,0:T(8,128)(2,1)S(1)} %shard_map.41.refs_4_), channel_id=1, source_target_pairs={{0,1},{1,0},{2,3},{3,2},{4,5},{5,4},{6,7},{7,6},{8,9},{9,8},{10,11... | collective-permute-start | bytes 393224 | tf_op jit(solution)/shard_map/ppermute | solution.py:212
  20.8 5.7 %collective-permute-start.8 = (bf16[8,16,512]{2,1,0:T(8,128)(2,1)S(1)}, bf16[8,16,512]{2,1,0:T(8,128)(2,1)S(1)}, u32[]{:S(2)}, u32[]{:S(2)}) collective-permute-start(bf16[8,16,512]{2,1,0:T(8,128)(2,1)S(1)} %shard_map.42), channel_id=1, source_target_pairs={{0,1},{1,0},{2,3},{3,2},{4,5},{5,4},{6,7},{7,6},{8,9},{9,8},{10,11... | collective-permute-start | bytes 393224 | tf_op jit(solution)/shard_map/ppermute | solution.py:212
  23.8 7.3 %collective-permute-start.10 = (bf16[4,16,512]{2,1,0:T(8,128)(2,1)S(1)}, bf16[4,16,512]{2,1,0:T(8,128)(2,1)S(1)}, u32[]{:S(2)}, u32[]{:S(2)}) collective-permute-start(bf16[4,16,512]{2,1,0:T(8,128)(2,1)S(1)} %add_convert_fusion), channel_id=1, source_target_pairs={{0,2},{1,3},{2,0},{3,1},{4,6},{5,7},{6,4},{7,5},{8,10},{9,11},{10,... | collective-permute-start | bytes 196616 | tf_op jit(solution)/shard_map/ppermute | solution.py:212
  26.6 5.8 %collective-permute-start.11 = (bf16[4,16,512]{2,1,0:T(8,128)(2,1)S(1)}, bf16[4,16,512]{2,1,0:T(8,128)(2,1)S(1)}, u32[]{:S(2)}, u32[]{:S(2)}) collective-permute-start(bf16[4,16,512]{2,1,0:T(8,128)(2,1)S(1)} %add_convert_fusion.1.refs_6_), channel_id=1, source_target_pairs={{0,2},{1,3},{2,0},{3,1},{4,6},{5,7},{6,4},{7,5},{8,10},{9,11},{10,... | collective-permute-start | bytes 196616 | tf_op jit(solution)/shard_map/ppermute | solution.py:212

commit v5 on v4

--- a/solution.py
+++ b/solution.py
@@ -40,9 +40,9 @@
     return result
 
 
-def whitened_rows(values, quality):
+def scaled_rows(values, quality):
     energy = jnp.sum(values * values, axis=-1, keepdims=True) / (values.shape[-1] // 2)
-    return (values * (quality / jnp.sqrt(energy + EPS))).astype(BF16).astype(F32)
+    return values * (quality / jnp.sqrt(energy + EPS))
 
 
 def sources_kernel(blocks_in, quality_in, spectra_in, *rest):
@@ -75,7 +75,7 @@
     for window in range(windows):
         for step, (aligned, upper, flags) in enumerate(chosen):
             rows = spectra[window, pl.ds(aligned, 16), :].astype(F32)
-            values = whitened_rows(jnp.where(upper, rows[SRC:], rows[:SRC]), flags)
+            values = scaled_rows(jnp.where(upper, rows[SRC:], rows[:SRC]), flags)
             low = jnp.concatenate([values[:, :part], values[:, bins : bins + part]], axis=1)
             high = jnp.concatenate([values[:, part:bins], values[:, bins + part :]], axis=1)
             outs[step][window] = jnp.where(even, low, high).astype(BF16)
@@ -86,7 +86,7 @@
     owners, windows, rows, _ = out.shape
     flags = column(owners * rows, lambda row: quality[row].astype(F32))
     for window in range(windows):
-        values = whitened_rows(spectra[window].astype(F32), flags)
+        values = scaled_rows(spectra[window].astype(F32), flags).astype(BF16).astype(F32)
         for owner in range(owners):
             out[owner, window] = values[owner * rows : (owner + 1) * rows]
 

time: 33.2 us -> 33.2 us (level)
  no operation moved by 1% of the time
where the time goes in v5:
time: 33.2 us; the launch traced here: 33.1 us
  starting transfers between devices  15.4 us (46%)
  Pallas kernels  11 us (33%)
  waiting for transfers between devices  6.36 us (19%)
    ppermute x12, starting transfers between devices, exchange(): lax.ppermute(value, axis, [(i, i ^ distances[i % len(distances)]) for i i...  15.4 us
    ppermute x12, waiting for transfers between devices, exchange(): lax.ppermute(value, axis, [(i, i ^ distances[i % len(distances)]) for i i...  6.36 us
    pallas_call x4, Pallas kernels, lagged_call(): pl.pallas_call(functools.partial(lagged_kernel, distances, plan), out_sha...  5.53 us
    pallas_call x1, Pallas kernels, body(): pl.pallas_call(functools.partial(table_kernel, factor), out_shape=jax.Sha...  2.08 us
    pallas_call x1, Pallas kernels, body(): pl.pallas_call(sources_kernel, out_shape=[jax.ShapeDtypeStruct((windows,...  1.63 us
    pallas_call x1, Pallas kernels, body(): pl.pallas_call(receivers_kernel, out_shape=jax.ShapeDtypeStruct((places,...  1.07 us
    pallas_call x1, Pallas kernels, body(): pl.pallas_call(functools.partial(stack_kernel, [[first for _, first in st...  0.7 us
  transfers between devices with their start and end apart: 12, of which 7 were waited for; matrix products, arithmetic and copies ran while one was open for 1% of the time, Pallas kernels for 26%

profile of v5, /device:TPU:0, one launch (start us, length us, event | category | flops | bytes accessed | tf_op | source)
XLA Modules:
  0.0 33.1 jit_solution(154793134856750411)
XLA Ops:
  0.0 1.6 %shard_map.37 = (bf16[4,8,2048]{2,1,0:T(8,128)(2,1)S(1)}, bf16[4,8,2048]{2,1,0:T(8,128)(2,1)S(1)}, bf16[4,8,2048]{2,1,0:T(8,128)(2,1)S(1)}, bf16[4,8,2048]{2,1,0:T(8,128)(2,1)S(1)}) custom-call(s32[2]{0:T(128)} %blocks_in.1, s32[32]{0:T(128)} %quality.1, bf16[4,32,4096]{2,1,0:T(8,128)(2,1)} %spectra), custom_call_target="tpu_custom_call" | custom-call | tf_op jit(solution)/shard_map/pallas_call | solution.py:224
  1.6 0.5 %collective-permute-start = (bf16[4,8,2048]{2,1,0:T(8,128)(2,1)S(1)}, bf16[4,8,2048]{2,1,0:T(8,128)(2,1)S(1)}, u32[]{:S(2)}, u32[]{:S(2)}) collective-permute-start(bf16[4,8,2048]{2,1,0:T(8,128)(2,1)S(1)} %get-tuple-element.19), channel_id=1, source_target_pairs={{0,4},{4,0},{8,12},{12,8},{16,20},{20,16},{24,28},{28,24},{1,5},{5... | collective-permute-start | bytes 393224 | tf_op jit(solution)/shard_map/ppermute | solution.py:212
  2.2 0.9 %collective-permute-done = bf16[4,8,2048]{2,1,0:T(8,128)(2,1)S(1)} collective-permute-done((bf16[4,8,2048]{2,1,0:T(8,128)(2,1)S(1)}, bf16[4,8,2048]{2,1,0:T(8,128)(2,1)S(1)}, u32[]{:S(2)}, u32[]{:S(2)}) %collective-permute-start) | collective-permute-done | bytes 131104 | tf_op jit(solution)/shard_map/ppermute | solution.py:212
  3.2 2.9 %collective-permute-start.1 = (bf16[4,8,2048]{2,1,0:T(8,128)(2,1)S(1)}, bf16[4,8,2048]{2,1,0:T(8,128)(2,1)S(1)}, u32[]{:S(2)}, u32[]{:S(2)}) collective-permute-start(bf16[4,8,2048]{2,1,0:T(8,128)(2,1)S(1)} %add.24), channel_id=1, source_target_pairs={{0,8},{4,20},{8,0},{12,28},{16,24},{20,4},{24,16},{28,12},{1,9},{5... | collective-permute-start | bytes 393224 | tf_op jit(solution)/shard_map/ppermute | solution.py:212
  6.1 0.1 collective-permute-start.4
  6.3 2.1 %shard_map.38.refs_5_.refs_3_ = bf16[4096,512]{1,0:T(8,128)(2,1)S(1)} custom-call(), custom_call_target="tpu_custom_call" | custom-call | tf_op jit(solution)/shard_map/pallas_call | solution.py:238
  8.4 0.7 %collective-permute-done.1 = bf16[4,8,2048]{2,1,0:T(8,128)(2,1)S(1)} collective-permute-done((bf16[4,8,2048]{2,1,0:T(8,128)(2,1)S(1)}, bf16[4,8,2048]{2,1,0:T(8,128)(2,1)S(1)}, u32[]{:S(2)}, u32[]{:S(2)}) %collective-permute-start.1) | collective-permute-done | bytes 131104 | tf_op jit(solution)/shard_map/ppermute | solution.py:212
  9.1 2.1 %collective-permute-start.2 = (bf16[4,8,2048]{2,1,0:T(8,128)(2,1)S(1)}, bf16[4,8,2048]{2,1,0:T(8,128)(2,1)S(1)}, u32[]{:S(2)}, u32[]{:S(2)}) collective-permute-start(bf16[4,8,2048]{2,1,0:T(8,128)(2,1)S(1)} %add.25), channel_id=1, source_target_pairs={{0,16},{4,12},{8,24},{12,4},{16,0},{20,28},{24,8},{28,20},{1,17},{... | collective-permute-start | bytes 393224 | tf_op jit(solution)/shard_map/ppermute | solution.py:212
  11.2 1.6 %collective-permute-start.5 = (bf16[4,8,2048]{2,1,0:T(8,128)(2,1)S(1)}, bf16[4,8,2048]{2,1,0:T(8,128)(2,1)S(1)}, u32[]{:S(2)}, u32[]{:S(2)}) collective-permute-start(bf16[4,8,2048]{2,1,0:T(8,128)(2,1)S(1)} %add.28), channel_id=1, source_target_pairs={{0,16},{4,12},{8,24},{12,4},{16,0},{20,28},{24,8},{28,20},{1,17},{... | collective-permute-start | bytes 393224 | tf_op jit(solution)/shard_map/ppermute | solution.py:212
  12.8 1.1 %shard_map.39.refs_4_.refs_2_ = f32[4,4,8,4096]{3,2,1,0:T(8,128)S(1)} custom-call(s32[32]{0:T(128)S(1)} %copy-done.1, bf16[4,32,4096]{2,1,0:T(8,128)(2,1)S(1)} %copy-done), custom_call_target="tpu_custom_call" | custom-call | tf_op jit(solution)/shard_map/pallas_call | solution.py:255
  13.9 0.3 collective-permute-done.2
  14.3 2.0 %collective-permute-done.5 = bf16[4,8,2048]{2,1,0:T(8,128)(2,1)S(1)} collective-permute-done((bf16[4,8,2048]{2,1,0:T(8,128)(2,1)S(1)}, bf16[4,8,2048]{2,1,0:T(8,128)(2,1)S(1)}, u32[]{:S(2)}, u32[]{:S(2)}) %collective-permute-start.5) | collective-permute-done | bytes 131104 | tf_op jit(solution)/shard_map/ppermute | solution.py:212
  16.4 1.4 %shard_map.41.refs_4_ = bf16[8,16,512]{2,1,0:T(8,128)(2,1)S(1)} custom-call(bf16[4,8,2048]{2,1,0:T(8,128)(2,1)S(1)} %add.26.refs_0_, bf16[4,8,2048]{2,1,0:T(8,128)(2,1)S(1)} %collective-permute-done.6.refs_2_.refs_1_, f32[4,4,8,4096]{3,2,1,0:T(8,128)S(1)} %shard_map.39.refs_4_.refs_2_, bf16[4096,512]{1,0:T(8,128)(2,1)S(1)} %shard_map.38.refs_5_.refs_3_), custom_call_target="tpu_custom_call" | custom-call | flops 536870912 | bytes 4194304 | tf_op jit(solution)/shard_map/pallas_call | solution.py:196
  17.8 1.6 %collective-permute-start.9 = (bf16[8,16,512]{2,1,0:T(8,128)(2,1)S(1)}, bf16[8,16,512]{2,1,0:T(8,128)(2,1)S(1)}, u32[]{:S(2)}, u32[]{:S(2)}) collective-permute-start(bf16[8,16,512]{2,1,0:T(8,128)(2,1)S(1)} %shard_map.41.refs_4_), channel_id=1, source_target_pairs={{0,1},{1,0},{2,3},{3,2},{4,5},{5,4},{6,7},{7,6},{8,9},{9,8},{10,11... | collective-permute-start | bytes 393224 | tf_op jit(solution)/shard_map/ppermute | solution.py:212
  19.4 1.4 %shard_map.42 = bf16[8,16,512]{2,1,0:T(8,128)(2,1)S(1)} custom-call(bf16[4,8,2048]{2,1,0:T(8,128)(2,1)S(1)} %add.29.refs_1_.refs_0_, bf16[4,8,2048]{2,1,0:T(8,128)(2,1)S(1)} %collective-permute-done.7.refs_3_.refs_1_, f32[4,4,8,4096]{3,2,1,0:T(8,128)S(1)} %shard_map.39.refs_4_.refs_2_, bf16[4096,512]{1,0:T(8,128)(2,1)S(1)} %shard_map.38.refs_5_.refs_3_, ...), custom_call_target="tpu_custom_call" | custom-call | flops 536870912 | bytes 4194304 | tf_op jit(solution)/shard_map/pallas_call | solution.py:196
  20.8 0.5 %collective-permute-start.8 = (bf16[8,16,512]{2,1,0:T(8,128)(2,1)S(1)}, bf16[8,16,512]{2,1,0:T(8,128)(2,1)S(1)}, u32[]{:S(2)}, u32[]{:S(2)}) collective-permute-start(bf16[8,16,512]{2,1,0:T(8,128)(2,1)S(1)} %shard_map.42), channel_id=1, source_target_pairs={{0,1},{1,0},{2,3},{3,2},{4,5},{5,4},{6,7},{7,6},{8,9},{9,8},{10,11... | collective-permute-start | bytes 393224 | tf_op jit(solution)/shard_map/ppermute | solution.py:212
  21.3 1.4 %shard_map.40 = (f32[4,16,512]{2,1,0:T(8,128)S(1)}, f32[4,16,512]{2,1,0:T(8,128)S(1)}) custom-call(bf16[4,8,2048]{2,1,0:T(8,128)(2,1)S(1)} %add.26.refs_0_, bf16[4,8,2048]{2,1,0:T(8,128)(2,1)S(1)} %add.29.refs_1_.refs_0_, bf16[4,8,2048]{2,1,0:T(8,128)(2,1)S(1)} %collective-permute-done.6.refs_2_.refs_1_, ...), custom_call_target="tpu_custom_call" | custom-call | flops 536870912 | bytes 4194304 | tf_op jit(solution)/shard_map/pallas_call | solution.py:196
  22.7 1.0 %collective-permute-done.9.refs_1_ = bf16[8,16,512]{2,1,0:T(8,128)(2,1)S(1)} collective-permute-done((bf16[8,16,512]{2,1,0:T(8,128)(2,1)S(1)}, bf16[8,16,512]{2,1,0:T(8,128)(2,1)S(1)}, u32[]{:S(2)}, u32[]{:S(2)}) %collective-permute-start.9) | collective-permute-done | bytes 131104 | tf_op jit(solution)/shard_map/ppermute | solution.py:212
  23.8 2.7 %collective-permute-start.10 = (bf16[4,16,512]{2,1,0:T(8,128)(2,1)S(1)}, bf16[4,16,512]{2,1,0:T(8,128)(2,1)S(1)}, u32[]{:S(2)}, u32[]{:S(2)}) collective-permute-start(bf16[4,16,512]{2,1,0:T(8,128)(2,1)S(1)} %add_convert_fusion), channel_id=1, source_target_pairs={{0,2},{1,3},{2,0},{3,1},{4,6},{5,7},{6,4},{7,5},{8,10},{9,11},{10,... | collective-permute-start | bytes 196616 | tf_op jit(solution)/shard_map/ppermute | solution.py:212
  26.4 0.1 collective-permute-done.8.refs_4_
  26.6 3.1 %collective-permute-start.11 = (bf16[4,16,512]{2,1,0:T(8,128)(2,1)S(1)}, bf16[4,16,512]{2,1,0:T(8,128)(2,1)S(1)}, u32[]{:S(2)}, u32[]{:S(2)}) collective-permute-start(bf16[4,16,512]{2,1,0:T(8,128)(2,1)S(1)} %add_convert_fusion.1.refs_6_), channel_id=1, source_target_pairs={{0,2},{1,3},{2,0},{3,1},{4,6},{5,7},{6,4},{7,5},{8,10},{9,11},{10,... | collective-permute-start | bytes 196616 | tf_op jit(solution)/shard_map/ppermute | solution.py:212
  29.7 1.4 %shard_map.43 = (f32[4,16,512]{2,1,0:T(8,128)S(1)}, f32[4,16,512]{2,1,0:T(8,128)S(1)}) custom-call(bf16[4,8,2048]{2,1,0:T(8,128)(2,1)S(1)} %add.26.refs_0_, bf16[4,8,2048]{2,1,0:T(8,128)(2,1)S(1)} %add.29.refs_1_.refs_0_, bf16[4,8,2048]{2,1,0:T(8,128)(2,1)S(1)} %collective-permute-done.6.refs_2_.refs_1_, ...), custom_call_target="tpu_custom_call" | custom-call | flops 536870912 | bytes 4194304 | tf_op jit(solution)/shard_map/pallas_call | solution.py:196
  31.1 1.3 %collective-permute-done.11.refs_5_ = bf16[4,16,512]{2,1,0:T(8,128)(2,1)S(1)} collective-permute-done((bf16[4,16,512]{2,1,0:T(8,128)(2,1)S(1)}, bf16[4,16,512]{2,1,0:T(8,128)(2,1)S(1)}, u32[]{:S(2)}, u32[]{:S(2)}) %collective-permute-start.11) | collective-permute-done | bytes 65568 | tf_op jit(solution)/shard_map/ppermute | solution.py:212
  32.4 0.7 %shard_map.44 = bf16[2,8,8,512]{3,2,1,0:T(8,128)(2,1)} custom-call(f32[4,16,512]{2,1,0:T(8,128)S(1)} %get-tuple-element.28.refs_0_, bf16[8,16,512]{2,1,0:T(8,128)(2,1)S(1)} %collective-permute-done.9.refs_1_, bf16[4,16,512]{2,1,0:T(8,128)(2,1)S(1)} %collective-permute-done.10.refs_2_, f32[4,16,512]{2,1,0:T(8,128)S(1)} %get-tuple-element.30.refs_3_, ...), custom_call_target="tpu_custom_call" | custom-call | tf_op jit(solution)/shard_map/pallas_call | solution.py:300
  (20 shorter events, 0.5 us)
Async XLA Ops:
  0.0 12.8 %copy-start = (bf16[4,32,4096]{2,1,0:T(8,128)(2,1)S(1)}, bf16[4,32,4096]{2,1,0:T(8,128)(2,1)}, u32[]{:S(2)}) copy-start(bf16[4,32,4096]{2,1,0:T(8,128)(2,1)} %spectra) | copy-start | bytes 3145732
  0.0 12.8 %copy-start.1 = (s32[32]{0:T(128)S(1)}, s32[32]{0:T(128)}, u32[]{:S(2)}) copy-start(s32[32]{0:T(128)} %quality.1) | copy-start | bytes 388
  1.6 1.5 %collective-permute-start = (bf16[4,8,2048]{2,1,0:T(8,128)(2,1)S(1)}, bf16[4,8,2048]{2,1,0:T(8,128)(2,1)S(1)}, u32[]{:S(2)}, u32[]{:S(2)}) collective-permute-start(bf16[4,8,2048]{2,1,0:T(8,128)(2,1)S(1)} %get-tuple-element.19), channel_id=1, source_target_pairs={{0,4},{4,0},{8,12},{12,8},{16,20},{20,16},{24,28},{28,24},{1,5},{5... | collective-permute-start | bytes 393224 | tf_op jit(solution)/shard_map/ppermute | solution.py:212
  2.2 3.9 %collective-permute-start.3 = (bf16[4,8,2048]{2,1,0:T(8,128)(2,1)S(1)}, bf16[4,8,2048]{2,1,0:T(8,128)(2,1)S(1)}, u32[]{:S(2)}, u32[]{:S(2)}) collective-permute-start(bf16[4,8,2048]{2,1,0:T(8,128)(2,1)S(1)} %get-tuple-element.24), channel_id=1, source_target_pairs={{0,4},{4,0},{8,12},{12,8},{16,20},{20,16},{24,28},{28,24},{1,5},{5... | collective-permute-start | bytes 393224 | tf_op jit(solution)/shard_map/ppermute | solution.py:212
  3.2 5.9 %collective-permute-start.1 = (bf16[4,8,2048]{2,1,0:T(8,128)(2,1)S(1)}, bf16[4,8,2048]{2,1,0:T(8,128)(2,1)S(1)}, u32[]{:S(2)}, u32[]{:S(2)}) collective-permute-start(bf16[4,8,2048]{2,1,0:T(8,128)(2,1)S(1)} %add.24), channel_id=1, source_target_pairs={{0,8},{4,20},{8,0},{12,28},{16,24},{20,4},{24,16},{28,12},{1,9},{5... | collective-permute-start | bytes 393224 | tf_op jit(solution)/shard_map/ppermute | solution.py:212
  6.1 5.1 %collective-permute-start.4 = (bf16[4,8,2048]{2,1,0:T(8,128)(2,1)S(1)}, bf16[4,8,2048]{2,1,0:T(8,128)(2,1)S(1)}, u32[]{:S(2)}, u32[]{:S(2)}) collective-permute-start(bf16[4,8,2048]{2,1,0:T(8,128)(2,1)S(1)} %add.27), channel_id=1, source_target_pairs={{0,8},{4,20},{8,0},{12,28},{16,24},{20,4},{24,16},{28,12},{1,9},{5... | collective-permute-start | bytes 393224 | tf_op jit(solution)/shard_map/ppermute | solution.py:212
  9.1 5.1 %collective-permute-start.2 = (bf16[4,8,2048]{2,1,0:T(8,128)(2,1)S(1)}, bf16[4,8,2048]{2,1,0:T(8,128)(2,1)S(1)}, u32[]{:S(2)}, u32[]{:S(2)}) collective-permute-start(bf16[4,8,2048]{2,1,0:T(8,128)(2,1)S(1)} %add.25), channel_id=1, source_target_pairs={{0,16},{4,12},{8,24},{12,4},{16,0},{20,28},{24,8},{28,20},{1,17},{... | collective-permute-start | bytes 393224 | tf_op jit(solution)/shard_map/ppermute | solution.py:212
  11.2 5.0 %collective-permute-start.5 = (bf16[4,8,2048]{2,1,0:T(8,128)(2,1)S(1)}, bf16[4,8,2048]{2,1,0:T(8,128)(2,1)S(1)}, u32[]{:S(2)}, u32[]{:S(2)}) collective-permute-start(bf16[4,8,2048]{2,1,0:T(8,128)(2,1)S(1)} %add.28), channel_id=1, source_target_pairs={{0,16},{4,12},{8,24},{12,4},{16,0},{20,28},{24,8},{28,20},{1,17},{... | collective-permute-start | bytes 393224 | tf_op jit(solution)/shard_map/ppermute | solution.py:212
  14.2 2.2 %collective-permute-start.6 = (bf16[4,8,2048]{2,1,0:T(8,128)(2,1)S(1)}, bf16[4,8,2048]{2,1,0:T(8,128)(2,1)S(1)}, u32[]{:S(2)}, u32[]{:S(2)}) collective-permute-start(bf16[4,8,2048]{2,1,0:T(8,128)(2,1)S(1)} %add.26.refs_0_), channel_id=1, source_target_pairs={{0,4},{4,0},{8,12},{12,8},{16,20},{20,16},{24,28},{28,24},{1,5},{5... | collective-permute-start | bytes 393224 | tf_op jit(solution)/shard_map/ppermute | solution.py:212
  16.3 3.1 %collective-permute-start.7 = (bf16[4,8,2048]{2,1,0:T(8,128)(2,1)S(1)}, bf16[4,8,2048]{2,1,0:T(8,128)(2,1)S(1)}, u32[]{:S(2)}, u32[]{:S(2)}) collective-permute-start(bf16[4,8,2048]{2,1,0:T(8,128)(2,1)S(1)} %add.29.refs_1_.refs_0_), channel_id=1, source_target_pairs={{0,4},{4,0},{8,12},{12,8},{16,20},{20,16},{24,28},{28,24},{1,5},{5... | collective-permute-start | bytes 393224 | tf_op jit(solution)/shard_map/ppermute | solution.py:212
  17.8 6.0 %collective-permute-start.9 = (bf16[8,16,512]{2,1,0:T(8,128)(2,1)S(1)}, bf16[8,16,512]{2,1,0:T(8,128)(2,1)S(1)}, u32[]{:S(2)}, u32[]{:S(2)}) collective-permute-start(bf16[8,16,512]{2,1,0:T(8,128)(2,1)S(1)} %shard_map.41.refs_4_), channel_id=1, source_target_pairs={{0,1},{1,0},{2,3},{3,2},{4,5},{5,4},{6,7},{7,6},{8,9},{9,8},{10,11... | collective-permute-start | bytes 393224 | tf_op jit(solution)/shard_map/ppermute | solution.py:212
  20.8 5.7 %collective-permute-start.8 = (bf16[8,16,512]{2,1,0:T(8,128)(2,1)S(1)}, bf16[8,16,512]{2,1,0:T(8,128)(2,1)S(1)}, u32[]{:S(2)}, u32[]{:S(2)}) collective-permute-start(bf16[8,16,512]{2,1,0:T(8,128)(2,1)S(1)} %shard_map.42), channel_id=1, source_target_pairs={{0,1},{1,0},{2,3},{3,2},{4,5},{5,4},{6,7},{7,6},{8,9},{9,8},{10,11... | collective-permute-start | bytes 393224 | tf_op jit(solution)/shard_map/ppermute | solution.py:212
  23.8 7.3 %collective-permute-start.10 = (bf16[4,16,512]{2,1,0:T(8,128)(2,1)S(1)}, bf16[4,16,512]{2,1,0:T(8,128)(2,1)S(1)}, u32[]{:S(2)}, u32[]{:S(2)}) collective-permute-start(bf16[4,16,512]{2,1,0:T(8,128)(2,1)S(1)} %add_convert_fusion), channel_id=1, source_target_pairs={{0,2},{1,3},{2,0},{3,1},{4,6},{5,7},{6,4},{7,5},{8,10},{9,11},{10,... | collective-permute-start | bytes 196616 | tf_op jit(solution)/shard_map/ppermute | solution.py:212
  26.6 5.8 %collective-permute-start.11 = (bf16[4,16,512]{2,1,0:T(8,128)(2,1)S(1)}, bf16[4,16,512]{2,1,0:T(8,128)(2,1)S(1)}, u32[]{:S(2)}, u32[]{:S(2)}) collective-permute-start(bf16[4,16,512]{2,1,0:T(8,128)(2,1)S(1)} %add_convert_fusion.1.refs_6_), channel_id=1, source_target_pairs={{0,2},{1,3},{2,0},{3,1},{4,6},{5,7},{6,4},{7,5},{8,10},{9,11},{10,... | collective-permute-start | bytes 196616 | tf_op jit(solution)/shard_map/ppermute | solution.py:212

commit v6 on v5

--- a/solution.py
+++ b/solution.py
@@ -12,7 +12,7 @@
 SRC = 8
 STEPS = 2
 LANES = 128
-TILES_PER_DOT = 4
+TILES_PER_DOT = 2
 TABLE_ROWS = 64
 EPS = 1e-06
 F32 = jnp.float32

time: 33.2 us -> 33.2 us (level)
  no operation moved by 1% of the time
where the time goes in v6:
time: 33.2 us; the launch traced here: 33.1 us
  starting transfers between devices  15.4 us (46%)
  Pallas kernels  11 us (33%)
  waiting for transfers between devices  6.39 us (19%)
    ppermute x12, starting transfers between devices, exchange(): lax.ppermute(value, axis, [(i, i ^ distances[i % len(distances)]) for i i...  15.4 us
    ppermute x12, waiting for transfers between devices, exchange(): lax.ppermute(value, axis, [(i, i ^ distances[i % len(distances)]) for i i...  6.39 us
    pallas_call x4, Pallas kernels, lagged_call(): pl.pallas_call(functools.partial(lagged_kernel, distances, plan), out_sha...  5.47 us
    pallas_call x1, Pallas kernels, body(): pl.pallas_call(functools.partial(table_kernel, factor), out_shape=jax.Sha...  2.08 us
    pallas_call x1, Pallas kernels, body(): pl.pallas_call(sources_kernel, out_shape=[jax.ShapeDtypeStruct((windows,...  1.63 us
    pallas_call x1, Pallas kernels, body(): pl.pallas_call(receivers_kernel, out_shape=jax.ShapeDtypeStruct((places,...  1.07 us
    pallas_call x1, Pallas kernels, body(): pl.pallas_call(functools.partial(stack_kernel, [[first for _, first in st...  0.7 us
  transfers between devices with their start and end apart: 12, of which 7 were waited for; matrix products, arithmetic and copies ran while one was open for 1% of the time, Pallas kernels for 26%

profile of v6, /device:TPU:0, one launch (start us, length us, event | category | flops | bytes accessed | tf_op | source)
XLA Modules:
  0.0 33.1 jit_solution(14038897013598782107)
XLA Ops:
  0.0 1.6 %shard_map.37 = (bf16[4,8,2048]{2,1,0:T(8,128)(2,1)S(1)}, bf16[4,8,2048]{2,1,0:T(8,128)(2,1)S(1)}, bf16[4,8,2048]{2,1,0:T(8,128)(2,1)S(1)}, bf16[4,8,2048]{2,1,0:T(8,128)(2,1)S(1)}) custom-call(s32[2]{0:T(128)} %blocks_in.1, s32[32]{0:T(128)} %quality.1, bf16[4,32,4096]{2,1,0:T(8,128)(2,1)} %spectra), custom_call_target="tpu_custom_call" | custom-call | tf_op jit(solution)/shard_map/pallas_call | solution.py:224
  1.6 0.5 %collective-permute-start = (bf16[4,8,2048]{2,1,0:T(8,128)(2,1)S(1)}, bf16[4,8,2048]{2,1,0:T(8,128)(2,1)S(1)}, u32[]{:S(2)}, u32[]{:S(2)}) collective-permute-start(bf16[4,8,2048]{2,1,0:T(8,128)(2,1)S(1)} %get-tuple-element.19), channel_id=1, source_target_pairs={{0,4},{4,0},{8,12},{12,8},{16,20},{20,16},{24,28},{28,24},{1,5},{5... | collective-permute-start | bytes 393224 | tf_op jit(solution)/shard_map/ppermute | solution.py:212
  2.2 0.9 %collective-permute-done = bf16[4,8,2048]{2,1,0:T(8,128)(2,1)S(1)} collective-permute-done((bf16[4,8,2048]{2,1,0:T(8,128)(2,1)S(1)}, bf16[4,8,2048]{2,1,0:T(8,128)(2,1)S(1)}, u32[]{:S(2)}, u32[]{:S(2)}) %collective-permute-start) | collective-permute-done | bytes 131104 | tf_op jit(solution)/shard_map/ppermute | solution.py:212
  3.2 2.9 %collective-permute-start.1 = (bf16[4,8,2048]{2,1,0:T(8,128)(2,1)S(1)}, bf16[4,8,2048]{2,1,0:T(8,128)(2,1)S(1)}, u32[]{:S(2)}, u32[]{:S(2)}) collective-permute-start(bf16[4,8,2048]{2,1,0:T(8,128)(2,1)S(1)} %add.24), channel_id=1, source_target_pairs={{0,8},{4,20},{8,0},{12,28},{16,24},{20,4},{24,16},{28,12},{1,9},{5... | collective-permute-start | bytes 393224 | tf_op jit(solution)/shard_map/ppermute | solution.py:212
  6.1 0.1 collective-permute-start.4
  6.3 2.1 %shard_map.38.refs_5_.refs_3_ = bf16[4096,512]{1,0:T(8,128)(2,1)S(1)} custom-call(), custom_call_target="tpu_custom_call" | custom-call | tf_op jit(solution)/shard_map/pallas_call | solution.py:238
  8.4 0.7 %collective-permute-done.1 = bf16[4,8,2048]{2,1,0:T(8,128)(2,1)S(1)} collective-permute-done((bf16[4,8,2048]{2,1,0:T(8,128)(2,1)S(1)}, bf16[4,8,2048]{2,1,0:T(8,128)(2,1)S(1)}, u32[]{:S(2)}, u32[]{:S(2)}) %collective-permute-start.1) | collective-permute-done | bytes 131104 | tf_op jit(solution)/shard_map/ppermute | solution.py:212
  9.1 2.1 %collective-permute-start.2 = (bf16[4,8,2048]{2,1,0:T(8,128)(2,1)S(1)}, bf16[4,8,2048]{2,1,0:T(8,128)(2,1)S(1)}, u32[]{:S(2)}, u32[]{:S(2)}) collective-permute-start(bf16[4,8,2048]{2,1,0:T(8,128)(2,1)S(1)} %add.25), channel_id=1, source_target_pairs={{0,16},{4,12},{8,24},{12,4},{16,0},{20,28},{24,8},{28,20},{1,17},{... | collective-permute-start | bytes 393224 | tf_op jit(solution)/shard_map/ppermute | solution.py:212
  11.2 1.6 %collective-permute-start.5 = (bf16[4,8,2048]{2,1,0:T(8,128)(2,1)S(1)}, bf16[4,8,2048]{2,1,0:T(8,128)(2,1)S(1)}, u32[]{:S(2)}, u32[]{:S(2)}) collective-permute-start(bf16[4,8,2048]{2,1,0:T(8,128)(2,1)S(1)} %add.28), channel_id=1, source_target_pairs={{0,16},{4,12},{8,24},{12,4},{16,0},{20,28},{24,8},{28,20},{1,17},{... | collective-permute-start | bytes 393224 | tf_op jit(solution)/shard_map/ppermute | solution.py:212
  12.8 1.1 %shard_map.39.refs_4_.refs_2_ = f32[4,4,8,4096]{3,2,1,0:T(8,128)S(1)} custom-call(s32[32]{0:T(128)S(1)} %copy-done.1, bf16[4,32,4096]{2,1,0:T(8,128)(2,1)S(1)} %copy-done), custom_call_target="tpu_custom_call" | custom-call | tf_op jit(solution)/shard_map/pallas_call | solution.py:255
  13.9 0.3 collective-permute-done.2
  14.3 2.0 %collective-permute-done.5 = bf16[4,8,2048]{2,1,0:T(8,128)(2,1)S(1)} collective-permute-done((bf16[4,8,2048]{2,1,0:T(8,128)(2,1)S(1)}, bf16[4,8,2048]{2,1,0:T(8,128)(2,1)S(1)}, u32[]{:S(2)}, u32[]{:S(2)}) %collective-permute-start.5) | collective-permute-done | bytes 131104 | tf_op jit(solution)/shard_map/ppermute | solution.py:212
  16.4 1.4 %shard_map.41.refs_4_ = bf16[8,16,512]{2,1,0:T(8,128)(2,1)S(1)} custom-call(bf16[4,8,2048]{2,1,0:T(8,128)(2,1)S(1)} %add.26.refs_0_, bf16[4,8,2048]{2,1,0:T(8,128)(2,1)S(1)} %collective-permute-done.6.refs_2_.refs_1_, f32[4,4,8,4096]{3,2,1,0:T(8,128)S(1)} %shard_map.39.refs_4_.refs_2_, bf16[4096,512]{1,0:T(8,128)(2,1)S(1)} %shard_map.38.refs_5_.refs_3_), custom_call_target="tpu_custom_call" | custom-call | flops 536870912 | bytes 4194304 | tf_op jit(solution)/shard_map/pallas_call | solution.py:196
  17.8 1.6 %collective-permute-start.9 = (bf16[8,16,512]{2,1,0:T(8,128)(2,1)S(1)}, bf16[8,16,512]{2,1,0:T(8,128)(2,1)S(1)}, u32[]{:S(2)}, u32[]{:S(2)}) collective-permute-start(bf16[8,16,512]{2,1,0:T(8,128)(2,1)S(1)} %shard_map.41.refs_4_), channel_id=1, source_target_pairs={{0,1},{1,0},{2,3},{3,2},{4,5},{5,4},{6,7},{7,6},{8,9},{9,8},{10,11... | collective-permute-start | bytes 393224 | tf_op jit(solution)/shard_map/ppermute | solution.py:212
  19.4 1.4 %shard_map.42 = bf16[8,16,512]{2,1,0:T(8,128)(2,1)S(1)} custom-call(bf16[4,8,2048]{2,1,0:T(8,128)(2,1)S(1)} %add.29.refs_1_.refs_0_, bf16[4,8,2048]{2,1,0:T(8,128)(2,1)S(1)} %collective-permute-done.7.refs_3_.refs_1_, f32[4,4,8,4096]{3,2,1,0:T(8,128)S(1)} %shard_map.39.refs_4_.refs_2_, bf16[4096,512]{1,0:T(8,128)(2,1)S(1)} %shard_map.38.refs_5_.refs_3_, ...), custom_call_target="tpu_custom_call" | custom-call | flops 536870912 | bytes 4194304 | tf_op jit(solution)/shard_map/pallas_call | solution.py:196
  20.8 0.5 %collective-permute-start.8 = (bf16[8,16,512]{2,1,0:T(8,128)(2,1)S(1)}, bf16[8,16,512]{2,1,0:T(8,128)(2,1)S(1)}, u32[]{:S(2)}, u32[]{:S(2)}) collective-permute-start(bf16[8,16,512]{2,1,0:T(8,128)(2,1)S(1)} %shard_map.42), channel_id=1, source_target_pairs={{0,1},{1,0},{2,3},{3,2},{4,5},{5,4},{6,7},{7,6},{8,9},{9,8},{10,11... | collective-permute-start | bytes 393224 | tf_op jit(solution)/shard_map/ppermute | solution.py:212
  21.3 1.4 %shard_map.40 = (f32[4,16,512]{2,1,0:T(8,128)S(1)}, f32[4,16,512]{2,1,0:T(8,128)S(1)}) custom-call(bf16[4,8,2048]{2,1,0:T(8,128)(2,1)S(1)} %add.26.refs_0_, bf16[4,8,2048]{2,1,0:T(8,128)(2,1)S(1)} %add.29.refs_1_.refs_0_, bf16[4,8,2048]{2,1,0:T(8,128)(2,1)S(1)} %collective-permute-done.6.refs_2_.refs_1_, ...), custom_call_target="tpu_custom_call" | custom-call | flops 536870912 | bytes 4194304 | tf_op jit(solution)/shard_map/pallas_call | solution.py:196
  22.7 1.1 %collective-permute-done.9.refs_1_ = bf16[8,16,512]{2,1,0:T(8,128)(2,1)S(1)} collective-permute-done((bf16[8,16,512]{2,1,0:T(8,128)(2,1)S(1)}, bf16[8,16,512]{2,1,0:T(8,128)(2,1)S(1)}, u32[]{:S(2)}, u32[]{:S(2)}) %collective-permute-start.9) | collective-permute-done | bytes 131104 | tf_op jit(solution)/shard_map/ppermute | solution.py:212
  23.8 2.7 %collective-permute-start.10 = (bf16[4,16,512]{2,1,0:T(8,128)(2,1)S(1)}, bf16[4,16,512]{2,1,0:T(8,128)(2,1)S(1)}, u32[]{:S(2)}, u32[]{:S(2)}) collective-permute-start(bf16[4,16,512]{2,1,0:T(8,128)(2,1)S(1)} %add_convert_fusion), channel_id=1, source_target_pairs={{0,2},{1,3},{2,0},{3,1},{4,6},{5,7},{6,4},{7,5},{8,10},{9,11},{10,... | collective-permute-start | bytes 196616 | tf_op jit(solution)/shard_map/ppermute | solution.py:212
  26.4 0.1 collective-permute-done.8.refs_4_
  26.5 3.1 %collective-permute-start.11 = (bf16[4,16,512]{2,1,0:T(8,128)(2,1)S(1)}, bf16[4,16,512]{2,1,0:T(8,128)(2,1)S(1)}, u32[]{:S(2)}, u32[]{:S(2)}) collective-permute-start(bf16[4,16,512]{2,1,0:T(8,128)(2,1)S(1)} %add_convert_fusion.1.refs_6_), channel_id=1, source_target_pairs={{0,2},{1,3},{2,0},{3,1},{4,6},{5,7},{6,4},{7,5},{8,10},{9,11},{10,... | collective-permute-start | bytes 196616 | tf_op jit(solution)/shard_map/ppermute | solution.py:212
  29.7 1.4 %shard_map.43 = (f32[4,16,512]{2,1,0:T(8,128)S(1)}, f32[4,16,512]{2,1,0:T(8,128)S(1)}) custom-call(bf16[4,8,2048]{2,1,0:T(8,128)(2,1)S(1)} %add.26.refs_0_, bf16[4,8,2048]{2,1,0:T(8,128)(2,1)S(1)} %add.29.refs_1_.refs_0_, bf16[4,8,2048]{2,1,0:T(8,128)(2,1)S(1)} %collective-permute-done.6.refs_2_.refs_1_, ...), custom_call_target="tpu_custom_call" | custom-call | flops 536870912 | bytes 4194304 | tf_op jit(solution)/shard_map/pallas_call | solution.py:196
  31.1 1.3 %collective-permute-done.11.refs_5_ = bf16[4,16,512]{2,1,0:T(8,128)(2,1)S(1)} collective-permute-done((bf16[4,16,512]{2,1,0:T(8,128)(2,1)S(1)}, bf16[4,16,512]{2,1,0:T(8,128)(2,1)S(1)}, u32[]{:S(2)}, u32[]{:S(2)}) %collective-permute-start.11) | collective-permute-done | bytes 65568 | tf_op jit(solution)/shard_map/ppermute | solution.py:212
  32.4 0.7 %shard_map.44 = bf16[2,8,8,512]{3,2,1,0:T(8,128)(2,1)} custom-call(f32[4,16,512]{2,1,0:T(8,128)S(1)} %get-tuple-element.28.refs_0_, bf16[8,16,512]{2,1,0:T(8,128)(2,1)S(1)} %collective-permute-done.9.refs_1_, bf16[4,16,512]{2,1,0:T(8,128)(2,1)S(1)} %collective-permute-done.10.refs_2_, f32[4,16,512]{2,1,0:T(8,128)S(1)} %get-tuple-element.30.refs_3_, ...), custom_call_target="tpu_custom_call" | custom-call | tf_op jit(solution)/shard_map/pallas_call | solution.py:300
  (20 shorter events, 0.5 us)
Async XLA Ops:
  0.0 12.8 %copy-start = (bf16[4,32,4096]{2,1,0:T(8,128)(2,1)S(1)}, bf16[4,32,4096]{2,1,0:T(8,128)(2,1)}, u32[]{:S(2)}) copy-start(bf16[4,32,4096]{2,1,0:T(8,128)(2,1)} %spectra) | copy-start | bytes 3145732
  0.0 12.8 %copy-start.1 = (s32[32]{0:T(128)S(1)}, s32[32]{0:T(128)}, u32[]{:S(2)}) copy-start(s32[32]{0:T(128)} %quality.1) | copy-start | bytes 388
  1.6 1.5 %collective-permute-start = (bf16[4,8,2048]{2,1,0:T(8,128)(2,1)S(1)}, bf16[4,8,2048]{2,1,0:T(8,128)(2,1)S(1)}, u32[]{:S(2)}, u32[]{:S(2)}) collective-permute-start(bf16[4,8,2048]{2,1,0:T(8,128)(2,1)S(1)} %get-tuple-element.19), channel_id=1, source_target_pairs={{0,4},{4,0},{8,12},{12,8},{16,20},{20,16},{24,28},{28,24},{1,5},{5... | collective-permute-start | bytes 393224 | tf_op jit(solution)/shard_map/ppermute | solution.py:212
  2.2 3.9 %collective-permute-start.3 = (bf16[4,8,2048]{2,1,0:T(8,128)(2,1)S(1)}, bf16[4,8,2048]{2,1,0:T(8,128)(2,1)S(1)}, u32[]{:S(2)}, u32[]{:S(2)}) collective-permute-start(bf16[4,8,2048]{2,1,0:T(8,128)(2,1)S(1)} %get-tuple-element.24), channel_id=1, source_target_pairs={{0,4},{4,0},{8,12},{12,8},{16,20},{20,16},{24,28},{28,24},{1,5},{5... | collective-permute-start | bytes 393224 | tf_op jit(solution)/shard_map/ppermute | solution.py:212
  3.2 5.9 %collective-permute-start.1 = (bf16[4,8,2048]{2,1,0:T(8,128)(2,1)S(1)}, bf16[4,8,2048]{2,1,0:T(8,128)(2,1)S(1)}, u32[]{:S(2)}, u32[]{:S(2)}) collective-permute-start(bf16[4,8,2048]{2,1,0:T(8,128)(2,1)S(1)} %add.24), channel_id=1, source_target_pairs={{0,8},{4,20},{8,0},{12,28},{16,24},{20,4},{24,16},{28,12},{1,9},{5... | collective-permute-start | bytes 393224 | tf_op jit(solution)/shard_map/ppermute | solution.py:212
  6.1 5.1 %collective-permute-start.4 = (bf16[4,8,2048]{2,1,0:T(8,128)(2,1)S(1)}, bf16[4,8,2048]{2,1,0:T(8,128)(2,1)S(1)}, u32[]{:S(2)}, u32[]{:S(2)}) collective-permute-start(bf16[4,8,2048]{2,1,0:T(8,128)(2,1)S(1)} %add.27), channel_id=1, source_target_pairs={{0,8},{4,20},{8,0},{12,28},{16,24},{20,4},{24,16},{28,12},{1,9},{5... | collective-permute-start | bytes 393224 | tf_op jit(solution)/shard_map/ppermute | solution.py:212
  9.1 5.1 %collective-permute-start.2 = (bf16[4,8,2048]{2,1,0:T(8,128)(2,1)S(1)}, bf16[4,8,2048]{2,1,0:T(8,128)(2,1)S(1)}, u32[]{:S(2)}, u32[]{:S(2)}) collective-permute-start(bf16[4,8,2048]{2,1,0:T(8,128)(2,1)S(1)} %add.25), channel_id=1, source_target_pairs={{0,16},{4,12},{8,24},{12,4},{16,0},{20,28},{24,8},{28,20},{1,17},{... | collective-permute-start | bytes 393224 | tf_op jit(solution)/shard_map/ppermute | solution.py:212
  11.2 5.0 %collective-permute-start.5 = (bf16[4,8,2048]{2,1,0:T(8,128)(2,1)S(1)}, bf16[4,8,2048]{2,1,0:T(8,128)(2,1)S(1)}, u32[]{:S(2)}, u32[]{:S(2)}) collective-permute-start(bf16[4,8,2048]{2,1,0:T(8,128)(2,1)S(1)} %add.28), channel_id=1, source_target_pairs={{0,16},{4,12},{8,24},{12,4},{16,0},{20,28},{24,8},{28,20},{1,17},{... | collective-permute-start | bytes 393224 | tf_op jit(solution)/shard_map/ppermute | solution.py:212
  14.2 2.2 %collective-permute-start.6 = (bf16[4,8,2048]{2,1,0:T(8,128)(2,1)S(1)}, bf16[4,8,2048]{2,1,0:T(8,128)(2,1)S(1)}, u32[]{:S(2)}, u32[]{:S(2)}) collective-permute-start(bf16[4,8,2048]{2,1,0:T(8,128)(2,1)S(1)} %add.26.refs_0_), channel_id=1, source_target_pairs={{0,4},{4,0},{8,12},{12,8},{16,20},{20,16},{24,28},{28,24},{1,5},{5... | collective-permute-start | bytes 393224 | tf_op jit(solution)/shard_map/ppermute | solution.py:212
  16.3 3.1 %collective-permute-start.7 = (bf16[4,8,2048]{2,1,0:T(8,128)(2,1)S(1)}, bf16[4,8,2048]{2,1,0:T(8,128)(2,1)S(1)}, u32[]{:S(2)}, u32[]{:S(2)}) collective-permute-start(bf16[4,8,2048]{2,1,0:T(8,128)(2,1)S(1)} %add.29.refs_1_.refs_0_), channel_id=1, source_target_pairs={{0,4},{4,0},{8,12},{12,8},{16,20},{20,16},{24,28},{28,24},{1,5},{5... | collective-permute-start | bytes 393224 | tf_op jit(solution)/shard_map/ppermute | solution.py:212
  17.8 6.0 %collective-permute-start.9 = (bf16[8,16,512]{2,1,0:T(8,128)(2,1)S(1)}, bf16[8,16,512]{2,1,0:T(8,128)(2,1)S(1)}, u32[]{:S(2)}, u32[]{:S(2)}) collective-permute-start(bf16[8,16,512]{2,1,0:T(8,128)(2,1)S(1)} %shard_map.41.refs_4_), channel_id=1, source_target_pairs={{0,1},{1,0},{2,3},{3,2},{4,5},{5,4},{6,7},{7,6},{8,9},{9,8},{10,11... | collective-permute-start | bytes 393224 | tf_op jit(solution)/shard_map/ppermute | solution.py:212
  20.8 5.7 %collective-permute-start.8 = (bf16[8,16,512]{2,1,0:T(8,128)(2,1)S(1)}, bf16[8,16,512]{2,1,0:T(8,128)(2,1)S(1)}, u32[]{:S(2)}, u32[]{:S(2)}) collective-permute-start(bf16[8,16,512]{2,1,0:T(8,128)(2,1)S(1)} %shard_map.42), channel_id=1, source_target_pairs={{0,1},{1,0},{2,3},{3,2},{4,5},{5,4},{6,7},{7,6},{8,9},{9,8},{10,11... | collective-permute-start | bytes 393224 | tf_op jit(solution)/shard_map/ppermute | solution.py:212
  23.8 7.3 %collective-permute-start.10 = (bf16[4,16,512]{2,1,0:T(8,128)(2,1)S(1)}, bf16[4,16,512]{2,1,0:T(8,128)(2,1)S(1)}, u32[]{:S(2)}, u32[]{:S(2)}) collective-permute-start(bf16[4,16,512]{2,1,0:T(8,128)(2,1)S(1)} %add_convert_fusion), channel_id=1, source_target_pairs={{0,2},{1,3},{2,0},{3,1},{4,6},{5,7},{6,4},{7,5},{8,10},{9,11},{10,... | collective-permute-start | bytes 196616 | tf_op jit(solution)/shard_map/ppermute | solution.py:212
  26.5 5.8 %collective-permute-start.11 = (bf16[4,16,512]{2,1,0:T(8,128)(2,1)S(1)}, bf16[4,16,512]{2,1,0:T(8,128)(2,1)S(1)}, u32[]{:S(2)}, u32[]{:S(2)}) collective-permute-start(bf16[4,16,512]{2,1,0:T(8,128)(2,1)S(1)} %add_convert_fusion.1.refs_6_), channel_id=1, source_target_pairs={{0,2},{1,3},{2,0},{3,1},{4,6},{5,7},{6,4},{7,5},{8,10},{9,11},{10,... | collective-permute-start | bytes 196616 | tf_op jit(solution)/shard_map/ppermute | solution.py:212
